TPU v7x, 32 devices: a whole 2x2x4 slice. The times are simulated.
32 devices in a mesh: grp: 2 (over x), wide: 16 (over z, y, core).
Axes of the slice: x: 2, y: 2, z: 4, core: 2. Of those that a mesh axis runs over, the one named last changes fastest.
Arguments:
- queries: bfloat16 [16384, 16384], P(('grp', 'wide')), parts along dimension 0, may hold values from -6 to 6
- train_rows: bfloat16 [1024, 16384], P(('grp', 'wide')), parts along dimension 0, may hold values from -0.015625 to 0.015625
- left_basis: bfloat16 [128, 128], replicated, may hold values from -0.5 to 0.5
- right_basis: bfloat16 [128, 128], replicated, may hold values from -0.5 to 0.5
- eigenvalues: float32 [128, 128], replicated, may hold values from 0.01 to 10
Outputs:
- scores: float32 [16384, 512], P(('grp', 'wide')), parts along dimension 0
There are 2 independent parts, one for each index of `grp`. A program takes and returns all parts, laid end to end along the dimension named above; an argument that names none is the same for every part. Nothing has to cross between parts.
All inputs are finite; a program needn't handle non-finite values.
Results may differ from a plain program's by a relative error of at most 0.0049.
Values may be sent and summed in bfloat16 or wider, within the bound.
No kernel may reach another device: no remote copies, remote signals or barrier semaphores. Data moves between devices by JAX's collectives and lax.ppermute only.
A program may use at most 128 MiB of HBM per device.

v0:
```python
import jax
import jax.numpy as jnp
from jax import lax
from jax.sharding import PartitionSpec as P

A_DIM = 128
B_DIM = 128


DAMPING = 0.1


def precondition(row_block, left_basis, right_basis, eigenvalues):
    count = row_block.shape[0]
    matrix = row_block.reshape(count, A_DIM, B_DIM)
    inward = jnp.einsum(
        "ai,qab->qib", left_basis, matrix, preferred_element_type=jnp.float32
    ).astype(jnp.bfloat16)
    rotated = jnp.einsum("qib,bj->qij", inward, right_basis, preferred_element_type=jnp.float32)
    scaled = (rotated / (eigenvalues + DAMPING)).astype(jnp.bfloat16)
    restored = jnp.einsum(
        "ai,qij->qaj", left_basis, scaled, preferred_element_type=jnp.float32
    ).astype(jnp.bfloat16)
    prepared = jnp.einsum(
        "qaj,bj->qab", restored, right_basis, preferred_element_type=jnp.float32
    ).astype(jnp.bfloat16)
    return prepared.reshape(count, A_DIM * B_DIM)


def against(query_rows, train_piece):
    return lax.dot_general(
        query_rows, train_piece, (((1,), (1,)), ((), ())), preferred_element_type=jnp.float32
    )


def per_device(queries, train_rows, left_basis, right_basis, eigenvalues):
    prepared = precondition(train_rows, left_basis, right_basis, eigenvalues)
    gathered = lax.all_gather(prepared, "wide", axis=0, tiled=True)
    scores = against(queries, gathered)
    return scores


def solution(mesh):
    in_specs = (P(("grp", "wide"), None), P(("grp", "wide"), None), P(), P(), P())
    out_specs = P(("grp", "wide"), None)
    return jax.shard_map(
        per_device, mesh=mesh, in_specs=in_specs, out_specs=out_specs, check_vma=False
    )
```

profile of v0, /device:TPU:0, one launch (start us, length us, event | category | flops | bytes accessed | tf_op | source)
XLA Modules:
  0.0 181.7 jit_solution(10402334974074522056)
XLA Ops:
  6.5 0.0 copy-start
  6.5 0.0 all-gather.2.cloned.1.call-start
  6.5 0.9 broadcast_add_fusion
  7.4 1.5 copy.7
  8.9 0.0 copy-done
  8.9 0.5 fusion.2
  9.4 1.6 fusion.3
  11.0 1.2 convolution_convert_fusion
  12.2 1.7 copy.10
  13.8 0.0 all-gather.2.cloned.1.call-update
  13.9 129.8 %all-gather.2.cloned.1.call-done = bf16[512,16384]{1,0:T(8,128)(2,1)} async-done(((bf16[32,16384]{1,0:T(8,128)(2,1)}), bf16[512,16384]{1,0:T(8,128)(2,1)}) %all-gather.2.cloned.1.call-update) | async-done | bytes 16777232 | tf_op jit(solution)/shard_map/all_gather | solution.py:38
  143.6 29.9 %convolution_bitcast_fusion = f32[512,512]{0,1:T(8,128)S(1)} fusion(bf16[512,16384]{1,0:T(8,128)(2,1)} %all-gather.2.cloned.1.call-done, bf16[512,16384]{1,0:T(8,128)(2,1)} %param.5), kind=kOutput, calls=%fused_computation.5 | convolution fusion | flops 8589934592 | bytes 34603008 | tf_op jit(solution)/shard_map/dot_general | solution.py:31
  173.6 1.3 copy.6
Async XLA Ops:
  6.5 2.3 %copy-start = (bf16[128,128]{1,0:T(8,128)(2,1)S(1)}, bf16[128,128]{1,0:T(8,128)(2,1)}, u32[]{:S(2)}) copy-start(bf16[128,128]{1,0:T(8,128)(2,1)} %param.7) | copy-start | bytes 98308
  6.5 137.1 %all-gather.2.cloned.1.call-start = ((), (), s32[]{:S(2)}) async-start(), calls=%async_computation | async-start | bytes 17825792 | tf_op jit(solution)/shard_map/all_gather | solution.py:38
Sparse Core Ops, SparseCore 0:
  14.0 129.5 all-gather.1
where the time goes:
time: 182 us
  waiting for transfers between devices  130 us (71%)
  matrix products  33.2 us (18%)
  between operations  13.4 us (7%)
  local copies, waits for them, and re-layouts  4.42 us (2%)
    all_gather x1, waiting for transfers between devices, per_device(): gathered = lax.all_gather(prepared, 'wide', axis=0, tiled=True)  130 us
    dot_general x1, matrix products, against(): lax.dot_general(query_rows, train_piece, (((1,), (1,)), ((), ())), prefer...  29.9 us
  transfers between devices with their start and end apart: 1, of which 1 were waited for; matrix products, arithmetic and copies ran while one was open for 0% of the time, Pallas kernels for 0%

commit v1 on v0

v1 whole, which is shorter than its diff:
```python
import functools

import jax
import jax.numpy as jnp
import numpy as np
from jax import lax
from jax.experimental import pallas as pl
from jax.experimental.pallas import tpu as pltpu
from jax.sharding import PartitionSpec as P

A_DIM = 128
B_DIM = 128
LANES = 128
K_TILE = 2048

DAMPING = 0.1


def chip_ring(chips):
    if chips == 8:
        return list(range(0, chips, 2)) + list(range(chips - 1, 0, -2))
    return list(range(chips))


def precondition_kernel(rows_ref, left_ref, right_ref, eig_ref, out_ref, gather_ref, spread_ref):
    count = rows_ref.shape[0]
    for a in range(A_DIM):
        gather_ref[a * count:(a + 1) * count, :] = rows_ref[:, a * B_DIM:(a + 1) * B_DIM].astype(jnp.float32)
    left = left_ref[...]
    right = right_ref[...]
    damped = eig_ref[...] + DAMPING

    def stack(wide):
        return jnp.concatenate([wide[:, q * B_DIM:(q + 1) * B_DIM] for q in range(count)], axis=0)

    matrix = jnp.concatenate(
        [gather_ref[pl.ds(q, A_DIM, stride=count), :].astype(jnp.bfloat16) for q in range(count)], axis=1
    )
    inward = lax.dot_general(left, matrix, (((0,), (0,)), ((), ())), preferred_element_type=jnp.float32)
    rotated = jnp.dot(stack(inward.astype(jnp.bfloat16)), right, preferred_element_type=jnp.float32)
    scaled = jnp.concatenate(
        [(rotated[q * A_DIM:(q + 1) * A_DIM] / damped).astype(jnp.bfloat16) for q in range(count)], axis=1
    )
    restored = jnp.dot(left, scaled, preferred_element_type=jnp.float32).astype(jnp.bfloat16)
    prepared = lax.dot_general(
        stack(restored), right, (((1,), (1,)), ((), ())), preferred_element_type=jnp.float32
    )
    for q in range(count):
        spread_ref[pl.ds(q, A_DIM, stride=count), :] = prepared[q * A_DIM:(q + 1) * A_DIM]
    for a in range(A_DIM):
        out_ref[:, a * B_DIM:(a + 1) * B_DIM] = spread_ref[a * count:(a + 1) * count, :].astype(jnp.bfloat16)


def precondition(train_rows, left_basis, right_basis, eigenvalues, half):
    count = train_rows.shape[0] // 2
    width = train_rows.shape[1]
    whole = lambda shape: pl.BlockSpec(shape, lambda i: (0, 0))
    return pl.pallas_call(
        precondition_kernel,
        grid=(1,),
        out_shape=jax.ShapeDtypeStruct((count, width), jnp.bfloat16),
        in_specs=[pl.BlockSpec((count, width), lambda i: (half, 0))]
        + [whole(m.shape) for m in (left_basis, right_basis, eigenvalues)],
        out_specs=whole((count, width)),
        scratch_shapes=[pltpu.VMEM((A_DIM * count, B_DIM), jnp.float32)] * 2,
        compiler_params=pltpu.CompilerParams(vmem_limit_bytes=24 << 20),
        cost_estimate=pl.CostEstimate(
            flops=8 * count * A_DIM * A_DIM * B_DIM * 4, bytes_accessed=4 * count * width, transcendentals=0
        ),
        name="precondition",
    )(train_rows, left_basis, right_basis, eigenvalues)


def scores_kernel(slots, first, place_ref, query_ref, *refs):
    blocks = refs[:len(slots)]
    refs = refs[len(slots):]
    if not first:
        total_ref, refs = refs[0], refs[1:]
    out_ref, weight_ref, sum_ref = refs
    step = pl.program_id(0)
    count = blocks[0].shape[0]
    core = place_ref[2]

    @pl.when(step == 0)
    def _():
        weight_ref[...] = jnp.zeros_like(weight_ref)
        sum_ref[...] = jnp.zeros_like(sum_ref)

    per_block = LANES // (4 * count)
    for (group, other, half), block in zip(slots, blocks):
        owner = 1 - core if other else core
        start = group * LANES + lax.rem(place_ref[group], per_block) * 4 * count + owner * 2 * count + half * count
        weight_ref[pl.ds(pl.multiple_of(start, count), count), :] = block[...]
    sum_ref[...] += lax.dot_general(
        query_ref[...], weight_ref[...], (((1,), (1,)), ((), ())), preferred_element_type=jnp.float32
    )

    @pl.when(step == pl.num_programs(0) - 1)
    def _():
        out_ref[...] = jnp.zeros_like(out_ref) if first else total_ref[...]
        for group in range(weight_ref.shape[0] // LANES):
            start = lax.div(place_ref[group], per_block) * LANES
            lanes = pl.ds(pl.multiple_of(start, LANES), LANES)
            out_ref[:, lanes] += sum_ref[:, group * LANES:(group + 1) * LANES]


def add_scores(total, queries, place, slots, blocks, train_count):
    rows, width = queries.shape
    first = total is None
    groups = 1 + max(group for group, _, _ in slots)
    totals = [] if first else [total]
    whole = pl.BlockSpec((rows, train_count), lambda i: (0, 0))
    return pl.pallas_call(
        functools.partial(scores_kernel, slots, first),
        grid=(width // K_TILE,),
        out_shape=jax.ShapeDtypeStruct((rows, train_count), jnp.float32),
        in_specs=[pl.BlockSpec(memory_space=pltpu.SMEM), pl.BlockSpec((rows, K_TILE), lambda i: (0, i))]
        + [pl.BlockSpec((b.shape[0], K_TILE), lambda i: (0, i)) for b in blocks]
        + [whole] * len(totals),
        out_specs=whole,
        scratch_shapes=[
            pltpu.VMEM((groups * LANES, K_TILE), jnp.bfloat16),
            pltpu.VMEM((rows, groups * LANES), jnp.float32),
        ],
        compiler_params=pltpu.CompilerParams(vmem_limit_bytes=24 << 20),
        cost_estimate=pl.CostEstimate(
            flops=2 * rows * width * 256, bytes_accessed=2 * rows * width, transcendentals=0
        ),
        name="scores",
    )(place, queries, *blocks, *totals)


def per_device(queries, train_rows, left_basis, right_basis, eigenvalues):
    devices = lax.axis_size("wide")
    chips = devices // 2
    ring = chip_ring(chips)
    hops = chips // 2
    train_count = devices * train_rows.shape[0]

    def shift(step):
        return [
            (2 * ring[i] + core, 2 * ring[(i + step) % chips] + core) for i in range(chips) for core in range(2)
        ]

    swap = [(d, d ^ 1) for d in range(devices)]
    send = lambda block, pairs: lax.ppermute(block, "wide", pairs)
    up, down = shift(1), shift(-1)

    table = np.zeros((devices, hops + 1, 4), np.int32)
    for i in range(chips):
        for core in range(2):
            for hop in range(hops + 1):
                table[2 * ring[i] + core, hop] = (ring[(i - hop) % chips], ring[(i + hop) % chips], core, 0)
    places = lax.dynamic_index_in_dim(jnp.asarray(table), lax.axis_index("wide"), 0, keepdims=False)

    own = [precondition(train_rows, left_basis, right_basis, eigenvalues, half) for half in range(2)]
    others = [send(block, swap) for block in own]
    total = add_scores(
        None, queries, places[0], [(0, 0, 0), (0, 0, 1), (0, 1, 0), (0, 1, 1)], own + others, train_count
    )
    rising, falling = list(own), list(own)
    for hop in range(1, hops + 1):
        slots, blocks = [], []
        last = hop == hops
        for half in range(2):
            if not last or half == 0:
                rising[half] = send(rising[half], up)
                blocks += [rising[half], send(rising[half], swap)]
                slots += [(0, 0, half), (0, 1, half)]
            if not last or half == 1:
                falling[half] = send(falling[half], down)
                blocks += [falling[half], send(falling[half], swap)]
                group = 0 if last else 1
                slots += [(group, 0, half), (group, 1, half)]
        total = add_scores(total, queries, places[hop], slots, blocks, train_count)
    return total


def solution(mesh):
    in_specs = (P(("grp", "wide"), None), P(("grp", "wide"), None), P(), P(), P())
    out_specs = P(("grp", "wide"), None)
    return jax.shard_map(
        per_device, mesh=mesh, in_specs=in_specs, out_specs=out_specs, check_vma=False
    )
```

time: 182 us -> 137 us (0.75)
  waiting for transfers between devices: 130 us -> 43.7 us
  Pallas kernels: 0 us -> 47 us
  matrix products: 33.2 us -> 0 us
  local copies, waits for them, and re-layouts: 4.42 us -> 28.4 us
  starting transfers between devices: 0.01 us -> 16.9 us
  between operations: 13.4 us -> 0.27 us
    all_gather x1 -> x0, waiting for transfers between devices: 130 us -> none  [per_device(): gathered = lax.all_gather(prepared, 'wide', axis=0, tiled=True)]
    pallas_call x0 -> x7, Pallas kernels: none -> 47 us  [the longest x5 44 us: add_scores(): pl.pallas_call(functools.partial(scores_kernel, slots, first), grid=(widt...]
    ppermute x0 -> x30, waiting for transfers between devices: none -> 43.7 us  [per_device(): send = lambda block, pairs: lax.ppermute(block, 'wide', pairs)]
    dot_general x4 -> x0, matrix products: 33.2 us -> none  [the longest x1 29.9 us: against(): lax.dot_general(query_rows, train_piece, (((1,), (1,)), ((), ())), prefer...]
    unnamed x4 -> x76, local copies, waits for them, and re-layouts: 3.12 us -> 27.7 us
    ppermute x0 -> x30, starting transfers between devices: none -> 16.9 us  [per_device(): send = lambda block, pairs: lax.ppermute(block, 'wide', pairs)]
  transfers between devices with their start and end apart: 1 -> 30, of which waited for: 1 -> 8; matrix products, arithmetic and copies ran while one was open for 0% -> 1% of each run, Pallas kernels for 0% -> 27%
where the time goes in v1:
time: 137 us; the launch traced here: 136 us
  Pallas kernels  47 us (34%)
  waiting for transfers between devices  43.7 us (32%)
  local copies, waits for them, and re-layouts  28.4 us (21%)
  starting transfers between devices  16.9 us (12%)
    pallas_call x5, Pallas kernels, add_scores(): pl.pallas_call(functools.partial(scores_kernel, slots, first), grid=(widt...  44 us
    ppermute x30, waiting for transfers between devices, per_device(): send = lambda block, pairs: lax.ppermute(block, 'wide', pairs)  43.7 us
    unnamed x76, local copies, waits for them, and re-layouts  27.7 us
    ppermute x30, starting transfers between devices, per_device(): send = lambda block, pairs: lax.ppermute(block, 'wide', pairs)  16.9 us
    pallas_call x2, Pallas kernels, precondition(): pl.pallas_call(precondition_kernel, grid=(1,), out_shape=jax.ShapeDtypeSt...  2.91 us
  transfers between devices with their start and end apart: 30, of which 8 were waited for; matrix products, arithmetic and copies ran while one was open for 1% of the time, Pallas kernels for 27%

profile of v1, /device:TPU:0, one launch (start us, length us, event | category | flops | bytes accessed | tf_op | source)
XLA Modules:
  0.0 136.3 jit_solution(8654683925695132011)
XLA Ops:
  0.0 1.2 copy-done.34
  1.2 0.8 copy-done.35
  2.1 0.8 copy-done.36
  2.8 0.8 copy-done.37
  3.6 1.5 %precondition.2.refs_0_ = bf16[16,16384]{1,0:T(8,128)(2,1)S(1)} custom-call(bf16[32,16384]{1,0:T(8,128)(2,1)S(1)} %copy-done.34, bf16[128,128]{1,0:T(8,128)(2,1)S(1)} %copy-done.36, bf16[128,128]{1,0:T(8,128)(2,1)S(1)} %copy-done.37, f32[128,128]{1,0:T(8,128)S(1)} %copy-done.35), custom_call_target="tpu_custom_call" | custom-call | flops 1073741824 | bytes 1048576 | tf_op jit(solution)/shard_map/precondition/pallas_call | solution.py:58
  5.0 0.0 copy-start.8
  5.1 0.5 collective-permute-start.28
  5.6 2.6 %collective-permute-start = (bf16[16,16384]{1,0:T(8,128)(2,1)S(1)}, bf16[16,16384]{1,0:T(8,128)(2,1)S(1)}, u32[]{:S(2)}, u32[]{:S(2)}) collective-permute-start(bf16[16,16384]{1,0:T(8,128)(2,1)S(1)} %precondition.2.refs_0_), channel_id=1, source_target_pairs={{0,4},{1,5},{4,8},{5,9},{8,12},{9,13},{12,14},{13,15},{14,10},{15,... | collective-permute-start | bytes 1572872 | tf_op jit(solution)/shard_map/ppermute | solution.py:146
  8.2 0.0 collective-permute-start.11
  8.2 1.5 %precondition.3.refs_1_ = bf16[16,16384]{1,0:T(8,128)(2,1)S(1)} custom-call(bf16[32,16384]{1,0:T(8,128)(2,1)S(1)} %copy-done.34, bf16[128,128]{1,0:T(8,128)(2,1)S(1)} %copy-done.36, bf16[128,128]{1,0:T(8,128)(2,1)S(1)} %copy-done.37, f32[128,128]{1,0:T(8,128)S(1)} %copy-done.35), custom_call_target="tpu_custom_call" | custom-call | flops 1073741824 | bytes 1048576 | tf_op jit(solution)/shard_map/precondition/pallas_call | solution.py:58
  9.7 2.1 %collective-permute-start.15 = (bf16[16,16384]{1,0:T(8,128)(2,1)S(1)}, bf16[16,16384]{1,0:T(8,128)(2,1)S(1)}, u32[]{:S(2)}, u32[]{:S(2)}) collective-permute-start(bf16[16,16384]{1,0:T(8,128)(2,1)S(1)} %precondition.3.refs_1_), channel_id=1, source_target_pairs={{0,4},{1,5},{4,8},{5,9},{8,12},{9,13},{12,14},{13,15},{14,10},{15,... | collective-permute-start | bytes 1572872 | tf_op jit(solution)/shard_map/ppermute | solution.py:146
  11.8 0.8 copy-done.10
  12.5 0.0 collective-permute-start.5
  12.6 0.8 copy-done.18
  13.4 7.5 %collective-permute-done.refs_0_ = bf16[16,16384]{1,0:T(8,128)(2,1)S(1)} collective-permute-done((bf16[16,16384]{1,0:T(8,128)(2,1)S(1)}, bf16[16,16384]{1,0:T(8,128)(2,1)S(1)}, u32[]{:S(2)}, u32[]{:S(2)}) %collective-permute-start) | collective-permute-done | bytes 524320 | tf_op jit(solution)/shard_map/ppermute | solution.py:146
  20.9 2.0 %collective-permute-done.11.refs_2_ = bf16[16,16384]{1,0:T(8,128)(2,1)S(1)} collective-permute-done((bf16[16,16384]{1,0:T(8,128)(2,1)S(1)}, bf16[16,16384]{1,0:T(8,128)(2,1)S(1)}, u32[]{:S(2)}, u32[]{:S(2)}) %collective-permute-start.11) | collective-permute-done | bytes 524320 | tf_op jit(solution)/shard_map/ppermute | solution.py:146
  23.0 8.9 %collective-permute-done.15.refs_4_ = bf16[16,16384]{1,0:T(8,128)(2,1)S(1)} collective-permute-done((bf16[16,16384]{1,0:T(8,128)(2,1)S(1)}, bf16[16,16384]{1,0:T(8,128)(2,1)S(1)}, u32[]{:S(2)}, u32[]{:S(2)}) %collective-permute-start.15) | collective-permute-done | bytes 524320 | tf_op jit(solution)/shard_map/ppermute | solution.py:146
  31.9 0.8 copy-done.22
  32.8 1.8 %collective-permute-start.1 = (bf16[16,16384]{1,0:T(8,128)(2,1)S(1)}, bf16[16,16384]{1,0:T(8,128)(2,1)S(1)}, u32[]{:S(2)}, u32[]{:S(2)}) collective-permute-start(bf16[16,16384]{1,0:T(8,128)(2,1)S(1)} %collective-permute-done.refs_0_), channel_id=1, source_target_pairs={{0,4},{1,5},{4,8},{5,9},{8,12},{9,13},{12,14},{13,15},{14,10},{15,... | collective-permute-start | bytes 1572872 | tf_op jit(solution)/shard_map/ppermute | solution.py:146
  34.6 0.2 collective-permute-start.12
  34.8 0.8 copy-done.2
  35.6 0.8 copy-done.12
  36.5 1.8 %collective-permute-start.16 = (bf16[16,16384]{1,0:T(8,128)(2,1)S(1)}, bf16[16,16384]{1,0:T(8,128)(2,1)}, u32[]{:S(2)}, u32[]{:S(2)}) collective-permute-start(bf16[16,16384]{1,0:T(8,128)(2,1)S(1)} %collective-permute-done.15.refs_4_), channel_id=1, source_target_pairs={{0,4},{1,5},{4,8},{5,9},{8,12},{9,13},{12,14},{13,15},{14,10},{15,... | collective-permute-start | bytes 1572872 | tf_op jit(solution)/shard_map/ppermute | solution.py:146
  38.3 0.8 copy-done.4
  39.1 0.8 copy-done.16
  39.9 0.8 copy-done.20
  40.7 0.2 collective-permute-start.6
  40.9 0.8 copy-done.6
  41.7 5.8 %collective-permute-done.1.refs_0_ = bf16[16,16384]{1,0:T(8,128)(2,1)S(1)} collective-permute-done((bf16[16,16384]{1,0:T(8,128)(2,1)S(1)}, bf16[16,16384]{1,0:T(8,128)(2,1)S(1)}, u32[]{:S(2)}, u32[]{:S(2)}) %collective-permute-start.1) | collective-permute-done | bytes 524320 | tf_op jit(solution)/shard_map/ppermute | solution.py:146
  47.5 1.9 %collective-permute-done.12.refs_2_ = bf16[16,16384]{1,0:T(8,128)(2,1)} collective-permute-done((bf16[16,16384]{1,0:T(8,128)(2,1)S(1)}, bf16[16,16384]{1,0:T(8,128)(2,1)}, u32[]{:S(2)}, u32[]{:S(2)}) %collective-permute-start.12) | collective-permute-done | bytes 524320 | tf_op jit(solution)/shard_map/ppermute | solution.py:146
  49.4 9.0 %collective-permute-done.16.refs_4_ = bf16[16,16384]{1,0:T(8,128)(2,1)} collective-permute-done((bf16[16,16384]{1,0:T(8,128)(2,1)S(1)}, bf16[16,16384]{1,0:T(8,128)(2,1)}, u32[]{:S(2)}, u32[]{:S(2)}) %collective-permute-start.16) | collective-permute-done | bytes 524320 | tf_op jit(solution)/shard_map/ppermute | solution.py:146
  58.4 0.8 copy-done.30
  59.3 1.8 %collective-permute-start.2 = (bf16[16,16384]{1,0:T(8,128)(2,1)S(1)}, bf16[16,16384]{1,0:T(8,128)(2,1)}, u32[]{:S(2)}, u32[]{:S(2)}) collective-permute-start(bf16[16,16384]{1,0:T(8,128)(2,1)S(1)} %collective-permute-done.1.refs_0_), channel_id=1, source_target_pairs={{0,4},{1,5},{4,8},{5,9},{8,12},{9,13},{12,14},{13,15},{14,10},{15,... | collective-permute-start | bytes 1572872 | tf_op jit(solution)/shard_map/ppermute | solution.py:146
  61.1 0.8 copy-done.14
  61.9 0.2 collective-permute-start.23
  62.1 0.8 copy-done.26
  62.9 0.2 collective-permute-start.7
  63.1 0.8 copy-done.24
  63.9 0.7 constant_dynamic-slice_fusion
  64.6 0.8 copy-done.28
  65.4 1.7 %collective-permute-start.13 = (bf16[16,16384]{1,0:T(8,128)(2,1)}, bf16[16,16384]{1,0:T(8,128)(2,1)}, u32[]{:S(2)}, u32[]{:S(2)}) collective-permute-start(bf16[16,16384]{1,0:T(8,128)(2,1)} %collective-permute-done.12.refs_2_), channel_id=1, source_target_pairs={{0,2},{1,3},{4,0},{5,1},{8,4},{9,5},{12,8},{13,9},{14,12},{15,13},... | collective-permute-start | bytes 1572872 | tf_op jit(solution)/shard_map/ppermute | solution.py:146
  67.2 0.3 collective-permute-start.17
  67.5 6.6 %collective-permute-done.2.refs_0_ = bf16[16,16384]{1,0:T(8,128)(2,1)} collective-permute-done((bf16[16,16384]{1,0:T(8,128)(2,1)S(1)}, bf16[16,16384]{1,0:T(8,128)(2,1)}, u32[]{:S(2)}, u32[]{:S(2)}) %collective-permute-start.2) | collective-permute-done | bytes 524320 | tf_op jit(solution)/shard_map/ppermute | solution.py:146
  74.1 1.9 %collective-permute-start.3 = (bf16[16,16384]{1,0:T(8,128)(2,1)}, bf16[16,16384]{1,0:T(8,128)(2,1)}, u32[]{:S(2)}, u32[]{:S(2)}) collective-permute-start(bf16[16,16384]{1,0:T(8,128)(2,1)} %collective-permute-done.2.refs_0_), channel_id=1, source_target_pairs={{0,4},{1,5},{4,8},{5,9},{8,12},{9,13},{12,14},{13,15},{14,10},{15,... | collective-permute-start | bytes 1572872 | tf_op jit(solution)/shard_map/ppermute | solution.py:146
  75.9 1.8 %collective-permute-done.7.refs_6_ = bf16[16,16384]{1,0:T(8,128)(2,1)} collective-permute-done((bf16[16,16384]{1,0:T(8,128)(2,1)S(1)}, bf16[16,16384]{1,0:T(8,128)(2,1)}, u32[]{:S(2)}, u32[]{:S(2)}) %collective-permute-start.7) | collective-permute-done | bytes 524320 | tf_op jit(solution)/shard_map/ppermute | solution.py:146
  77.7 0.2 collective-permute-start.8
  78.0 5.8 %copy-done = bf16[512,16384]{1,0:T(8,128)(2,1)S(1)} copy-done((bf16[512,16384]{1,0:T(8,128)(2,1)S(1)}, bf16[512,16384]{1,0:T(8,128)(2,1)}, u32[]{:S(2)}) %copy-start) | copy-done | bytes 16777240
  83.7 1.0 copy-done.9
  84.8 1.0 copy-done.11
  85.8 1.0 copy-done.19
  86.8 1.0 copy-done.23
  87.9 7.9 %scores.5.refs_8_ = f32[512,512]{1,0:T(8,128)S(1)} custom-call(s32[4]{0:T(128)S(1)} %get-tuple-element.5.place_ref, bf16[512,16384]{1,0:T(8,128)(2,1)S(1)} %copy-done, bf16[16,16384]{1,0:T(8,128)(2,1)S(1)} %copy-done.9, bf16[16,16384]{1,0:T(8,128)(2,1)S(1)} %copy-done.19, bf16[16,16384]{1,0:T(8,128)(2,1)S(1)} %copy-done.11, bf16[16,16384]{1,0:T(8,128)(2,1)S(1)} %copy-done.23), custom_call_target="tpu_custom_call" | custom-call | flops 4294967296 | bytes 16777216 | tf_op jit(solution)/shard_map/scores/pallas_call | solution.py:113
  95.9 0.1 collective-permute-start.19
  95.9 0.5 collective-permute-start.14
  96.4 0.8 copy-done.32
  97.2 0.1 collective-permute-start.18
  97.4 1.0 copy-done.21
  98.4 1.0 copy-done.31
  99.4 8.7 %scores.6.refs_8_ = f32[512,512]{1,0:T(8,128)S(1)} custom-call(s32[4]{0:T(128)S(1)} %get-tuple-element.6.place_ref, bf16[512,16384]{1,0:T(8,128)(2,1)S(1)} %copy-done.1, bf16[16,16384]{1,0:T(8,128)(2,1)S(1)} %collective-permute-done.refs_0_, bf16[16,16384]{1,0:T(8,128)(2,1)S(1)} %copy-done.13, bf16[16,16384]{1,0:T(8,128)(2,1)S(1)} %copy-done.3, ...), custom_call_target="tpu_custom_call" | custom-call | flops 4294967296 | bytes 16777216 | tf_op jit(solution)/shard_map/scores/pallas_call | solution.py:113
  108.2 0.5 collective-permute-start.4
  108.7 0.1 collective-permute-start.9
  108.8 9.1 %scores.7.refs_8_ = f32[512,512]{1,0:T(8,128)S(1)} custom-call(s32[4]{0:T(128)S(1)} %get-tuple-element.7.place_ref, bf16[512,16384]{1,0:T(8,128)(2,1)S(1)} %copy-done.1, bf16[16,16384]{1,0:T(8,128)(2,1)S(1)} %copy-done.15, bf16[16,16384]{1,0:T(8,128)(2,1)S(1)} %copy-done.27, bf16[16,16384]{1,0:T(8,128)(2,1)} %collective-permute-done.12.refs_2_, ...), custom_call_target="tpu_custom_call" | custom-call | flops 4294967296 | bytes 16777216 | tf_op jit(solution)/shard_map/scores/pallas_call | solution.py:113
  118.0 9.0 %scores.8.refs_4_ = f32[512,512]{1,0:T(8,128)S(1)} custom-call(s32[4]{0:T(128)S(1)} %get-tuple-element.8.place_ref, bf16[512,16384]{1,0:T(8,128)(2,1)S(1)} %copy-done.1, bf16[16,16384]{1,0:T(8,128)(2,1)} %collective-permute-done.2.refs_0_, bf16[16,16384]{1,0:T(8,128)(2,1)S(1)} %copy-done.33, bf16[16,16384]{1,0:T(8,128)(2,1)} %collective-permute-done.13.refs_2_, ...), custom_call_target="tpu_custom_call" | custom-call | flops 4294967296 | bytes 16777216 | tf_op jit(solution)/shard_map/scores/pallas_call | solution.py:113
  127.0 9.3 %scores.9 = f32[512,512]{1,0:T(8,128)} custom-call(s32[4]{0:T(128)S(1)} %get-tuple-element.9.place_ref, bf16[512,16384]{1,0:T(8,128)(2,1)S(1)} %copy-done.1, bf16[16,16384]{1,0:T(8,128)(2,1)} %collective-permute-done.3.refs_0_, bf16[16,16384]{1,0:T(8,128)(2,1)S(1)} %collective-permute-done.4.refs_1_, bf16[16,16384]{1,0:T(8,128)(2,1)} %collective-permute-done.8.refs_2_, ...), custom_call_target="tpu_custom_call" | custom-call | flops 4294967296 | bytes 16777216 | tf_op jit(solution)/shard_map/scores/pallas_call | solution.py:113
  (81 shorter events, 0.2 us)
Async XLA Ops:
  0.0 1.2 copy-start.34
  1.2 0.8 copy-start.35
  5.0 56.8 %copy-start.8 = (bf16[16,16384]{1,0:T(8,128)(2,1)}, bf16[16,16384]{1,0:T(8,128)(2,1)S(1)}, u32[]{:S(2)}) copy-start(bf16[16,16384]{1,0:T(8,128)(2,1)S(1)} %precondition.2.refs_0_) | copy-start | bytes 1572868
  5.1 6.7 %collective-permute-start.28 = (bf16[16,16384]{1,0:T(8,128)(2,1)S(1)}, bf16[16,16384]{1,0:T(8,128)(2,1)S(1)}, u32[]{:S(2)}, u32[]{:S(2)}) collective-permute-start(bf16[16,16384]{1,0:T(8,128)(2,1)S(1)} %precondition.2.refs_0_), channel_id=1, source_target_pairs={{0,1},{1,0},{2,3},{3,2},{4,5},{5,4},{6,7},{7,6},{8,9},{9,8},{10,11... | collective-permute-start | bytes 1572872 | tf_op jit(solution)/shard_map/ppermute | solution.py:146
  5.6 15.4 %collective-permute-start = (bf16[16,16384]{1,0:T(8,128)(2,1)S(1)}, bf16[16,16384]{1,0:T(8,128)(2,1)S(1)}, u32[]{:S(2)}, u32[]{:S(2)}) collective-permute-start(bf16[16,16384]{1,0:T(8,128)(2,1)S(1)} %precondition.2.refs_0_), channel_id=1, source_target_pairs={{0,4},{1,5},{4,8},{5,9},{8,12},{9,13},{12,14},{13,15},{14,10},{15,... | collective-permute-start | bytes 1572872 | tf_op jit(solution)/shard_map/ppermute | solution.py:146
  8.2 14.8 %collective-permute-start.11 = (bf16[16,16384]{1,0:T(8,128)(2,1)S(1)}, bf16[16,16384]{1,0:T(8,128)(2,1)S(1)}, u32[]{:S(2)}, u32[]{:S(2)}) collective-permute-start(bf16[16,16384]{1,0:T(8,128)(2,1)S(1)} %precondition.2.refs_0_), channel_id=1, source_target_pairs={{0,2},{1,3},{4,0},{5,1},{8,4},{9,5},{12,8},{13,9},{14,12},{15,13},... | collective-permute-start | bytes 1572872 | tf_op jit(solution)/shard_map/ppermute | solution.py:146
  9.7 22.2 %collective-permute-start.15 = (bf16[16,16384]{1,0:T(8,128)(2,1)S(1)}, bf16[16,16384]{1,0:T(8,128)(2,1)S(1)}, u32[]{:S(2)}, u32[]{:S(2)}) collective-permute-start(bf16[16,16384]{1,0:T(8,128)(2,1)S(1)} %precondition.3.refs_1_), channel_id=1, source_target_pairs={{0,4},{1,5},{4,8},{5,9},{8,12},{9,13},{12,14},{13,15},{14,10},{15,... | collective-permute-start | bytes 1572872 | tf_op jit(solution)/shard_map/ppermute | solution.py:146
  11.8 20.2 %collective-permute-start.29 = (bf16[16,16384]{1,0:T(8,128)(2,1)S(1)}, bf16[16,16384]{1,0:T(8,128)(2,1)S(1)}, u32[]{:S(2)}, u32[]{:S(2)}) collective-permute-start(bf16[16,16384]{1,0:T(8,128)(2,1)S(1)} %precondition.3.refs_1_), channel_id=1, source_target_pairs={{0,1},{1,0},{2,3},{3,2},{4,5},{5,4},{6,7},{7,6},{8,9},{9,8},{10,11... | collective-permute-start | bytes 1572872 | tf_op jit(solution)/shard_map/ppermute | solution.py:146
  12.5 22.0 %collective-permute-start.5 = (bf16[16,16384]{1,0:T(8,128)(2,1)S(1)}, bf16[16,16384]{1,0:T(8,128)(2,1)S(1)}, u32[]{:S(2)}, u32[]{:S(2)}) collective-permute-start(bf16[16,16384]{1,0:T(8,128)(2,1)S(1)} %precondition.3.refs_1_), channel_id=1, source_target_pairs={{0,2},{1,3},{4,0},{5,1},{8,4},{9,5},{12,8},{13,9},{14,12},{15,13},... | collective-permute-start | bytes 1572872 | tf_op jit(solution)/shard_map/ppermute | solution.py:146
  12.6 0.8 copy-start.18
  20.9 14.7 %collective-permute-start.24 = (bf16[16,16384]{1,0:T(8,128)(2,1)S(1)}, bf16[16,16384]{1,0:T(8,128)(2,1)S(1)}, u32[]{:S(2)}, u32[]{:S(2)}) collective-permute-start(bf16[16,16384]{1,0:T(8,128)(2,1)S(1)} %collective-permute-done.refs_0_), channel_id=1, source_target_pairs={{0,1},{1,0},{2,3},{3,2},{4,5},{5,4},{6,7},{7,6},{8,9},{9,8},{10,11... | collective-permute-start | bytes 1572872 | tf_op jit(solution)/shard_map/ppermute | solution.py:146
  23.0 16.1 %collective-permute-start.25 = (bf16[16,16384]{1,0:T(8,128)(2,1)S(1)}, bf16[16,16384]{1,0:T(8,128)(2,1)S(1)}, u32[]{:S(2)}, u32[]{:S(2)}) collective-permute-start(bf16[16,16384]{1,0:T(8,128)(2,1)S(1)} %collective-permute-done.11.refs_2_), channel_id=1, source_target_pairs={{0,1},{1,0},{2,3},{3,2},{4,5},{5,4},{6,7},{7,6},{8,9},{9,8},{10,11... | collective-permute-start | bytes 1572872 | tf_op jit(solution)/shard_map/ppermute | solution.py:146
  31.9 8.0 %collective-permute-start.26 = (bf16[16,16384]{1,0:T(8,128)(2,1)S(1)}, bf16[16,16384]{1,0:T(8,128)(2,1)S(1)}, u32[]{:S(2)}, u32[]{:S(2)}) collective-permute-start(bf16[16,16384]{1,0:T(8,128)(2,1)S(1)} %collective-permute-done.15.refs_4_), channel_id=1, source_target_pairs={{0,1},{1,0},{2,3},{3,2},{4,5},{5,4},{6,7},{7,6},{8,9},{9,8},{10,11... | collective-permute-start | bytes 1572872 | tf_op jit(solution)/shard_map/ppermute | solution.py:146
  31.9 0.8 copy-start.22
  32.8 14.7 %collective-permute-start.1 = (bf16[16,16384]{1,0:T(8,128)(2,1)S(1)}, bf16[16,16384]{1,0:T(8,128)(2,1)S(1)}, u32[]{:S(2)}, u32[]{:S(2)}) collective-permute-start(bf16[16,16384]{1,0:T(8,128)(2,1)S(1)} %collective-permute-done.refs_0_), channel_id=1, source_target_pairs={{0,4},{1,5},{4,8},{5,9},{8,12},{9,13},{12,14},{13,15},{14,10},{15,... | collective-permute-start | bytes 1572872 | tf_op jit(solution)/shard_map/ppermute | solution.py:146
  34.6 14.9 %collective-permute-start.12 = (bf16[16,16384]{1,0:T(8,128)(2,1)S(1)}, bf16[16,16384]{1,0:T(8,128)(2,1)}, u32[]{:S(2)}, u32[]{:S(2)}) collective-permute-start(bf16[16,16384]{1,0:T(8,128)(2,1)S(1)} %collective-permute-done.11.refs_2_), channel_id=1, source_target_pairs={{0,2},{1,3},{4,0},{5,1},{8,4},{9,5},{12,8},{13,9},{14,12},{15,13},... | collective-permute-start | bytes 1572872 | tf_op jit(solution)/shard_map/ppermute | solution.py:146
  34.8 0.8 copy-start.2
  35.6 0.8 copy-start.12
  36.5 22.0 %collective-permute-start.16 = (bf16[16,16384]{1,0:T(8,128)(2,1)S(1)}, bf16[16,16384]{1,0:T(8,128)(2,1)}, u32[]{:S(2)}, u32[]{:S(2)}) collective-permute-start(bf16[16,16384]{1,0:T(8,128)(2,1)S(1)} %collective-permute-done.15.refs_4_), channel_id=1, source_target_pairs={{0,4},{1,5},{4,8},{5,9},{8,12},{9,13},{12,14},{13,15},{14,10},{15,... | collective-permute-start | bytes 1572872 | tf_op jit(solution)/shard_map/ppermute | solution.py:146
  39.0 0.8 copy-start.16
  39.9 18.6 %collective-permute-start.27 = (bf16[16,16384]{1,0:T(8,128)(2,1)S(1)}, bf16[16,16384]{1,0:T(8,128)(2,1)S(1)}, u32[]{:S(2)}, u32[]{:S(2)}) collective-permute-start(bf16[16,16384]{1,0:T(8,128)(2,1)S(1)} %collective-permute-done.5.refs_6_), channel_id=1, source_target_pairs={{0,1},{1,0},{2,3},{3,2},{4,5},{5,4},{6,7},{7,6},{8,9},{9,8},{10,11... | collective-permute-start | bytes 1572872 | tf_op jit(solution)/shard_map/ppermute | solution.py:146
  39.9 0.8 copy-start.20
  40.7 21.2 %collective-permute-start.6 = (bf16[16,16384]{1,0:T(8,128)(2,1)S(1)}, bf16[16,16384]{1,0:T(8,128)(2,1)S(1)}, u32[]{:S(2)}, u32[]{:S(2)}) collective-permute-start(bf16[16,16384]{1,0:T(8,128)(2,1)S(1)} %collective-permute-done.5.refs_6_), channel_id=1, source_target_pairs={{0,2},{1,3},{4,0},{5,1},{8,4},{9,5},{12,8},{13,9},{14,12},{15,13},... | collective-permute-start | bytes 1572872 | tf_op jit(solution)/shard_map/ppermute | solution.py:146
  40.9 0.8 copy-start.6
  47.5 14.6 %collective-permute-start.20 = (bf16[16,16384]{1,0:T(8,128)(2,1)S(1)}, bf16[16,16384]{1,0:T(8,128)(2,1)S(1)}, u32[]{:S(2)}, u32[]{:S(2)}) collective-permute-start(bf16[16,16384]{1,0:T(8,128)(2,1)S(1)} %collective-permute-done.1.refs_0_), channel_id=1, source_target_pairs={{0,1},{1,0},{2,3},{3,2},{4,5},{5,4},{6,7},{7,6},{8,9},{9,8},{10,11... | collective-permute-start | bytes 1572872 | tf_op jit(solution)/shard_map/ppermute | solution.py:146
  49.4 15.2 %collective-permute-start.21 = (bf16[16,16384]{1,0:T(8,128)(2,1)}, bf16[16,16384]{1,0:T(8,128)(2,1)S(1)}, u32[]{:S(2)}, u32[]{:S(2)}) collective-permute-start(bf16[16,16384]{1,0:T(8,128)(2,1)} %collective-permute-done.12.refs_2_), channel_id=1, source_target_pairs={{0,1},{1,0},{2,3},{3,2},{4,5},{5,4},{6,7},{7,6},{8,9},{9,8},{10,11... | collective-permute-start | bytes 1572872 | tf_op jit(solution)/shard_map/ppermute | solution.py:146
  58.4 8.7 %collective-permute-start.22 = (bf16[16,16384]{1,0:T(8,128)(2,1)}, bf16[16,16384]{1,0:T(8,128)(2,1)}, u32[]{:S(2)}, u32[]{:S(2)}) collective-permute-start(bf16[16,16384]{1,0:T(8,128)(2,1)} %collective-permute-done.16.refs_4_), channel_id=1, source_target_pairs={{0,1},{1,0},{2,3},{3,2},{4,5},{5,4},{6,7},{7,6},{8,9},{9,8},{10,11... | collective-permute-start | bytes 1572872 | tf_op jit(solution)/shard_map/ppermute | solution.py:146
  58.4 0.8 copy-start.30
  59.3 14.8 %collective-permute-start.2 = (bf16[16,16384]{1,0:T(8,128)(2,1)S(1)}, bf16[16,16384]{1,0:T(8,128)(2,1)}, u32[]{:S(2)}, u32[]{:S(2)}) collective-permute-start(bf16[16,16384]{1,0:T(8,128)(2,1)S(1)} %collective-permute-done.1.refs_0_), channel_id=1, source_target_pairs={{0,4},{1,5},{4,8},{5,9},{8,12},{9,13},{12,14},{13,15},{14,10},{15,... | collective-permute-start | bytes 1572872 | tf_op jit(solution)/shard_map/ppermute | solution.py:146
  61.1 0.8 copy-start.14
  61.9 12.2 %collective-permute-start.23 = (bf16[16,16384]{1,0:T(8,128)(2,1)S(1)}, bf16[16,16384]{1,0:T(8,128)(2,1)}, u32[]{:S(2)}, u32[]{:S(2)}) collective-permute-start(bf16[16,16384]{1,0:T(8,128)(2,1)S(1)} %collective-permute-done.6.refs_6_), channel_id=1, source_target_pairs={{0,1},{1,0},{2,3},{3,2},{4,5},{5,4},{6,7},{7,6},{8,9},{9,8},{10,11... | collective-permute-start | bytes 1572872 | tf_op jit(solution)/shard_map/ppermute | solution.py:146
  62.1 0.8 copy-start.26
  62.9 14.9 %collective-permute-start.7 = (bf16[16,16384]{1,0:T(8,128)(2,1)S(1)}, bf16[16,16384]{1,0:T(8,128)(2,1)}, u32[]{:S(2)}, u32[]{:S(2)}) collective-permute-start(bf16[16,16384]{1,0:T(8,128)(2,1)S(1)} %collective-permute-done.6.refs_6_), channel_id=1, source_target_pairs={{0,2},{1,3},{4,0},{5,1},{8,4},{9,5},{12,8},{13,9},{14,12},{15,13},... | collective-permute-start | bytes 1572872 | tf_op jit(solution)/shard_map/ppermute | solution.py:146
  63.1 0.8 copy-start.24
  64.6 0.8 copy-start.28
  65.4 30.4 %collective-permute-start.13 = (bf16[16,16384]{1,0:T(8,128)(2,1)}, bf16[16,16384]{1,0:T(8,128)(2,1)}, u32[]{:S(2)}, u32[]{:S(2)}) collective-permute-start(bf16[16,16384]{1,0:T(8,128)(2,1)} %collective-permute-done.12.refs_2_), channel_id=1, source_target_pairs={{0,2},{1,3},{4,0},{5,1},{8,4},{9,5},{12,8},{13,9},{14,12},{15,13},... | collective-permute-start | bytes 1572872 | tf_op jit(solution)/shard_map/ppermute | solution.py:146
  67.2 28.7 %collective-permute-start.17 = (bf16[16,16384]{1,0:T(8,128)(2,1)}, bf16[16,16384]{1,0:T(8,128)(2,1)}, u32[]{:S(2)}, u32[]{:S(2)}) collective-permute-start(bf16[16,16384]{1,0:T(8,128)(2,1)} %collective-permute-done.16.refs_4_), channel_id=1, source_target_pairs={{0,4},{1,5},{4,8},{5,9},{8,12},{9,13},{12,14},{13,15},{14,10},{15,... | collective-permute-start | bytes 1572872 | tf_op jit(solution)/shard_map/ppermute | solution.py:146
  74.1 22.4 %collective-permute-start.10 = (bf16[16,16384]{1,0:T(8,128)(2,1)}, bf16[16,16384]{1,0:T(8,128)(2,1)S(1)}, u32[]{:S(2)}, u32[]{:S(2)}) collective-permute-start(bf16[16,16384]{1,0:T(8,128)(2,1)} %collective-permute-done.2.refs_0_), channel_id=1, source_target_pairs={{0,1},{1,0},{2,3},{3,2},{4,5},{5,4},{6,7},{7,6},{8,9},{9,8},{10,11... | collective-permute-start | bytes 1572872 | tf_op jit(solution)/shard_map/ppermute | solution.py:146
  74.1 34.1 %collective-permute-start.3 = (bf16[16,16384]{1,0:T(8,128)(2,1)}, bf16[16,16384]{1,0:T(8,128)(2,1)}, u32[]{:S(2)}, u32[]{:S(2)}) collective-permute-start(bf16[16,16384]{1,0:T(8,128)(2,1)} %collective-permute-done.2.refs_0_), channel_id=1, source_target_pairs={{0,4},{1,5},{4,8},{5,9},{8,12},{9,13},{12,14},{13,15},{14,10},{15,... | collective-permute-start | bytes 1572872 | tf_op jit(solution)/shard_map/ppermute | solution.py:146
  77.7 31.0 %collective-permute-start.8 = (bf16[16,16384]{1,0:T(8,128)(2,1)}, bf16[16,16384]{1,0:T(8,128)(2,1)}, u32[]{:S(2)}, u32[]{:S(2)}) collective-permute-start(bf16[16,16384]{1,0:T(8,128)(2,1)} %collective-permute-done.7.refs_6_), channel_id=1, source_target_pairs={{0,2},{1,3},{4,0},{5,1},{8,4},{9,5},{12,8},{13,9},{14,12},{15,13},... | collective-permute-start | bytes 1572872 | tf_op jit(solution)/shard_map/ppermute | solution.py:146
  78.0 5.8 %copy-start = (bf16[512,16384]{1,0:T(8,128)(2,1)S(1)}, bf16[512,16384]{1,0:T(8,128)(2,1)}, u32[]{:S(2)}) copy-start(bf16[512,16384]{1,0:T(8,128)(2,1)} %query_ref.9) | copy-start | bytes 50331652
  83.7 1.0 copy-start.9
  84.8 1.0 copy-start.11
  85.8 1.0 copy-start.19
  86.8 1.0 copy-start.23
  87.9 9.4 %copy-start.1 = (bf16[512,16384]{1,0:T(8,128)(2,1)S(1)}, bf16[512,16384]{1,0:T(8,128)(2,1)}, u32[]{:S(2)}) copy-start(bf16[512,16384]{1,0:T(8,128)(2,1)} %query_ref.9) | copy-start | bytes 50331652
  87.9 9.4 %copy-start.3 = (bf16[16,16384]{1,0:T(8,128)(2,1)S(1)}, bf16[16,16384]{1,0:T(8,128)(2,1)}, u32[]{:S(2)}) copy-start(bf16[16,16384]{1,0:T(8,128)(2,1)} %copy-done.2) | copy-start | bytes 1572868
  87.9 9.4 %copy-start.5 = (bf16[16,16384]{1,0:T(8,128)(2,1)S(1)}, bf16[16,16384]{1,0:T(8,128)(2,1)}, u32[]{:S(2)}) copy-start(bf16[16,16384]{1,0:T(8,128)(2,1)} %copy-done.4) | copy-start | bytes 1572868
  87.9 9.4 %copy-start.7 = (bf16[16,16384]{1,0:T(8,128)(2,1)S(1)}, bf16[16,16384]{1,0:T(8,128)(2,1)}, u32[]{:S(2)}) copy-start(bf16[16,16384]{1,0:T(8,128)(2,1)} %copy-done.6) | copy-start | bytes 1572868
  87.9 9.4 %copy-start.13 = (bf16[16,16384]{1,0:T(8,128)(2,1)S(1)}, bf16[16,16384]{1,0:T(8,128)(2,1)}, u32[]{:S(2)}) copy-start(bf16[16,16384]{1,0:T(8,128)(2,1)} %copy-done.12) | copy-start | bytes 1572868
  87.9 9.4 %copy-start.17 = (bf16[16,16384]{1,0:T(8,128)(2,1)S(1)}, bf16[16,16384]{1,0:T(8,128)(2,1)}, u32[]{:S(2)}) copy-start(bf16[16,16384]{1,0:T(8,128)(2,1)} %copy-done.16) | copy-start | bytes 1572868
  87.9 20.9 %copy-start.15 = (bf16[16,16384]{1,0:T(8,128)(2,1)S(1)}, bf16[16,16384]{1,0:T(8,128)(2,1)}, u32[]{:S(2)}) copy-start(bf16[16,16384]{1,0:T(8,128)(2,1)} %copy-done.14) | copy-start | bytes 1572868
  95.9 22.1 %collective-permute-start.19 = (bf16[16,16384]{1,0:T(8,128)(2,1)}, bf16[16,16384]{1,0:T(8,128)(2,1)S(1)}, u32[]{:S(2)}, u32[]{:S(2)}) collective-permute-start(bf16[16,16384]{1,0:T(8,128)(2,1)} %collective-permute-done.7.refs_6_), channel_id=1, source_target_pairs={{0,1},{1,0},{2,3},{3,2},{4,5},{5,4},{6,7},{7,6},{8,9},{9,8},{10,11... | collective-permute-start | bytes 1572872 | tf_op jit(solution)/shard_map/ppermute | solution.py:146
  95.9 22.0 %collective-permute-start.14 = (bf16[16,16384]{1,0:T(8,128)(2,1)}, bf16[16,16384]{1,0:T(8,128)(2,1)S(1)}, u32[]{:S(2)}, u32[]{:S(2)}) collective-permute-start(bf16[16,16384]{1,0:T(8,128)(2,1)} %collective-permute-done.13.refs_2_), channel_id=1, source_target_pairs={{0,1},{1,0},{2,3},{3,2},{4,5},{5,4},{6,7},{7,6},{8,9},{9,8},{10,11... | collective-permute-start | bytes 1572872 | tf_op jit(solution)/shard_map/ppermute | solution.py:146
  96.4 0.8 copy-start.32
  97.2 20.7 %collective-permute-start.18 = (bf16[16,16384]{1,0:T(8,128)(2,1)}, bf16[16,16384]{1,0:T(8,128)(2,1)S(1)}, u32[]{:S(2)}, u32[]{:S(2)}) collective-permute-start(bf16[16,16384]{1,0:T(8,128)(2,1)} %collective-permute-done.17.refs_4_), channel_id=1, source_target_pairs={{0,1},{1,0},{2,3},{3,2},{4,5},{5,4},{6,7},{7,6},{8,9},{9,8},{10,11... | collective-permute-start | bytes 1572872 | tf_op jit(solution)/shard_map/ppermute | solution.py:146
  97.3 1.0 copy-start.21
  98.4 1.0 copy-start.31
  99.4 9.4 %copy-start.25 = (bf16[16,16384]{1,0:T(8,128)(2,1)S(1)}, bf16[16,16384]{1,0:T(8,128)(2,1)}, u32[]{:S(2)}) copy-start(bf16[16,16384]{1,0:T(8,128)(2,1)} %copy-done.24) | copy-start | bytes 1572868
  99.4 9.4 %copy-start.27 = (bf16[16,16384]{1,0:T(8,128)(2,1)S(1)}, bf16[16,16384]{1,0:T(8,128)(2,1)}, u32[]{:S(2)}) copy-start(bf16[16,16384]{1,0:T(8,128)(2,1)} %copy-done.26) | copy-start | bytes 1572868
  99.4 9.4 %copy-start.29 = (bf16[16,16384]{1,0:T(8,128)(2,1)S(1)}, bf16[16,16384]{1,0:T(8,128)(2,1)}, u32[]{:S(2)}) copy-start(bf16[16,16384]{1,0:T(8,128)(2,1)} %copy-done.28) | copy-start | bytes 1572868
  108.2 9.8 %copy-start.33 = (bf16[16,16384]{1,0:T(8,128)(2,1)S(1)}, bf16[16,16384]{1,0:T(8,128)(2,1)}, u32[]{:S(2)}) copy-start(bf16[16,16384]{1,0:T(8,128)(2,1)} %copy-done.32) | copy-start | bytes 1572868
  108.2 18.8 %collective-permute-start.4 = (bf16[16,16384]{1,0:T(8,128)(2,1)}, bf16[16,16384]{1,0:T(8,128)(2,1)S(1)}, u32[]{:S(2)}, u32[]{:S(2)}) collective-permute-start(bf16[16,16384]{1,0:T(8,128)(2,1)} %collective-permute-done.3.refs_0_), channel_id=1, source_target_pairs={{0,1},{1,0},{2,3},{3,2},{4,5},{5,4},{6,7},{7,6},{8,9},{9,8},{10,11... | collective-permute-start | bytes 1572872 | tf_op jit(solution)/shard_map/ppermute | solution.py:146
  108.7 18.3 %collective-permute-start.9 = (bf16[16,16384]{1,0:T(8,128)(2,1)}, bf16[16,16384]{1,0:T(8,128)(2,1)S(1)}, u32[]{:S(2)}, u32[]{:S(2)}) collective-permute-start(bf16[16,16384]{1,0:T(8,128)(2,1)} %collective-permute-done.8.refs_2_), channel_id=1, source_target_pairs={{0,1},{1,0},{2,3},{3,2},{4,5},{5,4},{6,7},{7,6},{8,9},{9,8},{10,11... | collective-permute-start | bytes 1572872 | tf_op jit(solution)/shard_map/ppermute | solution.py:146
  (4 other events, 3.1 us)

commit v2 on v0

v2 whole, which is shorter than its diff:
```python
import functools

import jax
import jax.numpy as jnp
import numpy as np
from jax import lax
from jax.experimental import pallas as pl
from jax.experimental.pallas import tpu as pltpu
from jax.sharding import PartitionSpec as P

A_DIM = 128
B_DIM = 128
LANES = 128
K_TILE = 4096
KERNEL_VMEM = 16 << 20
PREPARE_COST = pl.CostEstimate(flops=1, bytes_accessed=1, transcendentals=0)
SCORE_COST = pl.CostEstimate(flops=1, bytes_accessed=1, transcendentals=0)
ANY_SPEC = pl.BlockSpec(memory_space=pl.ANY)
VMEM_SPEC = pl.BlockSpec(memory_space=pltpu.VMEM)

DAMPING = 0.1


def chip_ring(chips):
    if chips == 8:
        return list(range(0, chips, 2)) + list(range(chips - 1, 0, -2))
    return list(range(chips))


def precondition_kernel(*refs):
    sources, out_ref, arrived = refs[:4], refs[4], refs[5:9]
    gather_ref, spread_ref, sems = refs[9:]
    fetches = [pltpu.make_async_copy(a, b, sems.at[i]) for i, (a, b) in enumerate(zip(sources, arrived))]
    for fetch in fetches:
        fetch.start()
    for fetch in fetches:
        fetch.wait()
    rows_ref, left_ref, right_ref, eig_ref = arrived
    count = gather_ref.shape[0] // A_DIM
    left = left_ref[...]
    right = right_ref[...]
    damped = eig_ref[...] + DAMPING

    def stack(wide):
        return jnp.concatenate([wide[:, q * B_DIM:(q + 1) * B_DIM] for q in range(count)], axis=0)

    for base in range(0, rows_ref.shape[0], count):
        rows = slice(base, base + count)
        for a in range(A_DIM):
            gather_ref[a * count:(a + 1) * count, :] = rows_ref[rows, a * B_DIM:(a + 1) * B_DIM].astype(jnp.float32)
        matrix = jnp.concatenate(
            [gather_ref[pl.ds(q, A_DIM, stride=count), :].astype(jnp.bfloat16) for q in range(count)], axis=1
        )
        inward = lax.dot_general(left, matrix, (((0,), (0,)), ((), ())), preferred_element_type=jnp.float32)
        rotated = jnp.dot(stack(inward.astype(jnp.bfloat16)), right, preferred_element_type=jnp.float32)
        scaled = jnp.concatenate(
            [(rotated[q * A_DIM:(q + 1) * A_DIM] / damped).astype(jnp.bfloat16) for q in range(count)], axis=1
        )
        restored = jnp.dot(left, scaled, preferred_element_type=jnp.float32).astype(jnp.bfloat16)
        prepared = lax.dot_general(
            stack(restored), right, (((1,), (1,)), ((), ())), preferred_element_type=jnp.float32
        )
        for q in range(count):
            spread_ref[pl.ds(q, A_DIM, stride=count), :] = prepared[q * A_DIM:(q + 1) * A_DIM]
        for a in range(A_DIM):
            out_ref[rows, a * B_DIM:(a + 1) * B_DIM] = spread_ref[a * count:(a + 1) * count, :].astype(jnp.bfloat16)


def precondition(rows, *factors):
    operands = rows, *[pltpu.with_memory_space_constraint(m, pltpu.HBM) for m in factors]
    return pl.pallas_call(
        precondition_kernel,
        out_shape=jax.ShapeDtypeStruct(rows.shape, jnp.bfloat16),
        in_specs=[ANY_SPEC] * 4,
        out_specs=VMEM_SPEC,
        scratch_shapes=[pltpu.VMEM(m.shape, m.dtype) for m in operands]
        + [pltpu.VMEM((A_DIM * 16, B_DIM), jnp.float32)] * 2
        + [pltpu.SemaphoreType.DMA((4,))],
        compiler_params=pltpu.CompilerParams(vmem_limit_bytes=KERNEL_VMEM),
        cost_estimate=PREPARE_COST,
        name="precondition",
    )(*operands)


def scores_kernel(entries, first, last, owners_ref, query_ref, *refs):
    blocks, refs = refs[:len(entries)], refs[len(entries):]
    if not first:
        total_ref, refs = refs[0], refs[1:]
    out_ref, weight_ref, sum_ref, sems = refs
    height, width = blocks[0].shape
    steps = width // K_TILE

    def fetches(step):
        return [
            pltpu.make_async_copy(
                block.at[:, pl.ds(pl.multiple_of(step * K_TILE, K_TILE), K_TILE)],
                weight_ref.at[lax.rem(step, 2), pl.ds(i * height, height), :],
                sems.at[lax.rem(step, 2), i],
            )
            for i, block in enumerate(blocks)
        ]

    for fetch in fetches(0):
        fetch.start()
    if first:
        out_ref[...] = jnp.zeros_like(out_ref)
    if last:
        out_ref[...] = total_ref[...]
    sum_ref[...] = jnp.zeros_like(sum_ref)

    @pl.loop(0, steps)
    def _(step):
        @pl.when(step + 1 < steps)
        def _():
            for fetch in fetches(step + 1):
                fetch.start()

        for fetch in fetches(step):
            fetch.wait()
        sum_ref[...] += lax.dot_general(
            query_ref[:, pl.ds(pl.multiple_of(step * K_TILE, K_TILE), K_TILE)],
            weight_ref[lax.rem(step, 2)],
            (((1,), (1,)), ((), ())),
            preferred_element_type=jnp.float32,
        )

    place = lax.broadcasted_iota(jnp.int32, sum_ref.shape, 1) // height
    per_tile = LANES // height
    for i, entry in enumerate(entries):
        owner = owners_ref[entry]
        spot = lax.rem(owner, per_tile)
        moved = pltpu.roll(sum_ref[...], lax.rem(spot - i + per_tile, per_tile) * height, 1)
        lanes = pl.ds(pl.multiple_of(lax.div(owner, per_tile) * LANES, LANES), LANES)
        out_ref[:, lanes] += jnp.where(place == spot, moved, 0.0)


def add_scores(total, queries, owners, entries, blocks, train_count, last):
    rows = queries.shape[0]
    first = total is None
    operands = [pltpu.with_memory_space_constraint(queries, pltpu.VMEM), *blocks] + ([] if first else [total])
    return pl.pallas_call(
        functools.partial(scores_kernel, entries, first, last),
        out_shape=jax.ShapeDtypeStruct((rows, train_count), jnp.float32),
        in_specs=[pl.BlockSpec(memory_space=pltpu.SMEM), VMEM_SPEC]
        + [ANY_SPEC] * len(blocks)
        + ([] if first else [VMEM_SPEC]),
        out_specs=VMEM_SPEC,
        scratch_shapes=[
            pltpu.VMEM((2, LANES, K_TILE), jnp.bfloat16),
            pltpu.VMEM((rows, LANES), jnp.float32),
            pltpu.SemaphoreType.DMA((2, len(blocks))),
        ],
        input_output_aliases={} if first or last else {len(operands): 0},
        compiler_params=pltpu.CompilerParams(vmem_limit_bytes=KERNEL_VMEM),
        cost_estimate=SCORE_COST,
        name="scores",
    )(owners, *operands)


def per_device(queries, train_rows, left_basis, right_basis, eigenvalues):
    devices = lax.axis_size("wide")
    chips = devices // 2
    ring = chip_ring(chips)
    hops = chips // 2
    train_count = devices * train_rows.shape[0]

    along = [
        (2 * ring[i] + core, 2 * ring[(i + (-1 if core else 1)) % chips] + core)
        for i in range(chips)
        for core in range(2)
    ]
    across = [(d, d ^ 1) for d in range(devices)]
    send = lambda block, pairs: lax.ppermute(block, "wide", pairs)

    table = np.zeros((devices, devices), np.int32)
    for i in range(chips):
        for core in range(2):
            row = [2 * ring[i] + core, 2 * ring[i] + 1 - core]
            for arrival in range(1, chips):
                hop, swapped = (arrival + 1) // 2, (arrival + 1) % 2
                step = hop if core else -hop
                row += [
                    2 * ring[(i + step) % chips] + (core ^ swapped),
                    2 * ring[(i - step) % chips] + (1 ^ core ^ swapped),
                ]
            table[row[0]] = row
    owners = lax.dynamic_index_in_dim(jnp.asarray(table), lax.axis_index("wide"), 0, keepdims=False)

    def after(block, array):
        return lax.optimization_barrier((block, array))

    raw = train_rows
    factors = left_basis, right_basis, eigenvalues
    other = precondition(send(train_rows, across), *factors)
    train_rows, other = after(train_rows, other)
    own = precondition(train_rows, *factors)
    chains = [raw, other]
    blocks = [own, other]
    total, done = None, 0
    for arrival in range(1, chips):
        chain = (arrival + 1) % 2
        block = send(chains[chain], along)
        if arrival > 2 and chain == 0:
            entries = list(range(done, done + 4))
            total = add_scores(total, queries, owners, entries, [blocks[e] for e in entries], train_count, False)
            done += 4
            block, total = after(block, total)
        if arrival == 1:
            block = precondition(block, *factors)
        if arrival > 1 and chain == 1:
            if total is None:
                own, block = after(own, block)
                blocks[0] = own
            else:
                total, block = after(total, block)
        chains[chain] = block
        blocks += [block, send(block, across)]
    return add_scores(total, queries, owners, list(range(done, devices)), blocks[done:], train_count, True)


def solution(mesh):
    in_specs = (P(("grp", "wide"), None), P(("grp", "wide"), None), P(), P(), P())
    out_specs = P(("grp", "wide"), None)
    return jax.shard_map(
        per_device, mesh=mesh, in_specs=in_specs, out_specs=out_specs, check_vma=False
    )
```

time: 182 us -> 95.5 us (0.52)
  waiting for transfers between devices: 130 us -> 30.2 us
  Pallas kernels: 0 us -> 39.4 us
  matrix products: 33.2 us -> 0 us
  starting transfers between devices: 0.01 us -> 17.5 us
  between operations: 13.4 us -> 0.25 us
  local copies, waits for them, and re-layouts: 4.42 us -> 7.69 us
    all_gather x1 -> x0, waiting for transfers between devices: 130 us -> none  [per_device(): gathered = lax.all_gather(prepared, 'wide', axis=0, tiled=True)]
    pallas_call x0 -> x7, Pallas kernels: none -> 39.4 us  [the longest x4 28.9 us: add_scores(): pl.pallas_call(functools.partial(scores_kernel, entries, first, last), ou...]
    dot_general x4 -> x0, matrix products: 33.2 us -> none  [the longest x1 29.9 us: against(): lax.dot_general(query_rows, train_piece, (((1,), (1,)), ((), ())), prefer...]
    ppermute x0 -> x15, waiting for transfers between devices: none -> 30.2 us  [per_device(): send = lambda block, pairs: lax.ppermute(block, 'wide', pairs)]
    ppermute x0 -> x15, starting transfers between devices: none -> 17.5 us  [per_device(): send = lambda block, pairs: lax.ppermute(block, 'wide', pairs)]
    unnamed x4 -> x6, local copies, waits for them, and re-layouts: 3.12 us -> 7 us
  transfers between devices with their start and end apart: 1 -> 15, of which waited for: 1 -> 8; matrix products, arithmetic and copies ran while one was open for 0% -> 1% of each run, Pallas kernels for 0% -> 34%
where the time goes in v2:
time: 95.5 us; the launch traced here: 95.1 us
  Pallas kernels  39.4 us (41%)
  waiting for transfers between devices  30.2 us (32%)
  starting transfers between devices  17.5 us (18%)
  local copies, waits for them, and re-layouts  7.69 us (8%)
    ppermute x15, waiting for transfers between devices, per_device(): send = lambda block, pairs: lax.ppermute(block, 'wide', pairs)  30.2 us
    pallas_call x4, Pallas kernels, add_scores(): pl.pallas_call(functools.partial(scores_kernel, entries, first, last), ou...  28.9 us
    ppermute x15, starting transfers between devices, per_device(): send = lambda block, pairs: lax.ppermute(block, 'wide', pairs)  17.5 us
    pallas_call x3, Pallas kernels, precondition(): pl.pallas_call(precondition_kernel, out_shape=jax.ShapeDtypeStruct(rows.s...  10.6 us
    unnamed x6, local copies, waits for them, and re-layouts  7 us
  transfers between devices with their start and end apart: 15, of which 8 were waited for; matrix products, arithmetic and copies ran while one was open for 1% of the time, Pallas kernels for 34%

profile of v2, /device:TPU:0, one launch (start us, length us, event | category | flops | bytes accessed | tf_op | source)
XLA Modules:
  0.0 95.1 jit_solution(2080033449954529328)
XLA Ops:
  0.0 0.5 collective-permute-start.2
  0.5 2.6 %collective-permute-start = (bf16[32,16384]{1,0:T(8,128)(2,1)}, bf16[32,16384]{1,0:T(8,128)(2,1)S(1)}, u32[]{:S(2)}, u32[]{:S(2)}) collective-permute-start(bf16[32,16384]{1,0:T(8,128)(2,1)} %refs_0_), channel_id=1, source_target_pairs={{0,4},{1,3},{4,8},{5,1},{8,12},{9,5},{12,14},{13,9},{14,10},{15,13... | collective-permute-start | bytes 3145736 | tf_op jit(solution)/shard_map/ppermute | solution.py:173
  3.0 0.0 collective-permute-done.2.refs_0_
  3.0 3.5 %precondition.4.refs_1_ = bf16[32,16384]{1,0:T(8,128)(2,1)S(1)} custom-call(bf16[32,16384]{1,0:T(8,128)(2,1)S(1)} %collective-permute-done.2.refs_0_, bf16[128,128]{1,0:T(8,128)(2,1)} %refs_1_.5, bf16[128,128]{1,0:T(8,128)(2,1)} %refs_2_.5, f32[128,128]{1,0:T(8,128)} %refs_3_.5), custom_call_target="tpu_custom_call" | custom-call | flops 1 | bytes 1 | tf_op jit(solution)/shard_map/precondition/pallas_call | solution.py:71
  6.6 2.9 %collective-permute-start.3 = (bf16[32,16384]{1,0:T(8,128)(2,1)S(1)}, bf16[32,16384]{1,0:T(8,128)(2,1)S(1)}, u32[]{:S(2)}, u32[]{:S(2)}) collective-permute-start(bf16[32,16384]{1,0:T(8,128)(2,1)S(1)} %precondition.4.refs_1_), channel_id=1, source_target_pairs={{0,4},{1,3},{4,8},{5,1},{8,12},{9,5},{12,14},{13,9},{14,10},{15,13... | collective-permute-start | bytes 3145736 | tf_op jit(solution)/shard_map/ppermute | solution.py:173
  9.5 6.5 %collective-permute-done.refs_0_ = bf16[32,16384]{1,0:T(8,128)(2,1)S(1)} collective-permute-done((bf16[32,16384]{1,0:T(8,128)(2,1)}, bf16[32,16384]{1,0:T(8,128)(2,1)S(1)}, u32[]{:S(2)}, u32[]{:S(2)}) %collective-permute-start) | collective-permute-done | bytes 1048608 | tf_op jit(solution)/shard_map/ppermute | solution.py:173
  16.0 3.5 %precondition.3.refs_2_ = bf16[32,16384]{1,0:T(8,128)(2,1)S(1)} custom-call(bf16[32,16384]{1,0:T(8,128)(2,1)S(1)} %collective-permute-done.refs_0_, bf16[128,128]{1,0:T(8,128)(2,1)} %refs_1_.5, bf16[128,128]{1,0:T(8,128)(2,1)} %refs_2_.5, f32[128,128]{1,0:T(8,128)} %refs_3_.5), custom_call_target="tpu_custom_call" | custom-call | flops 1 | bytes 1 | tf_op jit(solution)/shard_map/precondition/pallas_call | solution.py:71
  19.5 0.1 collective-permute-start.4
  19.6 2.1 %collective-permute-start.1 = (bf16[32,16384]{1,0:T(8,128)(2,1)S(1)}, bf16[32,16384]{1,0:T(8,128)(2,1)}, u32[]{:S(2)}, u32[]{:S(2)}) collective-permute-start(bf16[32,16384]{1,0:T(8,128)(2,1)S(1)} %precondition.3.refs_2_), channel_id=1, source_target_pairs={{0,4},{1,3},{4,8},{5,1},{8,12},{9,5},{12,14},{13,9},{14,10},{15,13... | collective-permute-start | bytes 3145736 | tf_op jit(solution)/shard_map/ppermute | solution.py:173
  21.7 0.7 dynamic-slice_bitcast_fusion.owners_ref
  22.4 0.0 copy-start.2
  22.4 1.2 %copy-done.2 = bf16[32,16384]{1,0:T(8,128)(2,1)S(1)} copy-done((bf16[32,16384]{1,0:T(8,128)(2,1)S(1)}, bf16[32,16384]{1,0:T(8,128)(2,1)}, u32[]{:S(2)}) %copy-start.2) | copy-done | bytes 1048600
  23.6 3.5 %precondition.5.refs_0_ = bf16[32,16384]{1,0:T(8,128)(2,1)S(1)} custom-call(bf16[32,16384]{1,0:T(8,128)(2,1)S(1)} %copy-done.2, bf16[128,128]{1,0:T(8,128)(2,1)} %refs_1_.5, bf16[128,128]{1,0:T(8,128)(2,1)} %refs_2_.5, f32[128,128]{1,0:T(8,128)} %refs_3_.5), custom_call_target="tpu_custom_call" | custom-call | flops 1 | bytes 1 | tf_op jit(solution)/shard_map/precondition/pallas_call | solution.py:71
  27.1 0.1 collective-permute-done.3.refs_0_
  27.2 2.1 %collective-permute-start.8 = (bf16[32,16384]{1,0:T(8,128)(2,1)S(1)}, bf16[32,16384]{1,0:T(8,128)(2,1)S(1)}, u32[]{:S(2)}, u32[]{:S(2)}) collective-permute-start(bf16[32,16384]{1,0:T(8,128)(2,1)S(1)} %collective-permute-done.3.refs_0_), channel_id=1, source_target_pairs={{0,4},{1,3},{4,8},{5,1},{8,12},{9,5},{12,14},{13,9},{14,10},{15,13... | collective-permute-start | bytes 3145736 | tf_op jit(solution)/shard_map/ppermute | solution.py:173
  29.3 0.0 collective-permute-done.4.refs_3_
  29.3 0.0 copy-start
  29.3 5.8 %copy-done = bf16[512,16384]{1,0:T(8,128)(2,1)S(1)} copy-done((bf16[512,16384]{1,0:T(8,128)(2,1)S(1)}, bf16[512,16384]{1,0:T(8,128)(2,1)}, u32[]{:S(2)}) %copy-start) | copy-done | bytes 16777240
  35.0 0.0 copy-start.1
  35.0 7.9 %scores.4.refs_4_ = f32[512,512]{1,0:T(8,128)S(1)} custom-call(s32[16]{0:T(128)S(1)} %dynamic-slice_bitcast_fusion.owners_ref, bf16[512,16384]{1,0:T(8,128)(2,1)S(1)} %copy-done, bf16[32,16384]{1,0:T(8,128)(2,1)S(1)} %precondition.5.refs_0_, bf16[32,16384]{1,0:T(8,128)(2,1)S(1)} %precondition.4.refs_1_, bf16[32,16384]{1,0:T(8,128)(2,1)S(1)} %precondition.3.refs_2_, ...), custom_call_target="tpu_custom_call" | custom-call | flops 1 | bytes 1 | tf_op jit(solution)/shard_map/scores/pallas_call | solution.py:141
  42.9 0.0 collective-permute-done.1.refs_2_
  42.9 0.1 collective-permute-start.7
  43.0 0.5 collective-permute-start.6
  43.5 1.6 %collective-permute-start.5 = (bf16[32,16384]{1,0:T(8,128)(2,1)}, bf16[32,16384]{1,0:T(8,128)(2,1)S(1)}, u32[]{:S(2)}, u32[]{:S(2)}) collective-permute-start(bf16[32,16384]{1,0:T(8,128)(2,1)} %collective-permute-done.1.refs_2_), channel_id=1, source_target_pairs={{0,4},{1,3},{4,8},{5,1},{8,12},{9,5},{12,14},{13,9},{14,10},{15,13... | collective-permute-start | bytes 3145736 | tf_op jit(solution)/shard_map/ppermute | solution.py:173
  45.1 4.6 %collective-permute-done.8.refs_0_ = bf16[32,16384]{1,0:T(8,128)(2,1)S(1)} collective-permute-done((bf16[32,16384]{1,0:T(8,128)(2,1)S(1)}, bf16[32,16384]{1,0:T(8,128)(2,1)S(1)}, u32[]{:S(2)}, u32[]{:S(2)}) %collective-permute-start.8) | collective-permute-done | bytes 1048608 | tf_op jit(solution)/shard_map/ppermute | solution.py:173
  49.7 2.1 %collective-permute-start.9 = (bf16[32,16384]{1,0:T(8,128)(2,1)S(1)}, bf16[32,16384]{1,0:T(8,128)(2,1)S(1)}, u32[]{:S(2)}, u32[]{:S(2)}) collective-permute-start(bf16[32,16384]{1,0:T(8,128)(2,1)S(1)} %collective-permute-done.8.refs_0_), channel_id=1, source_target_pairs={{0,4},{1,3},{4,8},{5,1},{8,12},{9,5},{12,14},{13,9},{14,10},{15,13... | collective-permute-start | bytes 3145736 | tf_op jit(solution)/shard_map/ppermute | solution.py:173
  51.7 0.0 collective-permute-done.7.refs_3_
  51.7 0.0 collective-permute-done.6.refs_1_
  51.8 0.0 copy-done.1
  51.8 7.2 %scores.5.refs_4_ = f32[512,512]{1,0:T(8,128)S(1)} custom-call(s32[16]{0:T(128)S(1)} %dynamic-slice_bitcast_fusion.owners_ref, bf16[512,16384]{1,0:T(8,128)(2,1)S(1)} %copy-done.1, bf16[32,16384]{1,0:T(8,128)(2,1)S(1)} %collective-permute-done.3.refs_0_, bf16[32,16384]{1,0:T(8,128)(2,1)S(1)} %collective-permute-done.6.refs_1_, ...), custom_call_target="tpu_custom_call", output_to_operand_aliasing={{}: (6, {})} | custom-call | flops 1 | bytes 1 | tf_op jit(solution)/shard_map/scores/pallas_call | solution.py:141
  58.9 2.0 %collective-permute-done.5.refs_2_ = bf16[32,16384]{1,0:T(8,128)(2,1)S(1)} collective-permute-done((bf16[32,16384]{1,0:T(8,128)(2,1)}, bf16[32,16384]{1,0:T(8,128)(2,1)S(1)}, u32[]{:S(2)}, u32[]{:S(2)}) %collective-permute-start.5) | collective-permute-done | bytes 1048608 | tf_op jit(solution)/shard_map/ppermute | solution.py:173
  60.9 0.0 collective-permute-start.13
  60.9 0.5 collective-permute-start.12
  61.4 2.1 %collective-permute-start.11 = (bf16[32,16384]{1,0:T(8,128)(2,1)S(1)}, bf16[32,16384]{1,0:T(8,128)(2,1)S(1)}, u32[]{:S(2)}, u32[]{:S(2)}) collective-permute-start(bf16[32,16384]{1,0:T(8,128)(2,1)S(1)} %collective-permute-done.5.refs_2_), channel_id=1, source_target_pairs={{0,4},{1,3},{4,8},{5,1},{8,12},{9,5},{12,14},{13,9},{14,10},{15,13... | collective-permute-start | bytes 3145736 | tf_op jit(solution)/shard_map/ppermute | solution.py:173
  63.5 8.6 %collective-permute-done.9.refs_0_ = bf16[32,16384]{1,0:T(8,128)(2,1)S(1)} collective-permute-done((bf16[32,16384]{1,0:T(8,128)(2,1)S(1)}, bf16[32,16384]{1,0:T(8,128)(2,1)S(1)}, u32[]{:S(2)}, u32[]{:S(2)}) %collective-permute-start.9) | collective-permute-done | bytes 1048608 | tf_op jit(solution)/shard_map/ppermute | solution.py:173
  72.1 0.0 collective-permute-done.13.refs_3_
  72.1 0.0 collective-permute-done.12.refs_1_
  72.1 6.4 %scores.6.refs_4_ = f32[512,512]{1,0:T(8,128)S(1)} custom-call(s32[16]{0:T(128)S(1)} %dynamic-slice_bitcast_fusion.owners_ref, bf16[512,16384]{1,0:T(8,128)(2,1)S(1)} %copy-done.1, bf16[32,16384]{1,0:T(8,128)(2,1)S(1)} %collective-permute-done.8.refs_0_, bf16[32,16384]{1,0:T(8,128)(2,1)S(1)} %collective-permute-done.12.refs_1_, ...), custom_call_target="tpu_custom_call", output_to_operand_aliasing={{}: (6, {})} | custom-call | flops 1 | bytes 1 | tf_op jit(solution)/shard_map/scores/pallas_call | solution.py:141
  78.5 4.8 %collective-permute-done.11.refs_2_ = bf16[32,16384]{1,0:T(8,128)(2,1)S(1)} collective-permute-done((bf16[32,16384]{1,0:T(8,128)(2,1)S(1)}, bf16[32,16384]{1,0:T(8,128)(2,1)S(1)}, u32[]{:S(2)}, u32[]{:S(2)}) %collective-permute-start.11) | collective-permute-done | bytes 1048608 | tf_op jit(solution)/shard_map/ppermute | solution.py:173
  83.4 0.0 collective-permute-start.14
  83.4 0.5 collective-permute-start.10
  83.9 2.1 %collective-permute-done.14.refs_3_ = bf16[32,16384]{1,0:T(8,128)(2,1)S(1)} collective-permute-done((bf16[32,16384]{1,0:T(8,128)(2,1)S(1)}, bf16[32,16384]{1,0:T(8,128)(2,1)S(1)}, u32[]{:S(2)}, u32[]{:S(2)}) %collective-permute-start.14) | collective-permute-done | bytes 1048608 | tf_op jit(solution)/shard_map/ppermute | solution.py:173
  86.0 1.5 %collective-permute-done.10.refs_1_ = bf16[32,16384]{1,0:T(8,128)(2,1)S(1)} collective-permute-done((bf16[32,16384]{1,0:T(8,128)(2,1)S(1)}, bf16[32,16384]{1,0:T(8,128)(2,1)S(1)}, u32[]{:S(2)}, u32[]{:S(2)}) %collective-permute-start.10) | collective-permute-done | bytes 1048608 | tf_op jit(solution)/shard_map/ppermute | solution.py:173
  87.5 7.4 %scores.7 = f32[512,512]{1,0:T(8,128)} custom-call(s32[16]{0:T(128)S(1)} %dynamic-slice_bitcast_fusion.owners_ref, bf16[512,16384]{1,0:T(8,128)(2,1)S(1)} %copy-done.1, bf16[32,16384]{1,0:T(8,128)(2,1)S(1)} %collective-permute-done.9.refs_0_, bf16[32,16384]{1,0:T(8,128)(2,1)S(1)} %collective-permute-done.10.refs_1_, ...), custom_call_target="tpu_custom_call" | custom-call | flops 1 | bytes 1 | tf_op jit(solution)/shard_map/scores/pallas_call | solution.py:141
Async XLA Ops:
  0.0 3.0 %collective-permute-start.2 = (bf16[32,16384]{1,0:T(8,128)(2,1)}, bf16[32,16384]{1,0:T(8,128)(2,1)S(1)}, u32[]{:S(2)}, u32[]{:S(2)}) collective-permute-start(bf16[32,16384]{1,0:T(8,128)(2,1)} %refs_0_), channel_id=1, source_target_pairs={{0,1},{1,0},{2,3},{3,2},{4,5},{5,4},{6,7},{7,6},{8,9},{9,8},{10,11... | collective-permute-start | bytes 3145736 | tf_op jit(solution)/shard_map/ppermute | solution.py:173
  0.5 15.5 %collective-permute-start = (bf16[32,16384]{1,0:T(8,128)(2,1)}, bf16[32,16384]{1,0:T(8,128)(2,1)S(1)}, u32[]{:S(2)}, u32[]{:S(2)}) collective-permute-start(bf16[32,16384]{1,0:T(8,128)(2,1)} %refs_0_), channel_id=1, source_target_pairs={{0,4},{1,3},{4,8},{5,1},{8,12},{9,5},{12,14},{13,9},{14,10},{15,13... | collective-permute-start | bytes 3145736 | tf_op jit(solution)/shard_map/ppermute | solution.py:173
  6.6 20.6 %collective-permute-start.3 = (bf16[32,16384]{1,0:T(8,128)(2,1)S(1)}, bf16[32,16384]{1,0:T(8,128)(2,1)S(1)}, u32[]{:S(2)}, u32[]{:S(2)}) collective-permute-start(bf16[32,16384]{1,0:T(8,128)(2,1)S(1)} %precondition.4.refs_1_), channel_id=1, source_target_pairs={{0,4},{1,3},{4,8},{5,1},{8,12},{9,5},{12,14},{13,9},{14,10},{15,13... | collective-permute-start | bytes 3145736 | tf_op jit(solution)/shard_map/ppermute | solution.py:173
  19.5 9.8 %collective-permute-start.4 = (bf16[32,16384]{1,0:T(8,128)(2,1)S(1)}, bf16[32,16384]{1,0:T(8,128)(2,1)}, u32[]{:S(2)}, u32[]{:S(2)}) collective-permute-start(bf16[32,16384]{1,0:T(8,128)(2,1)S(1)} %precondition.3.refs_2_), channel_id=1, source_target_pairs={{0,1},{1,0},{2,3},{3,2},{4,5},{5,4},{6,7},{7,6},{8,9},{9,8},{10,11... | collective-permute-start | bytes 3145736 | tf_op jit(solution)/shard_map/ppermute | solution.py:173
  19.6 23.4 %collective-permute-start.1 = (bf16[32,16384]{1,0:T(8,128)(2,1)S(1)}, bf16[32,16384]{1,0:T(8,128)(2,1)}, u32[]{:S(2)}, u32[]{:S(2)}) collective-permute-start(bf16[32,16384]{1,0:T(8,128)(2,1)S(1)} %precondition.3.refs_2_), channel_id=1, source_target_pairs={{0,4},{1,3},{4,8},{5,1},{8,12},{9,5},{12,14},{13,9},{14,10},{15,13... | collective-permute-start | bytes 3145736 | tf_op jit(solution)/shard_map/ppermute | solution.py:173
  22.4 1.2 %copy-start.2 = (bf16[32,16384]{1,0:T(8,128)(2,1)S(1)}, bf16[32,16384]{1,0:T(8,128)(2,1)}, u32[]{:S(2)}) copy-start(bf16[32,16384]{1,0:T(8,128)(2,1)} %refs_0_) | copy-start | bytes 3145732
  27.2 22.5 %collective-permute-start.8 = (bf16[32,16384]{1,0:T(8,128)(2,1)S(1)}, bf16[32,16384]{1,0:T(8,128)(2,1)S(1)}, u32[]{:S(2)}, u32[]{:S(2)}) collective-permute-start(bf16[32,16384]{1,0:T(8,128)(2,1)S(1)} %collective-permute-done.3.refs_0_), channel_id=1, source_target_pairs={{0,4},{1,3},{4,8},{5,1},{8,12},{9,5},{12,14},{13,9},{14,10},{15,13... | collective-permute-start | bytes 3145736 | tf_op jit(solution)/shard_map/ppermute | solution.py:173
  29.3 5.8 %copy-start = (bf16[512,16384]{1,0:T(8,128)(2,1)S(1)}, bf16[512,16384]{1,0:T(8,128)(2,1)}, u32[]{:S(2)}) copy-start(bf16[512,16384]{1,0:T(8,128)(2,1)} %query_ref.7) | copy-start | bytes 50331652
  35.0 16.7 %copy-start.1 = (bf16[512,16384]{1,0:T(8,128)(2,1)S(1)}, bf16[512,16384]{1,0:T(8,128)(2,1)}, u32[]{:S(2)}) copy-start(bf16[512,16384]{1,0:T(8,128)(2,1)} %query_ref.7) | copy-start | bytes 50331652
  42.9 8.8 %collective-permute-start.7 = (bf16[32,16384]{1,0:T(8,128)(2,1)}, bf16[32,16384]{1,0:T(8,128)(2,1)S(1)}, u32[]{:S(2)}, u32[]{:S(2)}) collective-permute-start(bf16[32,16384]{1,0:T(8,128)(2,1)} %collective-permute-done.1.refs_2_), channel_id=1, source_target_pairs={{0,1},{1,0},{2,3},{3,2},{4,5},{5,4},{6,7},{7,6},{8,9},{9,8},{10,11... | collective-permute-start | bytes 3145736 | tf_op jit(solution)/shard_map/ppermute | solution.py:173
  43.0 8.7 %collective-permute-start.6 = (bf16[32,16384]{1,0:T(8,128)(2,1)S(1)}, bf16[32,16384]{1,0:T(8,128)(2,1)S(1)}, u32[]{:S(2)}, u32[]{:S(2)}) collective-permute-start(bf16[32,16384]{1,0:T(8,128)(2,1)S(1)} %collective-permute-done.3.refs_0_), channel_id=1, source_target_pairs={{0,1},{1,0},{2,3},{3,2},{4,5},{5,4},{6,7},{7,6},{8,9},{9,8},{10,11... | collective-permute-start | bytes 3145736 | tf_op jit(solution)/shard_map/ppermute | solution.py:173
  43.5 17.4 %collective-permute-start.5 = (bf16[32,16384]{1,0:T(8,128)(2,1)}, bf16[32,16384]{1,0:T(8,128)(2,1)S(1)}, u32[]{:S(2)}, u32[]{:S(2)}) collective-permute-start(bf16[32,16384]{1,0:T(8,128)(2,1)} %collective-permute-done.1.refs_2_), channel_id=1, source_target_pairs={{0,4},{1,3},{4,8},{5,1},{8,12},{9,5},{12,14},{13,9},{14,10},{15,13... | collective-permute-start | bytes 3145736 | tf_op jit(solution)/shard_map/ppermute | solution.py:173
  49.7 22.5 %collective-permute-start.9 = (bf16[32,16384]{1,0:T(8,128)(2,1)S(1)}, bf16[32,16384]{1,0:T(8,128)(2,1)S(1)}, u32[]{:S(2)}, u32[]{:S(2)}) collective-permute-start(bf16[32,16384]{1,0:T(8,128)(2,1)S(1)} %collective-permute-done.8.refs_0_), channel_id=1, source_target_pairs={{0,4},{1,3},{4,8},{5,1},{8,12},{9,5},{12,14},{13,9},{14,10},{15,13... | collective-permute-start | bytes 3145736 | tf_op jit(solution)/shard_map/ppermute | solution.py:173
  60.9 11.2 %collective-permute-start.13 = (bf16[32,16384]{1,0:T(8,128)(2,1)S(1)}, bf16[32,16384]{1,0:T(8,128)(2,1)S(1)}, u32[]{:S(2)}, u32[]{:S(2)}) collective-permute-start(bf16[32,16384]{1,0:T(8,128)(2,1)S(1)} %collective-permute-done.5.refs_2_), channel_id=1, source_target_pairs={{0,1},{1,0},{2,3},{3,2},{4,5},{5,4},{6,7},{7,6},{8,9},{9,8},{10,11... | collective-permute-start | bytes 3145736 | tf_op jit(solution)/shard_map/ppermute | solution.py:173
  60.9 11.2 %collective-permute-start.12 = (bf16[32,16384]{1,0:T(8,128)(2,1)S(1)}, bf16[32,16384]{1,0:T(8,128)(2,1)S(1)}, u32[]{:S(2)}, u32[]{:S(2)}) collective-permute-start(bf16[32,16384]{1,0:T(8,128)(2,1)S(1)} %collective-permute-done.8.refs_0_), channel_id=1, source_target_pairs={{0,1},{1,0},{2,3},{3,2},{4,5},{5,4},{6,7},{7,6},{8,9},{9,8},{10,11... | collective-permute-start | bytes 3145736 | tf_op jit(solution)/shard_map/ppermute | solution.py:173
  61.4 22.0 %collective-permute-start.11 = (bf16[32,16384]{1,0:T(8,128)(2,1)S(1)}, bf16[32,16384]{1,0:T(8,128)(2,1)S(1)}, u32[]{:S(2)}, u32[]{:S(2)}) collective-permute-start(bf16[32,16384]{1,0:T(8,128)(2,1)S(1)} %collective-permute-done.5.refs_2_), channel_id=1, source_target_pairs={{0,4},{1,3},{4,8},{5,1},{8,12},{9,5},{12,14},{13,9},{14,10},{15,13... | collective-permute-start | bytes 3145736 | tf_op jit(solution)/shard_map/ppermute | solution.py:173
  83.4 2.7 %collective-permute-start.14 = (bf16[32,16384]{1,0:T(8,128)(2,1)S(1)}, bf16[32,16384]{1,0:T(8,128)(2,1)S(1)}, u32[]{:S(2)}, u32[]{:S(2)}) collective-permute-start(bf16[32,16384]{1,0:T(8,128)(2,1)S(1)} %collective-permute-done.11.refs_2_), channel_id=1, source_target_pairs={{0,1},{1,0},{2,3},{3,2},{4,5},{5,4},{6,7},{7,6},{8,9},{9,8},{10,11... | collective-permute-start | bytes 3145736 | tf_op jit(solution)/shard_map/ppermute | solution.py:173
  83.4 4.2 %collective-permute-start.10 = (bf16[32,16384]{1,0:T(8,128)(2,1)S(1)}, bf16[32,16384]{1,0:T(8,128)(2,1)S(1)}, u32[]{:S(2)}, u32[]{:S(2)}) collective-permute-start(bf16[32,16384]{1,0:T(8,128)(2,1)S(1)} %collective-permute-done.9.refs_0_), channel_id=1, source_target_pairs={{0,1},{1,0},{2,3},{3,2},{4,5},{5,4},{6,7},{7,6},{8,9},{9,8},{10,11... | collective-permute-start | bytes 3145736 | tf_op jit(solution)/shard_map/ppermute | solution.py:173

commit v3 on v2

--- a/solution.py
+++ b/solution.py
@@ -11,10 +11,12 @@
 A_DIM = 128
 B_DIM = 128
 LANES = 128
-K_TILE = 4096
+K_TILE = 4608
 KERNEL_VMEM = 16 << 20
 PREPARE_COST = pl.CostEstimate(flops=1, bytes_accessed=1, transcendentals=0)
 SCORE_COST = pl.CostEstimate(flops=1, bytes_accessed=1, transcendentals=0)
+CUT_COST = pl.CostEstimate(flops=1, bytes_accessed=1, transcendentals=0)
+LAST_PARTS = 7, 9
 ANY_SPEC = pl.BlockSpec(memory_space=pl.ANY)
 VMEM_SPEC = pl.BlockSpec(memory_space=pltpu.VMEM)
 
@@ -82,79 +84,85 @@
     )(*operands)
 
 
-def scores_kernel(entries, first, last, owners_ref, query_ref, *refs):
-    blocks, refs = refs[:len(entries)], refs[len(entries):]
+def scores_kernel(entries, count, begin, first, last, owners_ref, query_ref, *refs):
+    blocks, refs = refs[:count], refs[count:]
     if not first:
         total_ref, refs = refs[0], refs[1:]
-    out_ref, weight_ref, sum_ref, sems = refs
-    height, width = blocks[0].shape
-    steps = width // K_TILE
-
-    def fetches(step):
-        return [
-            pltpu.make_async_copy(
-                block.at[:, pl.ds(pl.multiple_of(step * K_TILE, K_TILE), K_TILE)],
-                weight_ref.at[lax.rem(step, 2), pl.ds(i * height, height), :],
-                sems.at[lax.rem(step, 2), i],
-            )
-            for i, block in enumerate(blocks)
-        ]
-
-    for fetch in fetches(0):
-        fetch.start()
+    out_ref, sum_ref = refs
+    height = blocks[0].shape[0]
+    width = min(block.shape[1] for block in blocks)
+    tile = column_tile(width)
+    missing = sum_ref.shape[1] - sum(block.shape[0] for block in blocks)
     if first:
         out_ref[...] = jnp.zeros_like(out_ref)
     if last:
         out_ref[...] = total_ref[...]
     sum_ref[...] = jnp.zeros_like(sum_ref)
 
-    @pl.loop(0, steps)
+    @pl.loop(0, width // tile)
     def _(step):
-        @pl.when(step + 1 < steps)
-        def _():
-            for fetch in fetches(step + 1):
-                fetch.start()
-
-        for fetch in fetches(step):
-            fetch.wait()
+        def columns(skipped):
+            return pl.ds(pl.multiple_of(skipped + step * tile, LANES), tile)
+
+        rows = [block[:, columns(begin if block.shape[1] > width else 0)] for block in blocks]
+        if missing:
+            rows.append(jnp.zeros((missing, tile), rows[0].dtype))
         sum_ref[...] += lax.dot_general(
-            query_ref[:, pl.ds(pl.multiple_of(step * K_TILE, K_TILE), K_TILE)],
-            weight_ref[lax.rem(step, 2)],
-            (((1,), (1,)), ((), ())),
+            query_ref[:, columns(begin)], jnp.concatenate(rows, axis=0), (((1,), (1,)), ((), ())),
             preferred_element_type=jnp.float32,
         )
 
-    place = lax.broadcasted_iota(jnp.int32, sum_ref.shape, 1) // height
     per_tile = LANES // height
+    place = lax.broadcasted_iota(jnp.int32, (sum_ref.shape[0], LANES), 1) // height
     for i, entry in enumerate(entries):
         owner = owners_ref[entry]
         spot = lax.rem(owner, per_tile)
-        moved = pltpu.roll(sum_ref[...], lax.rem(spot - i + per_tile, per_tile) * height, 1)
+        held = sum_ref[:, i // per_tile * LANES:(i // per_tile + 1) * LANES]
+        moved = pltpu.roll(held, lax.rem(spot - i % per_tile + per_tile, per_tile) * height, 1)
         lanes = pl.ds(pl.multiple_of(lax.div(owner, per_tile) * LANES, LANES), LANES)
         out_ref[:, lanes] += jnp.where(place == spot, moved, 0.0)
 
 
-def add_scores(total, queries, owners, entries, blocks, train_count, last):
+def column_tile(width):
+    return max(t for t in range(LANES, min(K_TILE, width) + 1, LANES) if width % t == 0)
+
+
+def add_scores(total, queries, owners, entries, blocks, train_count, begin=0, last=False):
     rows = queries.shape[0]
     first = total is None
     operands = [pltpu.with_memory_space_constraint(queries, pltpu.VMEM), *blocks] + ([] if first else [total])
+    lanes = -(-len(entries) * blocks[0].shape[0] // LANES) * LANES
     return pl.pallas_call(
-        functools.partial(scores_kernel, entries, first, last),
+        functools.partial(scores_kernel, entries, len(blocks), begin, first, last),
         out_shape=jax.ShapeDtypeStruct((rows, train_count), jnp.float32),
-        in_specs=[pl.BlockSpec(memory_space=pltpu.SMEM), VMEM_SPEC]
-        + [ANY_SPEC] * len(blocks)
-        + ([] if first else [VMEM_SPEC]),
+        in_specs=[pl.BlockSpec(memory_space=pltpu.SMEM)] + [VMEM_SPEC] * len(operands),
         out_specs=VMEM_SPEC,
-        scratch_shapes=[
-            pltpu.VMEM((2, LANES, K_TILE), jnp.bfloat16),
-            pltpu.VMEM((rows, LANES), jnp.float32),
-            pltpu.SemaphoreType.DMA((2, len(blocks))),
-        ],
+        scratch_shapes=[pltpu.VMEM((rows, lanes), jnp.float32)],
         input_output_aliases={} if first or last else {len(operands): 0},
         compiler_params=pltpu.CompilerParams(vmem_limit_bytes=KERNEL_VMEM),
         cost_estimate=SCORE_COST,
         name="scores",
     )(owners, *operands)
+
+
+def cut_kernel(source_ref, *pieces):
+    row, column = 0, 0
+    for piece in pieces:
+        height, width = piece.shape
+        piece[...] = source_ref[row:row + height, column:column + width]
+        row, column = (row + height) % source_ref.shape[0], (column + width) % source_ref.shape[1]
+
+
+def cut(block, shapes):
+    return pl.pallas_call(
+        cut_kernel,
+        out_shape=[jax.ShapeDtypeStruct(shape, block.dtype) for shape in shapes],
+        in_specs=[VMEM_SPEC],
+        out_specs=[VMEM_SPEC] * len(shapes),
+        compiler_params=pltpu.CompilerParams(vmem_limit_bytes=KERNEL_VMEM),
+        cost_estimate=CUT_COST,
+        name="cut",
+    )(block)
 
 
 def per_device(queries, train_rows, left_basis, right_basis, eigenvalues):
@@ -163,6 +171,7 @@
     ring = chip_ring(chips)
     hops = chips // 2
     train_count = devices * train_rows.shape[0]
+    height, width = train_rows.shape
 
     along = [
         (2 * ring[i] + core, 2 * ring[(i + (-1 if core else 1)) % chips] + core)
@@ -196,26 +205,46 @@
     own = precondition(train_rows, *factors)
     chains = [raw, other]
     blocks = [own, other]
-    total, done = None, 0
-    for arrival in range(1, chips):
+    score = lambda total, arrivals, blocks, **kw: add_scores(
+        total, queries, owners, [e for a in arrivals for e in (2 * a, 2 * a + 1)], blocks, train_count, **kw
+    )
+    pairs = [[own, other]]
+    groups = [[a, a + 1] for a in range(0, chips - 6, 2)] + [[chips - 6, chips - 5, chips - 4]]
+    total = None
+    for arrival in range(1, chips - 1):
         chain = (arrival + 1) % 2
         block = send(chains[chain], along)
-        if arrival > 2 and chain == 0:
-            entries = list(range(done, done + 4))
-            total = add_scores(total, queries, owners, entries, [blocks[e] for e in entries], train_count, False)
-            done += 4
+        if groups[0][-1] == arrival - 2:
+            total = score(total, groups[0], [block for a in groups[0] for block in pairs[a]])
+            groups.pop(0)
             block, total = after(block, total)
         if arrival == 1:
             block = precondition(block, *factors)
-        if arrival > 1 and chain == 1:
+        if groups and groups[0][-1] == arrival - 1:
             if total is None:
-                own, block = after(own, block)
-                blocks[0] = own
+                pairs[0][0], block = after(pairs[0][0], block)
             else:
                 total, block = after(total, block)
         chains[chain] = block
-        blocks += [block, send(block, across)]
-    return add_scores(total, queries, owners, list(range(done, devices)), blocks[done:], train_count, True)
+        halves = cut(block, [(height // 2, width)] * 2) if arrival == chips - 2 else [block]
+        pairs.append([block] + [send(half, across) for half in halves])
+
+    group = [chips - 3, chips - 2, chips - 1]
+    widths = [width * part // sum(LAST_PARTS) for part in LAST_PARTS]
+    begin = 0
+    for i, piece in enumerate(cut(chains[0], [(height, w) for w in widths])):
+        if i == 1:
+            piece, block = after(piece, block)
+            pairs[-2 if len(pairs) == chips else -1][0] = block
+        last = i == len(widths) - 1
+        part = send(piece, along)
+        if i:
+            total = score(total, group, blocks, begin=begin)
+            begin += widths[i - 1]
+            part, total = after(part, total)
+        swapped = [part] if last else cut(part, [(height // 2, widths[i])] * 2)
+        blocks = pairs[chips - 3] + pairs[chips - 2] + [part] + [send(piece, across) for piece in swapped]
+    return score(total, group, blocks, begin=begin, last=True)
 
 
 def solution(mesh):

time: 95.5 us -> 90.8 us (0.951)
  Pallas kernels: 39.4 us -> 33.3 us
  starting transfers between devices: 17.5 us -> 19.6 us
    pallas_call x4 -> x7, Pallas kernels: 28.9 us -> 22.7 us  [the longest x4 22.6 us: add_scores(): pl.pallas_call(functools.partial(scores_kernel, entries, len(blocks), beg...]
    ppermute x15 -> x19, starting transfers between devices: 17.5 us -> 19.6 us  [per_device(): send = lambda block, pairs: lax.ppermute(block, 'wide', pairs)]
    ppermute x15 -> x19, waiting for transfers between devices: 30.2 us -> 29.7 us  [per_device(): send = lambda block, pairs: lax.ppermute(block, 'wide', pairs)]
  transfers between devices with their start and end apart: 15 -> 19, of which waited for: 8 -> 9; matrix products, arithmetic and copies ran while one was open for 1% -> 1% of each run, Pallas kernels for 34% -> 31%
where the time goes in v3:
time: 90.8 us; the launch traced here: 90.4 us
  Pallas kernels  33.3 us (37%)
  waiting for transfers between devices  29.7 us (33%)
  starting transfers between devices  19.6 us (22%)
  local copies, waits for them, and re-layouts  7.69 us (8%)
    ppermute x19, waiting for transfers between devices, per_device(): send = lambda block, pairs: lax.ppermute(block, 'wide', pairs)  29.7 us
    pallas_call x4, Pallas kernels, add_scores(): pl.pallas_call(functools.partial(scores_kernel, entries, len(blocks), beg...  22.6 us
    ppermute x19, starting transfers between devices, per_device(): send = lambda block, pairs: lax.ppermute(block, 'wide', pairs)  19.6 us
    pallas_call x3, Pallas kernels, precondition(): pl.pallas_call(precondition_kernel, out_shape=jax.ShapeDtypeStruct(rows.s...  10.6 us
    unnamed x6, local copies, waits for them, and re-layouts  7 us
  transfers between devices with their start and end apart: 19, of which 9 were waited for; matrix products, arithmetic and copies ran while one was open for 1% of the time, Pallas kernels for 31%

profile of v3, /device:TPU:0, one launch (start us, length us, event | category | flops | bytes accessed | tf_op | source)
XLA Modules:
  0.0 90.4 jit_solution(8562980815525521679)
XLA Ops:
  0.0 0.5 collective-permute-start.2
  0.5 2.6 %collective-permute-start = (bf16[32,16384]{1,0:T(8,128)(2,1)}, bf16[32,16384]{1,0:T(8,128)(2,1)S(1)}, u32[]{:S(2)}, u32[]{:S(2)}) collective-permute-start(bf16[32,16384]{1,0:T(8,128)(2,1)} %refs_0_), channel_id=1, source_target_pairs={{0,4},{1,3},{4,8},{5,1},{8,12},{9,5},{12,14},{13,9},{14,10},{15,13... | collective-permute-start | bytes 3145736 | tf_op jit(solution)/shard_map/ppermute | solution.py:182
  3.0 0.0 collective-permute-done.2.refs_0_
  3.0 3.5 %precondition.4.refs_1_ = bf16[32,16384]{1,0:T(8,128)(2,1)S(1)} custom-call(bf16[32,16384]{1,0:T(8,128)(2,1)S(1)} %collective-permute-done.2.refs_0_, bf16[128,128]{1,0:T(8,128)(2,1)} %refs_1_.5, bf16[128,128]{1,0:T(8,128)(2,1)} %refs_2_.5, f32[128,128]{1,0:T(8,128)} %refs_3_.5), custom_call_target="tpu_custom_call" | custom-call | flops 1 | bytes 1 | tf_op jit(solution)/shard_map/precondition/pallas_call | solution.py:73
  6.6 2.9 %collective-permute-start.3 = (bf16[32,16384]{1,0:T(8,128)(2,1)S(1)}, bf16[32,16384]{1,0:T(8,128)(2,1)}, u32[]{:S(2)}, u32[]{:S(2)}) collective-permute-start(bf16[32,16384]{1,0:T(8,128)(2,1)S(1)} %precondition.4.refs_1_), channel_id=1, source_target_pairs={{0,4},{1,3},{4,8},{5,1},{8,12},{9,5},{12,14},{13,9},{14,10},{15,13... | collective-permute-start | bytes 3145736 | tf_op jit(solution)/shard_map/ppermute | solution.py:182
  9.5 6.5 %collective-permute-done.refs_0_ = bf16[32,16384]{1,0:T(8,128)(2,1)S(1)} collective-permute-done((bf16[32,16384]{1,0:T(8,128)(2,1)}, bf16[32,16384]{1,0:T(8,128)(2,1)S(1)}, u32[]{:S(2)}, u32[]{:S(2)}) %collective-permute-start) | collective-permute-done | bytes 1048608 | tf_op jit(solution)/shard_map/ppermute | solution.py:182
  16.0 3.5 %precondition.3.refs_2_ = bf16[32,16384]{1,0:T(8,128)(2,1)S(1)} custom-call(bf16[32,16384]{1,0:T(8,128)(2,1)S(1)} %collective-permute-done.refs_0_, bf16[128,128]{1,0:T(8,128)(2,1)} %refs_1_.5, bf16[128,128]{1,0:T(8,128)(2,1)} %refs_2_.5, f32[128,128]{1,0:T(8,128)} %refs_3_.5), custom_call_target="tpu_custom_call" | custom-call | flops 1 | bytes 1 | tf_op jit(solution)/shard_map/precondition/pallas_call | solution.py:73
  19.5 0.1 collective-permute-start.4
  19.6 2.1 %collective-permute-start.1 = (bf16[32,16384]{1,0:T(8,128)(2,1)S(1)}, bf16[32,16384]{1,0:T(8,128)(2,1)}, u32[]{:S(2)}, u32[]{:S(2)}) collective-permute-start(bf16[32,16384]{1,0:T(8,128)(2,1)S(1)} %precondition.3.refs_2_), channel_id=1, source_target_pairs={{0,4},{1,3},{4,8},{5,1},{8,12},{9,5},{12,14},{13,9},{14,10},{15,13... | collective-permute-start | bytes 3145736 | tf_op jit(solution)/shard_map/ppermute | solution.py:182
  21.7 0.0 copy-start.2
  21.7 1.2 %copy-done.2 = bf16[32,16384]{1,0:T(8,128)(2,1)S(1)} copy-done((bf16[32,16384]{1,0:T(8,128)(2,1)S(1)}, bf16[32,16384]{1,0:T(8,128)(2,1)}, u32[]{:S(2)}) %copy-start.2) | copy-done | bytes 1048600
  22.9 3.5 %precondition.5.refs_0_ = bf16[32,16384]{1,0:T(8,128)(2,1)S(1)} custom-call(bf16[32,16384]{1,0:T(8,128)(2,1)S(1)} %copy-done.2, bf16[128,128]{1,0:T(8,128)(2,1)} %refs_1_.5, bf16[128,128]{1,0:T(8,128)(2,1)} %refs_2_.5, f32[128,128]{1,0:T(8,128)} %refs_3_.5), custom_call_target="tpu_custom_call" | custom-call | flops 1 | bytes 1 | tf_op jit(solution)/shard_map/precondition/pallas_call | solution.py:73
  26.4 0.9 collective-permute-done.3.refs_0_
  27.3 2.1 %collective-permute-start.7 = (bf16[32,16384]{1,0:T(8,128)(2,1)}, bf16[32,16384]{1,0:T(8,128)(2,1)}, u32[]{:S(2)}, u32[]{:S(2)}) collective-permute-start(bf16[32,16384]{1,0:T(8,128)(2,1)} %collective-permute-done.3.refs_0_), channel_id=1, source_target_pairs={{0,4},{1,3},{4,8},{5,1},{8,12},{9,5},{12,14},{13,9},{14,10},{15,13... | collective-permute-start | bytes 3145736 | tf_op jit(solution)/shard_map/ppermute | solution.py:182
  29.4 0.7 dynamic-slice_bitcast_fusion.owners_ref
  30.1 0.0 collective-permute-done.4.refs_3_
  30.1 0.0 copy-start
  30.1 5.8 %copy-done = bf16[512,16384]{1,0:T(8,128)(2,1)S(1)} copy-done((bf16[512,16384]{1,0:T(8,128)(2,1)S(1)}, bf16[512,16384]{1,0:T(8,128)(2,1)}, u32[]{:S(2)}) %copy-start) | copy-done | bytes 16777240
  35.8 0.0 copy-start.1
  35.8 6.9 %scores.4.refs_6_ = f32[512,512]{1,0:T(8,128)S(1)} custom-call(s32[16]{0:T(128)S(1)} %dynamic-slice_bitcast_fusion.owners_ref, bf16[512,16384]{1,0:T(8,128)(2,1)S(1)} %copy-done, bf16[32,16384]{1,0:T(8,128)(2,1)S(1)} %precondition.5.refs_0_, bf16[32,16384]{1,0:T(8,128)(2,1)S(1)} %precondition.4.refs_1_, bf16[32,16384]{1,0:T(8,128)(2,1)S(1)} %precondition.3.refs_2_, ...), custom_call_target="tpu_custom_call" | custom-call | flops 1 | bytes 1 | tf_op jit(solution)/shard_map/scores/pallas_call | solution.py:135
  42.7 0.0 collective-permute-done.1.refs_2_
  42.7 1.6 %collective-permute-start.5 = (bf16[32,16384]{1,0:T(8,128)(2,1)}, bf16[32,16384]{1,0:T(8,128)(2,1)S(1)}, u32[]{:S(2)}, u32[]{:S(2)}) collective-permute-start(bf16[32,16384]{1,0:T(8,128)(2,1)} %collective-permute-done.1.refs_2_), channel_id=1, source_target_pairs={{0,4},{1,3},{4,8},{5,1},{8,12},{9,5},{12,14},{13,9},{14,10},{15,13... | collective-permute-start | bytes 3145736 | tf_op jit(solution)/shard_map/ppermute | solution.py:182
  44.4 0.0 collective-permute-start.10
  44.4 0.5 collective-permute-start.9
  44.9 4.9 %collective-permute-done.7.refs_4_ = bf16[32,16384]{1,0:T(8,128)(2,1)} collective-permute-done((bf16[32,16384]{1,0:T(8,128)(2,1)}, bf16[32,16384]{1,0:T(8,128)(2,1)}, u32[]{:S(2)}, u32[]{:S(2)}) %collective-permute-start.7) | collective-permute-done | bytes 1048608 | tf_op jit(solution)/shard_map/ppermute | solution.py:182
  49.8 0.0 collective-permute-start.11
  49.8 2.1 %collective-permute-start.8 = (bf16[32,16384]{1,0:T(8,128)(2,1)}, bf16[32,16384]{1,0:T(8,128)(2,1)S(1)}, u32[]{:S(2)}, u32[]{:S(2)}) collective-permute-start(bf16[32,16384]{1,0:T(8,128)(2,1)} %collective-permute-done.7.refs_4_), channel_id=1, source_target_pairs={{0,4},{1,3},{4,8},{5,1},{8,12},{9,5},{12,14},{13,9},{14,10},{15,13... | collective-permute-start | bytes 3145736 | tf_op jit(solution)/shard_map/ppermute | solution.py:182
  51.9 9.0 %collective-permute-done.5.source_ref.refs_0_ = bf16[32,16384]{1,0:T(8,128)(2,1)S(1)} collective-permute-done((bf16[32,16384]{1,0:T(8,128)(2,1)}, bf16[32,16384]{1,0:T(8,128)(2,1)S(1)}, u32[]{:S(2)}, u32[]{:S(2)}) %collective-permute-start.5) | collective-permute-done | bytes 1048608 | tf_op jit(solution)/shard_map/ppermute | solution.py:182
  60.9 0.0 collective-permute-start.6
  60.9 0.1 cut.3
  61.0 0.0 collective-permute-done.10.refs_3_
  61.0 2.1 %collective-permute-start.15 = (bf16[32,7168]{1,0:T(8,128)(2,1)S(1)}, bf16[32,7168]{1,0:T(8,128)(2,1)S(1)}, u32[]{:S(2)}, u32[]{:S(2)}) collective-permute-start(bf16[32,7168]{1,0:T(8,128)(2,1)S(1)} %get-tuple-element.39), channel_id=1, source_target_pairs={{0,4},{1,3},{4,8},{5,1},{8,12},{9,5},{12,14},{13,9},{14,10},{15,13... | collective-permute-start | bytes 1376264 | tf_op jit(solution)/shard_map/ppermute | solution.py:182
  63.1 0.0 collective-permute-done.9.refs_1_
  63.1 0.0 collective-permute-done.11.refs_5_
  63.1 0.0 copy-done.1
  63.1 7.5 %scores.5.refs_8_ = f32[512,512]{1,0:T(8,128)S(1)} custom-call(s32[16]{0:T(128)S(1)} %dynamic-slice_bitcast_fusion.owners_ref, bf16[512,16384]{1,0:T(8,128)(2,1)S(1)} %copy-done.1, bf16[32,16384]{1,0:T(8,128)(2,1)} %collective-permute-done.3.refs_0_, bf16[32,16384]{1,0:T(8,128)(2,1)S(1)} %collective-permute-done.9.refs_1_, ...), custom_call_target="tpu_custom_call", output_to_operand_aliasing={{}: (8, {})} | custom-call | flops 1 | bytes 1 | tf_op jit(solution)/shard_map/scores/pallas_call | solution.py:135
  70.6 1.5 %collective-permute-done.8.source_ref.refs_2_ = bf16[32,16384]{1,0:T(8,128)(2,1)S(1)} collective-permute-done((bf16[32,16384]{1,0:T(8,128)(2,1)}, bf16[32,16384]{1,0:T(8,128)(2,1)S(1)}, u32[]{:S(2)}, u32[]{:S(2)}) %collective-permute-start.8) | collective-permute-done | bytes 1048608 | tf_op jit(solution)/shard_map/ppermute | solution.py:182
  72.1 2.1 %collective-permute-start.14 = (bf16[32,9216]{1,0:T(8,128)(2,1)S(1)}, bf16[32,9216]{1,0:T(8,128)(2,1)S(1)}, u32[]{:S(2)}, u32[]{:S(2)}) collective-permute-start(bf16[32,9216]{1,0:T(8,128)(2,1)S(1)} %get-tuple-element.38), channel_id=1, source_target_pairs={{0,4},{1,3},{4,8},{5,1},{8,12},{9,5},{12,14},{13,9},{14,10},{15,13... | collective-permute-start | bytes 1769480 | tf_op jit(solution)/shard_map/ppermute | solution.py:182
  74.2 0.1 cut.4
  74.3 0.1 collective-permute-start.12
  74.4 0.5 collective-permute-start.13
  74.9 2.2 %collective-permute-done.15.source_ref.refs_5_ = bf16[32,7168]{1,0:T(8,128)(2,1)S(1)} collective-permute-done((bf16[32,7168]{1,0:T(8,128)(2,1)S(1)}, bf16[32,7168]{1,0:T(8,128)(2,1)S(1)}, u32[]{:S(2)}, u32[]{:S(2)}) %collective-permute-start.15) | collective-permute-done | bytes 458784 | tf_op jit(solution)/shard_map/ppermute | solution.py:182
  77.1 0.1 collective-permute-start.16
  77.2 1.5 %collective-permute-done.16.refs_6_ = bf16[16,7168]{1,0:T(8,128)(2,1)S(1)} collective-permute-done((bf16[16,7168]{1,0:T(8,128)(2,1)S(1)}, bf16[16,7168]{1,0:T(8,128)(2,1)S(1)}, u32[]{:S(2)}, u32[]{:S(2)}) %collective-permute-start.16) | collective-permute-done | bytes 229408 | tf_op jit(solution)/shard_map/ppermute | solution.py:182
  78.6 0.1 collective-permute-start.17
  78.8 1.4 %collective-permute-done.17.refs_7_ = bf16[16,7168]{1,0:T(8,128)(2,1)S(1)} collective-permute-done((bf16[16,7168]{1,0:T(8,128)(2,1)S(1)}, bf16[16,7168]{1,0:T(8,128)(2,1)S(1)}, u32[]{:S(2)}, u32[]{:S(2)}) %collective-permute-start.17) | collective-permute-done | bytes 229408 | tf_op jit(solution)/shard_map/ppermute | solution.py:182
  80.1 0.0 collective-permute-done.6.refs_1_
  80.1 0.0 collective-permute-done.12.refs_3_
  80.1 0.0 collective-permute-done.13.refs_4_
  80.1 3.3 %scores.6.refs_7_ = f32[512,512]{1,0:T(8,128)S(1)} custom-call(s32[16]{0:T(128)S(1)} %dynamic-slice_bitcast_fusion.owners_ref, bf16[512,16384]{1,0:T(8,128)(2,1)S(1)} %copy-done.1, bf16[32,16384]{1,0:T(8,128)(2,1)S(1)} %collective-permute-done.5.source_ref.refs_0_, ...), custom_call_target="tpu_custom_call", output_to_operand_aliasing={{}: (10, {})} | custom-call | flops 1 | bytes 1 | tf_op jit(solution)/shard_map/scores/pallas_call | solution.py:135
  83.5 0.0 collective-permute-done.14.refs_5_
  83.5 0.2 collective-permute-start.18
  83.7 1.9 %collective-permute-done.18.refs_6_ = bf16[32,9216]{1,0:T(8,128)(2,1)S(1)} collective-permute-done((bf16[32,9216]{1,0:T(8,128)(2,1)S(1)}, bf16[32,9216]{1,0:T(8,128)(2,1)S(1)}, u32[]{:S(2)}, u32[]{:S(2)}) %collective-permute-start.18) | collective-permute-done | bytes 589856 | tf_op jit(solution)/shard_map/ppermute | solution.py:182
  85.5 4.9 %scores.7 = f32[512,512]{1,0:T(8,128)} custom-call(s32[16]{0:T(128)S(1)} %dynamic-slice_bitcast_fusion.owners_ref, bf16[512,16384]{1,0:T(8,128)(2,1)S(1)} %copy-done.1, bf16[32,16384]{1,0:T(8,128)(2,1)S(1)} %collective-permute-done.5.source_ref.refs_0_, bf16[32,16384]{1,0:T(8,128)(2,1)S(1)} %collective-permute-done.6.refs_1_, ...), custom_call_target="tpu_custom_call" | custom-call | flops 1 | bytes 1 | tf_op jit(solution)/shard_map/scores/pallas_call | solution.py:135
  (1 shorter events, 0.0 us)
Async XLA Ops:
  0.0 3.0 %collective-permute-start.2 = (bf16[32,16384]{1,0:T(8,128)(2,1)}, bf16[32,16384]{1,0:T(8,128)(2,1)S(1)}, u32[]{:S(2)}, u32[]{:S(2)}) collective-permute-start(bf16[32,16384]{1,0:T(8,128)(2,1)} %refs_0_), channel_id=1, source_target_pairs={{0,1},{1,0},{2,3},{3,2},{4,5},{5,4},{6,7},{7,6},{8,9},{9,8},{10,11... | collective-permute-start | bytes 3145736 | tf_op jit(solution)/shard_map/ppermute | solution.py:182
  0.5 15.5 %collective-permute-start = (bf16[32,16384]{1,0:T(8,128)(2,1)}, bf16[32,16384]{1,0:T(8,128)(2,1)S(1)}, u32[]{:S(2)}, u32[]{:S(2)}) collective-permute-start(bf16[32,16384]{1,0:T(8,128)(2,1)} %refs_0_), channel_id=1, source_target_pairs={{0,4},{1,3},{4,8},{5,1},{8,12},{9,5},{12,14},{13,9},{14,10},{15,13... | collective-permute-start | bytes 3145736 | tf_op jit(solution)/shard_map/ppermute | solution.py:182
  6.6 20.7 %collective-permute-start.3 = (bf16[32,16384]{1,0:T(8,128)(2,1)S(1)}, bf16[32,16384]{1,0:T(8,128)(2,1)}, u32[]{:S(2)}, u32[]{:S(2)}) collective-permute-start(bf16[32,16384]{1,0:T(8,128)(2,1)S(1)} %precondition.4.refs_1_), channel_id=1, source_target_pairs={{0,4},{1,3},{4,8},{5,1},{8,12},{9,5},{12,14},{13,9},{14,10},{15,13... | collective-permute-start | bytes 3145736 | tf_op jit(solution)/shard_map/ppermute | solution.py:182
  19.5 10.6 %collective-permute-start.4 = (bf16[32,16384]{1,0:T(8,128)(2,1)S(1)}, bf16[32,16384]{1,0:T(8,128)(2,1)}, u32[]{:S(2)}, u32[]{:S(2)}) collective-permute-start(bf16[32,16384]{1,0:T(8,128)(2,1)S(1)} %precondition.3.refs_2_), channel_id=1, source_target_pairs={{0,1},{1,0},{2,3},{3,2},{4,5},{5,4},{6,7},{7,6},{8,9},{9,8},{10,11... | collective-permute-start | bytes 3145736 | tf_op jit(solution)/shard_map/ppermute | solution.py:182
  19.6 23.1 %collective-permute-start.1 = (bf16[32,16384]{1,0:T(8,128)(2,1)S(1)}, bf16[32,16384]{1,0:T(8,128)(2,1)}, u32[]{:S(2)}, u32[]{:S(2)}) collective-permute-start(bf16[32,16384]{1,0:T(8,128)(2,1)S(1)} %precondition.3.refs_2_), channel_id=1, source_target_pairs={{0,4},{1,3},{4,8},{5,1},{8,12},{9,5},{12,14},{13,9},{14,10},{15,13... | collective-permute-start | bytes 3145736 | tf_op jit(solution)/shard_map/ppermute | solution.py:182
  21.7 1.2 %copy-start.2 = (bf16[32,16384]{1,0:T(8,128)(2,1)S(1)}, bf16[32,16384]{1,0:T(8,128)(2,1)}, u32[]{:S(2)}) copy-start(bf16[32,16384]{1,0:T(8,128)(2,1)} %refs_0_) | copy-start | bytes 3145732
  27.3 22.5 %collective-permute-start.7 = (bf16[32,16384]{1,0:T(8,128)(2,1)}, bf16[32,16384]{1,0:T(8,128)(2,1)}, u32[]{:S(2)}, u32[]{:S(2)}) collective-permute-start(bf16[32,16384]{1,0:T(8,128)(2,1)} %collective-permute-done.3.refs_0_), channel_id=1, source_target_pairs={{0,4},{1,3},{4,8},{5,1},{8,12},{9,5},{12,14},{13,9},{14,10},{15,13... | collective-permute-start | bytes 3145736 | tf_op jit(solution)/shard_map/ppermute | solution.py:182
  30.1 5.8 %copy-start = (bf16[512,16384]{1,0:T(8,128)(2,1)S(1)}, bf16[512,16384]{1,0:T(8,128)(2,1)}, u32[]{:S(2)}) copy-start(bf16[512,16384]{1,0:T(8,128)(2,1)} %query_ref.7) | copy-start | bytes 50331652
  35.8 27.3 %copy-start.1 = (bf16[512,16384]{1,0:T(8,128)(2,1)S(1)}, bf16[512,16384]{1,0:T(8,128)(2,1)}, u32[]{:S(2)}) copy-start(bf16[512,16384]{1,0:T(8,128)(2,1)} %query_ref.7) | copy-start | bytes 50331652
  42.7 18.2 %collective-permute-start.5 = (bf16[32,16384]{1,0:T(8,128)(2,1)}, bf16[32,16384]{1,0:T(8,128)(2,1)S(1)}, u32[]{:S(2)}, u32[]{:S(2)}) collective-permute-start(bf16[32,16384]{1,0:T(8,128)(2,1)} %collective-permute-done.1.refs_2_), channel_id=1, source_target_pairs={{0,4},{1,3},{4,8},{5,1},{8,12},{9,5},{12,14},{13,9},{14,10},{15,13... | collective-permute-start | bytes 3145736 | tf_op jit(solution)/shard_map/ppermute | solution.py:182
  44.4 16.6 %collective-permute-start.10 = (bf16[32,16384]{1,0:T(8,128)(2,1)}, bf16[32,16384]{1,0:T(8,128)(2,1)S(1)}, u32[]{:S(2)}, u32[]{:S(2)}) collective-permute-start(bf16[32,16384]{1,0:T(8,128)(2,1)} %collective-permute-done.1.refs_2_), channel_id=1, source_target_pairs={{0,1},{1,0},{2,3},{3,2},{4,5},{5,4},{6,7},{7,6},{8,9},{9,8},{10,11... | collective-permute-start | bytes 3145736 | tf_op jit(solution)/shard_map/ppermute | solution.py:182
  44.4 18.8 %collective-permute-start.9 = (bf16[32,16384]{1,0:T(8,128)(2,1)}, bf16[32,16384]{1,0:T(8,128)(2,1)S(1)}, u32[]{:S(2)}, u32[]{:S(2)}) collective-permute-start(bf16[32,16384]{1,0:T(8,128)(2,1)} %collective-permute-done.3.refs_0_), channel_id=1, source_target_pairs={{0,1},{1,0},{2,3},{3,2},{4,5},{5,4},{6,7},{7,6},{8,9},{9,8},{10,11... | collective-permute-start | bytes 3145736 | tf_op jit(solution)/shard_map/ppermute | solution.py:182
  49.8 13.4 %collective-permute-start.11 = (bf16[32,16384]{1,0:T(8,128)(2,1)}, bf16[32,16384]{1,0:T(8,128)(2,1)S(1)}, u32[]{:S(2)}, u32[]{:S(2)}) collective-permute-start(bf16[32,16384]{1,0:T(8,128)(2,1)} %collective-permute-done.7.refs_4_), channel_id=1, source_target_pairs={{0,1},{1,0},{2,3},{3,2},{4,5},{5,4},{6,7},{7,6},{8,9},{9,8},{10,11... | collective-permute-start | bytes 3145736 | tf_op jit(solution)/shard_map/ppermute | solution.py:182
  49.8 22.4 %collective-permute-start.8 = (bf16[32,16384]{1,0:T(8,128)(2,1)}, bf16[32,16384]{1,0:T(8,128)(2,1)S(1)}, u32[]{:S(2)}, u32[]{:S(2)}) collective-permute-start(bf16[32,16384]{1,0:T(8,128)(2,1)} %collective-permute-done.7.refs_4_), channel_id=1, source_target_pairs={{0,4},{1,3},{4,8},{5,1},{8,12},{9,5},{12,14},{13,9},{14,10},{15,13... | collective-permute-start | bytes 3145736 | tf_op jit(solution)/shard_map/ppermute | solution.py:182
  60.9 19.2 %collective-permute-start.6 = (bf16[32,16384]{1,0:T(8,128)(2,1)S(1)}, bf16[32,16384]{1,0:T(8,128)(2,1)S(1)}, u32[]{:S(2)}, u32[]{:S(2)}) collective-permute-start(bf16[32,16384]{1,0:T(8,128)(2,1)S(1)} %collective-permute-done.5.source_ref.refs_0_), channel_id=1, source_target_pairs={{0,1},{1,0},{2,3},{3,2},{4,5},{5,4},{6,7},{7,6},{8,9},{9,8},{10,11... | collective-permute-start | bytes 3145736 | tf_op jit(solution)/shard_map/ppermute | solution.py:182
  61.0 16.1 %collective-permute-start.15 = (bf16[32,7168]{1,0:T(8,128)(2,1)S(1)}, bf16[32,7168]{1,0:T(8,128)(2,1)S(1)}, u32[]{:S(2)}, u32[]{:S(2)}) collective-permute-start(bf16[32,7168]{1,0:T(8,128)(2,1)S(1)} %get-tuple-element.39), channel_id=1, source_target_pairs={{0,4},{1,3},{4,8},{5,1},{8,12},{9,5},{12,14},{13,9},{14,10},{15,13... | collective-permute-start | bytes 1376264 | tf_op jit(solution)/shard_map/ppermute | solution.py:182
  72.1 11.3 %collective-permute-start.14 = (bf16[32,9216]{1,0:T(8,128)(2,1)S(1)}, bf16[32,9216]{1,0:T(8,128)(2,1)S(1)}, u32[]{:S(2)}, u32[]{:S(2)}) collective-permute-start(bf16[32,9216]{1,0:T(8,128)(2,1)S(1)} %get-tuple-element.38), channel_id=1, source_target_pairs={{0,4},{1,3},{4,8},{5,1},{8,12},{9,5},{12,14},{13,9},{14,10},{15,13... | collective-permute-start | bytes 1769480 | tf_op jit(solution)/shard_map/ppermute | solution.py:182
  74.3 5.8 %collective-permute-start.12 = (bf16[16,16384]{1,0:T(8,128)(2,1)S(1)}, bf16[16,16384]{1,0:T(8,128)(2,1)S(1)}, u32[]{:S(2)}, u32[]{:S(2)}) collective-permute-start(bf16[16,16384]{1,0:T(8,128)(2,1)S(1)} %get-tuple-element.36), channel_id=1, source_target_pairs={{0,1},{1,0},{2,3},{3,2},{4,5},{5,4},{6,7},{7,6},{8,9},{9,8},{10,11... | collective-permute-start | bytes 1572872 | tf_op jit(solution)/shard_map/ppermute | solution.py:182
  74.4 5.8 %collective-permute-start.13 = (bf16[16,16384]{1,0:T(8,128)(2,1)S(1)}, bf16[16,16384]{1,0:T(8,128)(2,1)S(1)}, u32[]{:S(2)}, u32[]{:S(2)}) collective-permute-start(bf16[16,16384]{1,0:T(8,128)(2,1)S(1)} %get-tuple-element.37), channel_id=1, source_target_pairs={{0,1},{1,0},{2,3},{3,2},{4,5},{5,4},{6,7},{7,6},{8,9},{9,8},{10,11... | collective-permute-start | bytes 1572872 | tf_op jit(solution)/shard_map/ppermute | solution.py:182
  77.1 1.6 %collective-permute-start.16 = (bf16[16,7168]{1,0:T(8,128)(2,1)S(1)}, bf16[16,7168]{1,0:T(8,128)(2,1)S(1)}, u32[]{:S(2)}, u32[]{:S(2)}) collective-permute-start(bf16[16,7168]{1,0:T(8,128)(2,1)S(1)} %get-tuple-element.40), channel_id=1, source_target_pairs={{0,1},{1,0},{2,3},{3,2},{4,5},{5,4},{6,7},{7,6},{8,9},{9,8},{10,11... | collective-permute-start | bytes 688136 | tf_op jit(solution)/shard_map/ppermute | solution.py:182
  78.6 1.5 %collective-permute-start.17 = (bf16[16,7168]{1,0:T(8,128)(2,1)S(1)}, bf16[16,7168]{1,0:T(8,128)(2,1)S(1)}, u32[]{:S(2)}, u32[]{:S(2)}) collective-permute-start(bf16[16,7168]{1,0:T(8,128)(2,1)S(1)} %get-tuple-element.41), channel_id=1, source_target_pairs={{0,1},{1,0},{2,3},{3,2},{4,5},{5,4},{6,7},{7,6},{8,9},{9,8},{10,11... | collective-permute-start | bytes 688136 | tf_op jit(solution)/shard_map/ppermute | solution.py:182
  83.5 2.1 %collective-permute-start.18 = (bf16[32,9216]{1,0:T(8,128)(2,1)S(1)}, bf16[32,9216]{1,0:T(8,128)(2,1)S(1)}, u32[]{:S(2)}, u32[]{:S(2)}) collective-permute-start(bf16[32,9216]{1,0:T(8,128)(2,1)S(1)} %collective-permute-done.14.refs_5_), channel_id=1, source_target_pairs={{0,1},{1,0},{2,3},{3,2},{4,5},{5,4},{6,7},{7,6},{8,9},{9,8},{10,11... | collective-permute-start | bytes 1769480 | tf_op jit(solution)/shard_map/ppermute | solution.py:182

commit v4 on v3

--- a/solution.py
+++ b/solution.py
@@ -2,7 +2,6 @@
 
 import jax
 import jax.numpy as jnp
-import numpy as np
 from jax import lax
 from jax.experimental import pallas as pl
 from jax.experimental.pallas import tpu as pltpu
@@ -11,12 +10,13 @@
 A_DIM = 128
 B_DIM = 128
 LANES = 128
-K_TILE = 4608
+K_TILE = 9216
+RESULT_PARTS = 4
 KERNEL_VMEM = 16 << 20
 PREPARE_COST = pl.CostEstimate(flops=1, bytes_accessed=1, transcendentals=0)
 SCORE_COST = pl.CostEstimate(flops=1, bytes_accessed=1, transcendentals=0)
 CUT_COST = pl.CostEstimate(flops=1, bytes_accessed=1, transcendentals=0)
-LAST_PARTS = 7, 9
+LAST_PARTS = 15, 17
 ANY_SPEC = pl.BlockSpec(memory_space=pl.ANY)
 VMEM_SPEC = pl.BlockSpec(memory_space=pltpu.VMEM)
 
@@ -84,65 +84,100 @@
     )(*operands)
 
 
-def scores_kernel(entries, count, begin, first, last, owners_ref, query_ref, *refs):
+def owner_of(entry, chips):
+    here = lax.axis_index("wide")
+    arrival, side = entry // 2, entry % 2
+    chip, core = lax.div(here, 2), lax.rem(here, 2)
+    hop, crossed = (arrival + 1) // 2, (arrival + 1) % 2 if arrival else 0
+    step = jnp.where(core == side, -hop, hop)
+    ladder = chips == 8
+    spot = jnp.where(lax.rem(chip, 2) == 0, lax.div(chip, 2), chips - 1 - lax.div(chip, 2)) if ladder else chip
+    spot = lax.rem(spot + step + chips, chips)
+    chip = jnp.where(spot < chips // 2, 2 * spot, 2 * chips - 1 - 2 * spot) if ladder else spot
+    return 2 * chip + (1 - core if (side + crossed) % 2 else core)
+
+
+def scores_kernel(entries, count, begin, first, last, query_ref, *refs):
     blocks, refs = refs[:count], refs[count:]
     if not first:
         total_ref, refs = refs[0], refs[1:]
-    out_ref, sum_ref = refs
+    out_ref, sum_ref = refs[:2]
     height = blocks[0].shape[0]
     width = min(block.shape[1] for block in blocks)
     tile = column_tile(width)
+    steps = width // tile
     missing = sum_ref.shape[1] - sum(block.shape[0] for block in blocks)
+    chips = out_ref.shape[1] // height // 2
     if first:
         out_ref[...] = jnp.zeros_like(out_ref)
-    if last:
-        out_ref[...] = total_ref[...]
-    sum_ref[...] = jnp.zeros_like(sum_ref)
-
-    @pl.loop(0, width // tile)
-    def _(step):
+
+    def product(step):
         def columns(skipped):
             return pl.ds(pl.multiple_of(skipped + step * tile, LANES), tile)
 
         rows = [block[:, columns(begin if block.shape[1] > width else 0)] for block in blocks]
         if missing:
             rows.append(jnp.zeros((missing, tile), rows[0].dtype))
-        sum_ref[...] += lax.dot_general(
+        return lax.dot_general(
             query_ref[:, columns(begin)], jnp.concatenate(rows, axis=0), (((1,), (1,)), ((), ())),
             preferred_element_type=jnp.float32,
         )
 
+    sum_ref[...] = product(0)
+    if steps > 1:
+        @pl.loop(1, steps)
+        def _(step):
+            sum_ref[...] += product(step)
+
     per_tile = LANES // height
-    place = lax.broadcasted_iota(jnp.int32, (sum_ref.shape[0], LANES), 1) // height
-    for i, entry in enumerate(entries):
-        owner = owners_ref[entry]
-        spot = lax.rem(owner, per_tile)
-        held = sum_ref[:, i // per_tile * LANES:(i // per_tile + 1) * LANES]
-        moved = pltpu.roll(held, lax.rem(spot - i % per_tile + per_tile, per_tile) * height, 1)
-        lanes = pl.ds(pl.multiple_of(lax.div(owner, per_tile) * LANES, LANES), LANES)
-        out_ref[:, lanes] += jnp.where(place == spot, moved, 0.0)
+    owners = [owner_of(entry, chips) for entry in entries]
+
+    def add(target_ref, rows):
+        place = lax.broadcasted_iota(jnp.int32, (rows.size, LANES), 1) // height
+        for i, owner in enumerate(owners):
+            spot = lax.rem(owner, per_tile)
+            held = sum_ref[rows, i // per_tile * LANES:(i // per_tile + 1) * LANES]
+            moved = pltpu.roll(held, lax.rem(spot - i % per_tile + per_tile, per_tile) * height, 1)
+            lanes = pl.ds(pl.multiple_of(lax.div(owner, per_tile) * LANES, LANES), LANES)
+            target_ref[rows, lanes] += jnp.where(place == spot, moved, 0.0)
+
+    if not last:
+        add(out_ref, pl.ds(0, out_ref.shape[0]))
+        return
+    result_ref, sems = refs[2:]
+    size = out_ref.shape[0] // RESULT_PARTS
+    copies = []
+    for i in range(RESULT_PARTS):
+        rows = pl.ds(i * size, size)
+        result_ref[rows, :] = total_ref[rows, :]
+        add(result_ref, rows)
+        copies.append(pltpu.make_async_copy(result_ref.at[rows, :], out_ref.at[rows, :], sems.at[i]))
+        copies[-1].start()
+    for copy in copies:
+        copy.wait()
 
 
 def column_tile(width):
     return max(t for t in range(LANES, min(K_TILE, width) + 1, LANES) if width % t == 0)
 
 
-def add_scores(total, queries, owners, entries, blocks, train_count, begin=0, last=False):
+def add_scores(total, queries, entries, blocks, train_count, begin=0, last=False):
     rows = queries.shape[0]
     first = total is None
     operands = [pltpu.with_memory_space_constraint(queries, pltpu.VMEM), *blocks] + ([] if first else [total])
     lanes = -(-len(entries) * blocks[0].shape[0] // LANES) * LANES
+    result = [pltpu.VMEM((rows, train_count), jnp.float32), pltpu.SemaphoreType.DMA((RESULT_PARTS,))]
     return pl.pallas_call(
         functools.partial(scores_kernel, entries, len(blocks), begin, first, last),
         out_shape=jax.ShapeDtypeStruct((rows, train_count), jnp.float32),
-        in_specs=[pl.BlockSpec(memory_space=pltpu.SMEM)] + [VMEM_SPEC] * len(operands),
-        out_specs=VMEM_SPEC,
-        scratch_shapes=[pltpu.VMEM((rows, lanes), jnp.float32)],
-        input_output_aliases={} if first or last else {len(operands): 0},
+        in_specs=[VMEM_SPEC] * len(operands),
+        out_specs=ANY_SPEC if last else VMEM_SPEC,
+        scratch_shapes=[pltpu.VMEM((rows, lanes), jnp.float32)] + (result if last else []),
+        input_output_aliases={} if first or last else {len(operands) - 1: 0},
         compiler_params=pltpu.CompilerParams(vmem_limit_bytes=KERNEL_VMEM),
         cost_estimate=SCORE_COST,
         name="scores",
-    )(owners, *operands)
+    )(*operands)
 
 
 def cut_kernel(source_ref, *pieces):
@@ -181,20 +216,6 @@
     across = [(d, d ^ 1) for d in range(devices)]
     send = lambda block, pairs: lax.ppermute(block, "wide", pairs)
 
-    table = np.zeros((devices, devices), np.int32)
-    for i in range(chips):
-        for core in range(2):
-            row = [2 * ring[i] + core, 2 * ring[i] + 1 - core]
-            for arrival in range(1, chips):
-                hop, swapped = (arrival + 1) // 2, (arrival + 1) % 2
-                step = hop if core else -hop
-                row += [
-                    2 * ring[(i + step) % chips] + (core ^ swapped),
-                    2 * ring[(i - step) % chips] + (1 ^ core ^ swapped),
-                ]
-            table[row[0]] = row
-    owners = lax.dynamic_index_in_dim(jnp.asarray(table), lax.axis_index("wide"), 0, keepdims=False)
-
     def after(block, array):
         return lax.optimization_barrier((block, array))
 
@@ -206,7 +227,7 @@
     chains = [raw, other]
     blocks = [own, other]
     score = lambda total, arrivals, blocks, **kw: add_scores(
-        total, queries, owners, [e for a in arrivals for e in (2 * a, 2 * a + 1)], blocks, train_count, **kw
+        total, queries, [e for a in arrivals for e in (2 * a, 2 * a + 1)], blocks, train_count, **kw
     )
     pairs = [[own, other]]
     groups = [[a, a + 1] for a in range(0, chips - 6, 2)] + [[chips - 6, chips - 5, chips - 4]]
@@ -242,7 +263,7 @@
             total = score(total, group, blocks, begin=begin)
             begin += widths[i - 1]
             part, total = after(part, total)
-        swapped = [part] if last else cut(part, [(height // 2, widths[i])] * 2)
+        swapped = [part]
         blocks = pairs[chips - 3] + pairs[chips - 2] + [part] + [send(piece, across) for piece in swapped]
     return score(total, group, blocks, begin=begin, last=True)
 

time: 90.8 us -> 89.6 us (0.987)
  Pallas kernels: 33.3 us -> 27 us
  waiting for transfers between devices: 29.7 us -> 35.5 us
    pallas_call x4, Pallas kernels: 22.6 us -> 16.3 us  [add_scores(): pl.pallas_call(functools.partial(scores_kernel, entries, len(blocks), beg...]
    ppermute x19 -> x18, waiting for transfers between devices: 29.7 us -> 35.5 us  [per_device(): send = lambda block, pairs: lax.ppermute(block, 'wide', pairs)]
    ppermute x19 -> x18, starting transfers between devices: 19.6 us -> 19.4 us  [per_device(): send = lambda block, pairs: lax.ppermute(block, 'wide', pairs)]
  transfers between devices with their start and end apart: 19 -> 18, of which waited for: 9 -> 9; matrix products, arithmetic and copies ran while one was open for 1% -> 0% of each run, Pallas kernels for 31% -> 26%
where the time goes in v4:
time: 89.6 us; the launch traced here: 89.2 us
  waiting for transfers between devices  35.5 us (40%)
  Pallas kernels  27 us (30%)
  starting transfers between devices  19.4 us (22%)
  local copies, waits for them, and re-layouts  7 us (8%)
    ppermute x18, waiting for transfers between devices, per_device(): send = lambda block, pairs: lax.ppermute(block, 'wide', pairs)  35.5 us
    ppermute x18, starting transfers between devices, per_device(): send = lambda block, pairs: lax.ppermute(block, 'wide', pairs)  19.4 us
    pallas_call x4, Pallas kernels, add_scores(): pl.pallas_call(functools.partial(scores_kernel, entries, len(blocks), beg...  16.3 us
    pallas_call x3, Pallas kernels, precondition(): pl.pallas_call(precondition_kernel, out_shape=jax.ShapeDtypeStruct(rows.s...  10.6 us
    unnamed x6, local copies, waits for them, and re-layouts  7 us
  transfers between devices with their start and end apart: 18, of which 9 were waited for; matrix products, arithmetic and copies ran while one was open for 0% of the time, Pallas kernels for 26%

profile of v4, /device:TPU:0, one launch (start us, length us, event | category | flops | bytes accessed | tf_op | source)
XLA Modules:
  0.0 89.2 jit_solution(15711943204032257158)
XLA Ops:
  0.0 0.5 collective-permute-start.2
  0.5 2.6 %collective-permute-start = (bf16[32,16384]{1,0:T(8,128)(2,1)}, bf16[32,16384]{1,0:T(8,128)(2,1)S(1)}, u32[]{:S(2)}, u32[]{:S(2)}) collective-permute-start(bf16[32,16384]{1,0:T(8,128)(2,1)} %refs_0_), channel_id=1, source_target_pairs={{0,4},{1,3},{4,8},{5,1},{8,12},{9,5},{12,14},{13,9},{14,10},{15,13... | collective-permute-start | bytes 3145736 | tf_op jit(solution)/shard_map/ppermute | solution.py:217
  3.0 0.0 collective-permute-done.2.refs_0_
  3.0 3.5 %precondition.4.refs_1_ = bf16[32,16384]{1,0:T(8,128)(2,1)S(1)} custom-call(bf16[32,16384]{1,0:T(8,128)(2,1)S(1)} %collective-permute-done.2.refs_0_, bf16[128,128]{1,0:T(8,128)(2,1)} %refs_1_.5, bf16[128,128]{1,0:T(8,128)(2,1)} %refs_2_.5, f32[128,128]{1,0:T(8,128)} %refs_3_.5), custom_call_target="tpu_custom_call" | custom-call | flops 1 | bytes 1 | tf_op jit(solution)/shard_map/precondition/pallas_call | solution.py:73
  6.6 2.9 %collective-permute-start.3 = (bf16[32,16384]{1,0:T(8,128)(2,1)S(1)}, bf16[32,16384]{1,0:T(8,128)(2,1)S(1)}, u32[]{:S(2)}, u32[]{:S(2)}) collective-permute-start(bf16[32,16384]{1,0:T(8,128)(2,1)S(1)} %precondition.4.refs_1_), channel_id=1, source_target_pairs={{0,4},{1,3},{4,8},{5,1},{8,12},{9,5},{12,14},{13,9},{14,10},{15,13... | collective-permute-start | bytes 3145736 | tf_op jit(solution)/shard_map/ppermute | solution.py:217
  9.5 6.5 %collective-permute-done.refs_0_ = bf16[32,16384]{1,0:T(8,128)(2,1)S(1)} collective-permute-done((bf16[32,16384]{1,0:T(8,128)(2,1)}, bf16[32,16384]{1,0:T(8,128)(2,1)S(1)}, u32[]{:S(2)}, u32[]{:S(2)}) %collective-permute-start) | collective-permute-done | bytes 1048608 | tf_op jit(solution)/shard_map/ppermute | solution.py:217
  16.0 3.5 %precondition.3.refs_2_ = bf16[32,16384]{1,0:T(8,128)(2,1)S(1)} custom-call(bf16[32,16384]{1,0:T(8,128)(2,1)S(1)} %collective-permute-done.refs_0_, bf16[128,128]{1,0:T(8,128)(2,1)} %refs_1_.5, bf16[128,128]{1,0:T(8,128)(2,1)} %refs_2_.5, f32[128,128]{1,0:T(8,128)} %refs_3_.5), custom_call_target="tpu_custom_call" | custom-call | flops 1 | bytes 1 | tf_op jit(solution)/shard_map/precondition/pallas_call | solution.py:73
  19.5 0.1 collective-permute-start.4
  19.6 2.1 %collective-permute-start.1 = (bf16[32,16384]{1,0:T(8,128)(2,1)S(1)}, bf16[32,16384]{1,0:T(8,128)(2,1)S(1)}, u32[]{:S(2)}, u32[]{:S(2)}) collective-permute-start(bf16[32,16384]{1,0:T(8,128)(2,1)S(1)} %precondition.3.refs_2_), channel_id=1, source_target_pairs={{0,4},{1,3},{4,8},{5,1},{8,12},{9,5},{12,14},{13,9},{14,10},{15,13... | collective-permute-start | bytes 3145736 | tf_op jit(solution)/shard_map/ppermute | solution.py:217
  21.7 0.0 copy-start.2
  21.7 1.2 %copy-done.2 = bf16[32,16384]{1,0:T(8,128)(2,1)S(1)} copy-done((bf16[32,16384]{1,0:T(8,128)(2,1)S(1)}, bf16[32,16384]{1,0:T(8,128)(2,1)}, u32[]{:S(2)}) %copy-start.2) | copy-done | bytes 1048600
  22.9 3.5 %precondition.5.refs_0_ = bf16[32,16384]{1,0:T(8,128)(2,1)S(1)} custom-call(bf16[32,16384]{1,0:T(8,128)(2,1)S(1)} %copy-done.2, bf16[128,128]{1,0:T(8,128)(2,1)} %refs_1_.5, bf16[128,128]{1,0:T(8,128)(2,1)} %refs_2_.5, f32[128,128]{1,0:T(8,128)} %refs_3_.5), custom_call_target="tpu_custom_call" | custom-call | flops 1 | bytes 1 | tf_op jit(solution)/shard_map/precondition/pallas_call | solution.py:73
  26.4 0.7 collective-permute-done.3.refs_0_
  27.2 2.1 %collective-permute-start.7 = (bf16[32,16384]{1,0:T(8,128)(2,1)S(1)}, bf16[32,16384]{1,0:T(8,128)(2,1)S(1)}, u32[]{:S(2)}, u32[]{:S(2)}) collective-permute-start(bf16[32,16384]{1,0:T(8,128)(2,1)S(1)} %collective-permute-done.3.refs_0_), channel_id=1, source_target_pairs={{0,4},{1,3},{4,8},{5,1},{8,12},{9,5},{12,14},{13,9},{14,10},{15,13... | collective-permute-start | bytes 3145736 | tf_op jit(solution)/shard_map/ppermute | solution.py:217
  29.3 0.0 collective-permute-done.4.refs_3_
  29.3 0.0 copy-start
  29.3 5.8 %copy-done = bf16[512,16384]{1,0:T(8,128)(2,1)S(1)} copy-done((bf16[512,16384]{1,0:T(8,128)(2,1)S(1)}, bf16[512,16384]{1,0:T(8,128)(2,1)}, u32[]{:S(2)}) %copy-start) | copy-done | bytes 16777240
  35.0 0.0 copy-start.1
  35.0 4.8 %scores.4.refs_6_ = f32[512,512]{1,0:T(8,128)S(1)} custom-call(bf16[512,16384]{1,0:T(8,128)(2,1)S(1)} %copy-done, bf16[32,16384]{1,0:T(8,128)(2,1)S(1)} %precondition.5.refs_0_, bf16[32,16384]{1,0:T(8,128)(2,1)S(1)} %precondition.4.refs_1_, bf16[32,16384]{1,0:T(8,128)(2,1)S(1)} %precondition.3.refs_2_, bf16[32,16384]{1,0:T(8,128)(2,1)S(1)} %collective-permute-done.4.refs_3_), custom_call_target="tpu_custom_call" | custom-call | flops 1 | bytes 1 | tf_op jit(solution)/shard_map/scores/pallas_call | solution.py:170
  39.9 0.0 collective-permute-done.1.refs_2_
  39.9 1.6 %collective-permute-start.5 = (bf16[32,16384]{1,0:T(8,128)(2,1)S(1)}, bf16[32,16384]{1,0:T(8,128)(2,1)S(1)}, u32[]{:S(2)}, u32[]{:S(2)}) collective-permute-start(bf16[32,16384]{1,0:T(8,128)(2,1)S(1)} %collective-permute-done.1.refs_2_), channel_id=1, source_target_pairs={{0,4},{1,3},{4,8},{5,1},{8,12},{9,5},{12,14},{13,9},{14,10},{15,13... | collective-permute-start | bytes 3145736 | tf_op jit(solution)/shard_map/ppermute | solution.py:217
  41.5 0.0 collective-permute-start.10
  41.5 0.5 collective-permute-start.9
  42.0 7.7 %collective-permute-done.7.refs_4_ = bf16[32,16384]{1,0:T(8,128)(2,1)S(1)} collective-permute-done((bf16[32,16384]{1,0:T(8,128)(2,1)S(1)}, bf16[32,16384]{1,0:T(8,128)(2,1)S(1)}, u32[]{:S(2)}, u32[]{:S(2)}) %collective-permute-start.7) | collective-permute-done | bytes 1048608 | tf_op jit(solution)/shard_map/ppermute | solution.py:217
  49.7 0.0 collective-permute-start.11
  49.7 2.1 %collective-permute-start.8 = (bf16[32,16384]{1,0:T(8,128)(2,1)S(1)}, bf16[32,16384]{1,0:T(8,128)(2,1)S(1)}, u32[]{:S(2)}, u32[]{:S(2)}) collective-permute-start(bf16[32,16384]{1,0:T(8,128)(2,1)S(1)} %collective-permute-done.7.refs_4_), channel_id=1, source_target_pairs={{0,4},{1,3},{4,8},{5,1},{8,12},{9,5},{12,14},{13,9},{14,10},{15,13... | collective-permute-start | bytes 3145736 | tf_op jit(solution)/shard_map/ppermute | solution.py:217
  51.7 9.2 %collective-permute-done.5.source_ref.refs_0_ = bf16[32,16384]{1,0:T(8,128)(2,1)S(1)} collective-permute-done((bf16[32,16384]{1,0:T(8,128)(2,1)S(1)}, bf16[32,16384]{1,0:T(8,128)(2,1)S(1)}, u32[]{:S(2)}, u32[]{:S(2)}) %collective-permute-start.5) | collective-permute-done | bytes 1048608 | tf_op jit(solution)/shard_map/ppermute | solution.py:217
  60.9 0.0 collective-permute-start.6
  60.9 0.1 cut.2
  61.0 0.0 collective-permute-done.10.refs_3_
  61.0 2.3 %collective-permute-start.15 = (bf16[32,7680]{1,0:T(8,128)(2,1)S(1)}, bf16[32,7680]{1,0:T(8,128)(2,1)S(1)}, u32[]{:S(2)}, u32[]{:S(2)}) collective-permute-start(bf16[32,7680]{1,0:T(8,128)(2,1)S(1)} %get-tuple-element.37), channel_id=1, source_target_pairs={{0,4},{1,3},{4,8},{5,1},{8,12},{9,5},{12,14},{13,9},{14,10},{15,13... | collective-permute-start | bytes 1474568 | tf_op jit(solution)/shard_map/ppermute | solution.py:217
  63.3 0.0 collective-permute-done.9.refs_1_
  63.3 0.0 collective-permute-done.11.refs_5_
  63.3 0.0 copy-done.1
  63.3 5.0 %scores.5.refs_7_ = f32[512,512]{1,0:T(8,128)S(1)} custom-call(bf16[512,16384]{1,0:T(8,128)(2,1)S(1)} %copy-done.1, bf16[32,16384]{1,0:T(8,128)(2,1)S(1)} %collective-permute-done.3.refs_0_, bf16[32,16384]{1,0:T(8,128)(2,1)S(1)} %collective-permute-done.9.refs_1_, ...), custom_call_target="tpu_custom_call", output_to_operand_aliasing={{}: (7, {})} | custom-call | flops 1 | bytes 1 | tf_op jit(solution)/shard_map/scores/pallas_call | solution.py:170
  68.4 3.8 %collective-permute-done.8.source_ref.refs_2_ = bf16[32,16384]{1,0:T(8,128)(2,1)S(1)} collective-permute-done((bf16[32,16384]{1,0:T(8,128)(2,1)S(1)}, bf16[32,16384]{1,0:T(8,128)(2,1)S(1)}, u32[]{:S(2)}, u32[]{:S(2)}) %collective-permute-start.8) | collective-permute-done | bytes 1048608 | tf_op jit(solution)/shard_map/ppermute | solution.py:217
  72.1 2.1 %collective-permute-start.14 = (bf16[32,8704]{1,0:T(8,128)(2,1)S(1)}, bf16[32,8704]{1,0:T(8,128)(2,1)S(1)}, u32[]{:S(2)}, u32[]{:S(2)}) collective-permute-start(bf16[32,8704]{1,0:T(8,128)(2,1)S(1)} %get-tuple-element.36), channel_id=1, source_target_pairs={{0,4},{1,3},{4,8},{5,1},{8,12},{9,5},{12,14},{13,9},{14,10},{15,13... | collective-permute-start | bytes 1671176 | tf_op jit(solution)/shard_map/ppermute | solution.py:217
  74.2 0.1 cut.3
  74.3 0.1 collective-permute-start.12
  74.4 0.5 collective-permute-start.13
  74.9 2.5 %collective-permute-done.15.refs_5_ = bf16[32,7680]{1,0:T(8,128)(2,1)S(1)} collective-permute-done((bf16[32,7680]{1,0:T(8,128)(2,1)S(1)}, bf16[32,7680]{1,0:T(8,128)(2,1)S(1)}, u32[]{:S(2)}, u32[]{:S(2)}) %collective-permute-start.15) | collective-permute-done | bytes 491552 | tf_op jit(solution)/shard_map/ppermute | solution.py:217
  77.4 0.0 collective-permute-start.16
  77.4 1.9 %collective-permute-done.16.refs_6_ = bf16[32,7680]{1,0:T(8,128)(2,1)S(1)} collective-permute-done((bf16[32,7680]{1,0:T(8,128)(2,1)S(1)}, bf16[32,7680]{1,0:T(8,128)(2,1)S(1)}, u32[]{:S(2)}, u32[]{:S(2)}) %collective-permute-start.16) | collective-permute-done | bytes 491552 | tf_op jit(solution)/shard_map/ppermute | solution.py:217
  79.3 0.0 collective-permute-done.6.refs_1_
  79.3 0.0 collective-permute-done.12.refs_3_
  79.3 0.0 collective-permute-done.13.refs_4_
  79.3 2.8 %scores.6.refs_7_ = f32[512,512]{1,0:T(8,128)S(1)} custom-call(bf16[512,16384]{1,0:T(8,128)(2,1)S(1)} %copy-done.1, bf16[32,16384]{1,0:T(8,128)(2,1)S(1)} %collective-permute-done.5.source_ref.refs_0_, bf16[32,16384]{1,0:T(8,128)(2,1)S(1)} %collective-permute-done.6.refs_1_, ...), custom_call_target="tpu_custom_call", output_to_operand_aliasing={{}: (8, {})} | custom-call | flops 1 | bytes 1 | tf_op jit(solution)/shard_map/scores/pallas_call | solution.py:170
  82.0 1.3 %collective-permute-done.14.refs_5_ = bf16[32,8704]{1,0:T(8,128)(2,1)S(1)} collective-permute-done((bf16[32,8704]{1,0:T(8,128)(2,1)S(1)}, bf16[32,8704]{1,0:T(8,128)(2,1)S(1)}, u32[]{:S(2)}, u32[]{:S(2)}) %collective-permute-start.14) | collective-permute-done | bytes 557088 | tf_op jit(solution)/shard_map/ppermute | solution.py:217
  83.4 0.0 collective-permute-start.17
  83.4 2.0 %collective-permute-done.17.refs_6_ = bf16[32,8704]{1,0:T(8,128)(2,1)S(1)} collective-permute-done((bf16[32,8704]{1,0:T(8,128)(2,1)S(1)}, bf16[32,8704]{1,0:T(8,128)(2,1)S(1)}, u32[]{:S(2)}, u32[]{:S(2)}) %collective-permute-start.17) | collective-permute-done | bytes 557088 | tf_op jit(solution)/shard_map/ppermute | solution.py:217
  85.3 3.7 %scores.7 = f32[512,512]{1,0:T(8,128)} custom-call(bf16[512,16384]{1,0:T(8,128)(2,1)S(1)} %copy-done.1, bf16[32,16384]{1,0:T(8,128)(2,1)S(1)} %collective-permute-done.5.source_ref.refs_0_, bf16[32,16384]{1,0:T(8,128)(2,1)S(1)} %collective-permute-done.6.refs_1_, bf16[32,16384]{1,0:T(8,128)(2,1)S(1)} %collective-permute-done.8.source_ref.refs_2_, ...), custom_call_target="tpu_custom_call" | custom-call | flops 1 | bytes 1 | tf_op jit(solution)/shard_map/scores/pallas_call | solution.py:170
Async XLA Ops:
  0.0 3.0 %collective-permute-start.2 = (bf16[32,16384]{1,0:T(8,128)(2,1)}, bf16[32,16384]{1,0:T(8,128)(2,1)S(1)}, u32[]{:S(2)}, u32[]{:S(2)}) collective-permute-start(bf16[32,16384]{1,0:T(8,128)(2,1)} %refs_0_), channel_id=1, source_target_pairs={{0,1},{1,0},{2,3},{3,2},{4,5},{5,4},{6,7},{7,6},{8,9},{9,8},{10,11... | collective-permute-start | bytes 3145736 | tf_op jit(solution)/shard_map/ppermute | solution.py:217
  0.5 15.5 %collective-permute-start = (bf16[32,16384]{1,0:T(8,128)(2,1)}, bf16[32,16384]{1,0:T(8,128)(2,1)S(1)}, u32[]{:S(2)}, u32[]{:S(2)}) collective-permute-start(bf16[32,16384]{1,0:T(8,128)(2,1)} %refs_0_), channel_id=1, source_target_pairs={{0,4},{1,3},{4,8},{5,1},{8,12},{9,5},{12,14},{13,9},{14,10},{15,13... | collective-permute-start | bytes 3145736 | tf_op jit(solution)/shard_map/ppermute | solution.py:217
  6.6 20.6 %collective-permute-start.3 = (bf16[32,16384]{1,0:T(8,128)(2,1)S(1)}, bf16[32,16384]{1,0:T(8,128)(2,1)S(1)}, u32[]{:S(2)}, u32[]{:S(2)}) collective-permute-start(bf16[32,16384]{1,0:T(8,128)(2,1)S(1)} %precondition.4.refs_1_), channel_id=1, source_target_pairs={{0,4},{1,3},{4,8},{5,1},{8,12},{9,5},{12,14},{13,9},{14,10},{15,13... | collective-permute-start | bytes 3145736 | tf_op jit(solution)/shard_map/ppermute | solution.py:217
  19.5 9.8 %collective-permute-start.4 = (bf16[32,16384]{1,0:T(8,128)(2,1)S(1)}, bf16[32,16384]{1,0:T(8,128)(2,1)S(1)}, u32[]{:S(2)}, u32[]{:S(2)}) collective-permute-start(bf16[32,16384]{1,0:T(8,128)(2,1)S(1)} %precondition.3.refs_2_), channel_id=1, source_target_pairs={{0,1},{1,0},{2,3},{3,2},{4,5},{5,4},{6,7},{7,6},{8,9},{9,8},{10,11... | collective-permute-start | bytes 3145736 | tf_op jit(solution)/shard_map/ppermute | solution.py:217
  19.6 20.3 %collective-permute-start.1 = (bf16[32,16384]{1,0:T(8,128)(2,1)S(1)}, bf16[32,16384]{1,0:T(8,128)(2,1)S(1)}, u32[]{:S(2)}, u32[]{:S(2)}) collective-permute-start(bf16[32,16384]{1,0:T(8,128)(2,1)S(1)} %precondition.3.refs_2_), channel_id=1, source_target_pairs={{0,4},{1,3},{4,8},{5,1},{8,12},{9,5},{12,14},{13,9},{14,10},{15,13... | collective-permute-start | bytes 3145736 | tf_op jit(solution)/shard_map/ppermute | solution.py:217
  21.7 1.2 %copy-start.2 = (bf16[32,16384]{1,0:T(8,128)(2,1)S(1)}, bf16[32,16384]{1,0:T(8,128)(2,1)}, u32[]{:S(2)}) copy-start(bf16[32,16384]{1,0:T(8,128)(2,1)} %refs_0_) | copy-start | bytes 3145732
  27.2 22.5 %collective-permute-start.7 = (bf16[32,16384]{1,0:T(8,128)(2,1)S(1)}, bf16[32,16384]{1,0:T(8,128)(2,1)S(1)}, u32[]{:S(2)}, u32[]{:S(2)}) collective-permute-start(bf16[32,16384]{1,0:T(8,128)(2,1)S(1)} %collective-permute-done.3.refs_0_), channel_id=1, source_target_pairs={{0,4},{1,3},{4,8},{5,1},{8,12},{9,5},{12,14},{13,9},{14,10},{15,13... | collective-permute-start | bytes 3145736 | tf_op jit(solution)/shard_map/ppermute | solution.py:217
  29.3 5.8 %copy-start = (bf16[512,16384]{1,0:T(8,128)(2,1)S(1)}, bf16[512,16384]{1,0:T(8,128)(2,1)}, u32[]{:S(2)}) copy-start(bf16[512,16384]{1,0:T(8,128)(2,1)} %query_ref.7) | copy-start | bytes 50331652
  35.0 28.3 %copy-start.1 = (bf16[512,16384]{1,0:T(8,128)(2,1)S(1)}, bf16[512,16384]{1,0:T(8,128)(2,1)}, u32[]{:S(2)}) copy-start(bf16[512,16384]{1,0:T(8,128)(2,1)} %query_ref.7) | copy-start | bytes 50331652
  39.9 21.0 %collective-permute-start.5 = (bf16[32,16384]{1,0:T(8,128)(2,1)S(1)}, bf16[32,16384]{1,0:T(8,128)(2,1)S(1)}, u32[]{:S(2)}, u32[]{:S(2)}) collective-permute-start(bf16[32,16384]{1,0:T(8,128)(2,1)S(1)} %collective-permute-done.1.refs_2_), channel_id=1, source_target_pairs={{0,4},{1,3},{4,8},{5,1},{8,12},{9,5},{12,14},{13,9},{14,10},{15,13... | collective-permute-start | bytes 3145736 | tf_op jit(solution)/shard_map/ppermute | solution.py:217
  41.5 19.5 %collective-permute-start.10 = (bf16[32,16384]{1,0:T(8,128)(2,1)S(1)}, bf16[32,16384]{1,0:T(8,128)(2,1)S(1)}, u32[]{:S(2)}, u32[]{:S(2)}) collective-permute-start(bf16[32,16384]{1,0:T(8,128)(2,1)S(1)} %collective-permute-done.1.refs_2_), channel_id=1, source_target_pairs={{0,1},{1,0},{2,3},{3,2},{4,5},{5,4},{6,7},{7,6},{8,9},{9,8},{10,11... | collective-permute-start | bytes 3145736 | tf_op jit(solution)/shard_map/ppermute | solution.py:217
  41.5 21.8 %collective-permute-start.9 = (bf16[32,16384]{1,0:T(8,128)(2,1)S(1)}, bf16[32,16384]{1,0:T(8,128)(2,1)S(1)}, u32[]{:S(2)}, u32[]{:S(2)}) collective-permute-start(bf16[32,16384]{1,0:T(8,128)(2,1)S(1)} %collective-permute-done.3.refs_0_), channel_id=1, source_target_pairs={{0,1},{1,0},{2,3},{3,2},{4,5},{5,4},{6,7},{7,6},{8,9},{9,8},{10,11... | collective-permute-start | bytes 3145736 | tf_op jit(solution)/shard_map/ppermute | solution.py:217
  49.7 13.6 %collective-permute-start.11 = (bf16[32,16384]{1,0:T(8,128)(2,1)S(1)}, bf16[32,16384]{1,0:T(8,128)(2,1)S(1)}, u32[]{:S(2)}, u32[]{:S(2)}) collective-permute-start(bf16[32,16384]{1,0:T(8,128)(2,1)S(1)} %collective-permute-done.7.refs_4_), channel_id=1, source_target_pairs={{0,1},{1,0},{2,3},{3,2},{4,5},{5,4},{6,7},{7,6},{8,9},{9,8},{10,11... | collective-permute-start | bytes 3145736 | tf_op jit(solution)/shard_map/ppermute | solution.py:217
  49.7 22.5 %collective-permute-start.8 = (bf16[32,16384]{1,0:T(8,128)(2,1)S(1)}, bf16[32,16384]{1,0:T(8,128)(2,1)S(1)}, u32[]{:S(2)}, u32[]{:S(2)}) collective-permute-start(bf16[32,16384]{1,0:T(8,128)(2,1)S(1)} %collective-permute-done.7.refs_4_), channel_id=1, source_target_pairs={{0,4},{1,3},{4,8},{5,1},{8,12},{9,5},{12,14},{13,9},{14,10},{15,13... | collective-permute-start | bytes 3145736 | tf_op jit(solution)/shard_map/ppermute | solution.py:217
  60.9 18.4 %collective-permute-start.6 = (bf16[32,16384]{1,0:T(8,128)(2,1)S(1)}, bf16[32,16384]{1,0:T(8,128)(2,1)S(1)}, u32[]{:S(2)}, u32[]{:S(2)}) collective-permute-start(bf16[32,16384]{1,0:T(8,128)(2,1)S(1)} %collective-permute-done.5.source_ref.refs_0_), channel_id=1, source_target_pairs={{0,1},{1,0},{2,3},{3,2},{4,5},{5,4},{6,7},{7,6},{8,9},{9,8},{10,11... | collective-permute-start | bytes 3145736 | tf_op jit(solution)/shard_map/ppermute | solution.py:217
  61.0 16.4 %collective-permute-start.15 = (bf16[32,7680]{1,0:T(8,128)(2,1)S(1)}, bf16[32,7680]{1,0:T(8,128)(2,1)S(1)}, u32[]{:S(2)}, u32[]{:S(2)}) collective-permute-start(bf16[32,7680]{1,0:T(8,128)(2,1)S(1)} %get-tuple-element.37), channel_id=1, source_target_pairs={{0,4},{1,3},{4,8},{5,1},{8,12},{9,5},{12,14},{13,9},{14,10},{15,13... | collective-permute-start | bytes 1474568 | tf_op jit(solution)/shard_map/ppermute | solution.py:217
  72.1 11.2 %collective-permute-start.14 = (bf16[32,8704]{1,0:T(8,128)(2,1)S(1)}, bf16[32,8704]{1,0:T(8,128)(2,1)S(1)}, u32[]{:S(2)}, u32[]{:S(2)}) collective-permute-start(bf16[32,8704]{1,0:T(8,128)(2,1)S(1)} %get-tuple-element.36), channel_id=1, source_target_pairs={{0,4},{1,3},{4,8},{5,1},{8,12},{9,5},{12,14},{13,9},{14,10},{15,13... | collective-permute-start | bytes 1671176 | tf_op jit(solution)/shard_map/ppermute | solution.py:217
  74.3 5.0 %collective-permute-start.12 = (bf16[16,16384]{1,0:T(8,128)(2,1)S(1)}, bf16[16,16384]{1,0:T(8,128)(2,1)S(1)}, u32[]{:S(2)}, u32[]{:S(2)}) collective-permute-start(bf16[16,16384]{1,0:T(8,128)(2,1)S(1)} %get-tuple-element.34), channel_id=1, source_target_pairs={{0,1},{1,0},{2,3},{3,2},{4,5},{5,4},{6,7},{7,6},{8,9},{9,8},{10,11... | collective-permute-start | bytes 1572872 | tf_op jit(solution)/shard_map/ppermute | solution.py:217
  74.4 4.9 %collective-permute-start.13 = (bf16[16,16384]{1,0:T(8,128)(2,1)S(1)}, bf16[16,16384]{1,0:T(8,128)(2,1)S(1)}, u32[]{:S(2)}, u32[]{:S(2)}) collective-permute-start(bf16[16,16384]{1,0:T(8,128)(2,1)S(1)} %get-tuple-element.35), channel_id=1, source_target_pairs={{0,1},{1,0},{2,3},{3,2},{4,5},{5,4},{6,7},{7,6},{8,9},{9,8},{10,11... | collective-permute-start | bytes 1572872 | tf_op jit(solution)/shard_map/ppermute | solution.py:217
  77.4 1.9 %collective-permute-start.16 = (bf16[32,7680]{1,0:T(8,128)(2,1)S(1)}, bf16[32,7680]{1,0:T(8,128)(2,1)S(1)}, u32[]{:S(2)}, u32[]{:S(2)}) collective-permute-start(bf16[32,7680]{1,0:T(8,128)(2,1)S(1)} %collective-permute-done.15.refs_5_), channel_id=1, source_target_pairs={{0,1},{1,0},{2,3},{3,2},{4,5},{5,4},{6,7},{7,6},{8,9},{9,8},{10,11... | collective-permute-start | bytes 1474568 | tf_op jit(solution)/shard_map/ppermute | solution.py:217
  83.4 2.0 %collective-permute-start.17 = (bf16[32,8704]{1,0:T(8,128)(2,1)S(1)}, bf16[32,8704]{1,0:T(8,128)(2,1)S(1)}, u32[]{:S(2)}, u32[]{:S(2)}) collective-permute-start(bf16[32,8704]{1,0:T(8,128)(2,1)S(1)} %collective-permute-done.14.refs_5_), channel_id=1, source_target_pairs={{0,1},{1,0},{2,3},{3,2},{4,5},{5,4},{6,7},{7,6},{8,9},{9,8},{10,11... | collective-permute-start | bytes 1671176 | tf_op jit(solution)/shard_map/ppermute | solution.py:217

commit v5 on v4

--- a/solution.py
+++ b/solution.py
@@ -16,7 +16,7 @@
 PREPARE_COST = pl.CostEstimate(flops=1, bytes_accessed=1, transcendentals=0)
 SCORE_COST = pl.CostEstimate(flops=1, bytes_accessed=1, transcendentals=0)
 CUT_COST = pl.CostEstimate(flops=1, bytes_accessed=1, transcendentals=0)
-LAST_PARTS = 15, 17
+LAST_PARTS = 17, 15
 ANY_SPEC = pl.BlockSpec(memory_space=pl.ANY)
 VMEM_SPEC = pl.BlockSpec(memory_space=pltpu.VMEM)
 
@@ -102,7 +102,7 @@
     if not first:
         total_ref, refs = refs[0], refs[1:]
     out_ref, sum_ref = refs[:2]
-    height = blocks[0].shape[0]
+    height = sum(block.shape[0] for block in blocks) // len(entries)
     width = min(block.shape[1] for block in blocks)
     tile = column_tile(width)
     steps = width // tile
@@ -165,7 +165,7 @@
     rows = queries.shape[0]
     first = total is None
     operands = [pltpu.with_memory_space_constraint(queries, pltpu.VMEM), *blocks] + ([] if first else [total])
-    lanes = -(-len(entries) * blocks[0].shape[0] // LANES) * LANES
+    lanes = -(-sum(block.shape[0] for block in blocks) // LANES) * LANES
     result = [pltpu.VMEM((rows, train_count), jnp.float32), pltpu.SemaphoreType.DMA((RESULT_PARTS,))]
     return pl.pallas_call(
         functools.partial(scores_kernel, entries, len(blocks), begin, first, last),
@@ -198,6 +198,27 @@
         cost_estimate=CUT_COST,
         name="cut",
     )(block)
+
+
+def join_kernel(*refs):
+    *blocks, out_ref = refs
+    row = 0
+    for block in blocks:
+        out_ref[row:row + block.shape[0], :] = block[...]
+        row += block.shape[0]
+
+
+def join(*blocks):
+    rows = sum(block.shape[0] for block in blocks)
+    return pl.pallas_call(
+        join_kernel,
+        out_shape=jax.ShapeDtypeStruct((rows, blocks[0].shape[1]), blocks[0].dtype),
+        in_specs=[VMEM_SPEC] * len(blocks),
+        out_specs=VMEM_SPEC,
+        compiler_params=pltpu.CompilerParams(vmem_limit_bytes=KERNEL_VMEM),
+        cost_estimate=CUT_COST,
+        name="join",
+    )(*blocks)
 
 
 def per_device(queries, train_rows, left_basis, right_basis, eigenvalues):
@@ -253,18 +274,21 @@
     group = [chips - 3, chips - 2, chips - 1]
     widths = [width * part // sum(LAST_PARTS) for part in LAST_PARTS]
     begin = 0
+    joined = join(*pairs[chips - 3])
     for i, piece in enumerate(cut(chains[0], [(height, w) for w in widths])):
         if i == 1:
             piece, block = after(piece, block)
             pairs[-2 if len(pairs) == chips else -1][0] = block
         last = i == len(widths) - 1
         part = send(piece, along)
+        if i == 0:
+            part, joined = after(part, joined)
         if i:
             total = score(total, group, blocks, begin=begin)
             begin += widths[i - 1]
             part, total = after(part, total)
-        swapped = [part]
-        blocks = pairs[chips - 3] + pairs[chips - 2] + [part] + [send(piece, across) for piece in swapped]
+        swapped = [part] if last else cut(part, [(height // 2, widths[i])] * 2)
+        blocks = [joined] + pairs[chips - 2] + [part] + [send(piece, across) for piece in swapped]
     return score(total, group, blocks, begin=begin, last=True)
 
 

time: 89.6 us -> 89.2 us (level)
  waiting for transfers between devices: 35.5 us -> 34.3 us
    ppermute x18 -> x19, waiting for transfers between devices: 35.5 us -> 34.3 us  [per_device(): send = lambda block, pairs: lax.ppermute(block, 'wide', pairs)]
    ppermute x18 -> x19, starting transfers between devices: 19.4 us -> 20 us  [per_device(): send = lambda block, pairs: lax.ppermute(block, 'wide', pairs)]
  transfers between devices with their start and end apart: 18 -> 19, of which waited for: 9 -> 10; matrix products, arithmetic and copies ran while one was open for 0% -> 0% of each run, Pallas kernels for 26% -> 27%
where the time goes in v5:
time: 89.2 us; the launch traced here: 88.9 us
  waiting for transfers between devices  34.3 us (38%)
  Pallas kernels  27.2 us (30%)
  starting transfers between devices  20 us (22%)
  local copies, waits for them, and re-layouts  7 us (8%)
    ppermute x19, waiting for transfers between devices, per_device(): send = lambda block, pairs: lax.ppermute(block, 'wide', pairs)  34.3 us
    ppermute x19, starting transfers between devices, per_device(): send = lambda block, pairs: lax.ppermute(block, 'wide', pairs)  20 us
    pallas_call x4, Pallas kernels, add_scores(): pl.pallas_call(functools.partial(scores_kernel, entries, len(blocks), beg...  16.3 us
    pallas_call x3, Pallas kernels, precondition(): pl.pallas_call(precondition_kernel, out_shape=jax.ShapeDtypeStruct(rows.s...  10.6 us
    unnamed x6, local copies, waits for them, and re-layouts  7 us
  transfers between devices with their start and end apart: 19, of which 10 were waited for; matrix products, arithmetic and copies ran while one was open for 0% of the time, Pallas kernels for 27%

profile of v5, /device:TPU:0, one launch (start us, length us, event | category | flops | bytes accessed | tf_op | source)
XLA Modules:
  0.0 88.9 jit_solution(10269384911809568975)
XLA Ops:
  0.0 0.5 collective-permute-start.2
  0.5 2.6 %collective-permute-start = (bf16[32,16384]{1,0:T(8,128)(2,1)}, bf16[32,16384]{1,0:T(8,128)(2,1)S(1)}, u32[]{:S(2)}, u32[]{:S(2)}) collective-permute-start(bf16[32,16384]{1,0:T(8,128)(2,1)} %refs_0_), channel_id=1, source_target_pairs={{0,4},{1,3},{4,8},{5,1},{8,12},{9,5},{12,14},{13,9},{14,10},{15,13... | collective-permute-start | bytes 3145736 | tf_op jit(solution)/shard_map/ppermute | solution.py:238
  3.0 0.0 collective-permute-done.2.refs_0_
  3.0 3.5 %precondition.4.refs_1_ = bf16[32,16384]{1,0:T(8,128)(2,1)S(1)} custom-call(bf16[32,16384]{1,0:T(8,128)(2,1)S(1)} %collective-permute-done.2.refs_0_, bf16[128,128]{1,0:T(8,128)(2,1)} %refs_1_.5, bf16[128,128]{1,0:T(8,128)(2,1)} %refs_2_.5, f32[128,128]{1,0:T(8,128)} %refs_3_.5), custom_call_target="tpu_custom_call" | custom-call | flops 1 | bytes 1 | tf_op jit(solution)/shard_map/precondition/pallas_call | solution.py:73
  6.6 2.9 %collective-permute-start.3 = (bf16[32,16384]{1,0:T(8,128)(2,1)S(1)}, bf16[32,16384]{1,0:T(8,128)(2,1)S(1)}, u32[]{:S(2)}, u32[]{:S(2)}) collective-permute-start(bf16[32,16384]{1,0:T(8,128)(2,1)S(1)} %precondition.4.refs_1_), channel_id=1, source_target_pairs={{0,4},{1,3},{4,8},{5,1},{8,12},{9,5},{12,14},{13,9},{14,10},{15,13... | collective-permute-start | bytes 3145736 | tf_op jit(solution)/shard_map/ppermute | solution.py:238
  9.5 6.5 %collective-permute-done.refs_0_ = bf16[32,16384]{1,0:T(8,128)(2,1)S(1)} collective-permute-done((bf16[32,16384]{1,0:T(8,128)(2,1)}, bf16[32,16384]{1,0:T(8,128)(2,1)S(1)}, u32[]{:S(2)}, u32[]{:S(2)}) %collective-permute-start) | collective-permute-done | bytes 1048608 | tf_op jit(solution)/shard_map/ppermute | solution.py:238
  16.0 3.5 %precondition.3.refs_2_ = bf16[32,16384]{1,0:T(8,128)(2,1)S(1)} custom-call(bf16[32,16384]{1,0:T(8,128)(2,1)S(1)} %collective-permute-done.refs_0_, bf16[128,128]{1,0:T(8,128)(2,1)} %refs_1_.5, bf16[128,128]{1,0:T(8,128)(2,1)} %refs_2_.5, f32[128,128]{1,0:T(8,128)} %refs_3_.5), custom_call_target="tpu_custom_call" | custom-call | flops 1 | bytes 1 | tf_op jit(solution)/shard_map/precondition/pallas_call | solution.py:73
  19.5 0.1 collective-permute-start.4
  19.6 2.1 %collective-permute-start.1 = (bf16[32,16384]{1,0:T(8,128)(2,1)S(1)}, bf16[32,16384]{1,0:T(8,128)(2,1)S(1)}, u32[]{:S(2)}, u32[]{:S(2)}) collective-permute-start(bf16[32,16384]{1,0:T(8,128)(2,1)S(1)} %precondition.3.refs_2_), channel_id=1, source_target_pairs={{0,4},{1,3},{4,8},{5,1},{8,12},{9,5},{12,14},{13,9},{14,10},{15,13... | collective-permute-start | bytes 3145736 | tf_op jit(solution)/shard_map/ppermute | solution.py:238
  21.7 0.0 copy-start.2
  21.7 1.2 %copy-done.2 = bf16[32,16384]{1,0:T(8,128)(2,1)S(1)} copy-done((bf16[32,16384]{1,0:T(8,128)(2,1)S(1)}, bf16[32,16384]{1,0:T(8,128)(2,1)}, u32[]{:S(2)}) %copy-start.2) | copy-done | bytes 1048600
  22.9 3.5 %precondition.5.refs_0_ = bf16[32,16384]{1,0:T(8,128)(2,1)S(1)} custom-call(bf16[32,16384]{1,0:T(8,128)(2,1)S(1)} %copy-done.2, bf16[128,128]{1,0:T(8,128)(2,1)} %refs_1_.5, bf16[128,128]{1,0:T(8,128)(2,1)} %refs_2_.5, f32[128,128]{1,0:T(8,128)} %refs_3_.5), custom_call_target="tpu_custom_call" | custom-call | flops 1 | bytes 1 | tf_op jit(solution)/shard_map/precondition/pallas_call | solution.py:73
  26.4 0.7 collective-permute-done.3.refs_0_
  27.2 2.1 %collective-permute-start.8 = (bf16[32,16384]{1,0:T(8,128)(2,1)S(1)}, bf16[32,16384]{1,0:T(8,128)(2,1)S(1)}, u32[]{:S(2)}, u32[]{:S(2)}) collective-permute-start(bf16[32,16384]{1,0:T(8,128)(2,1)S(1)} %collective-permute-done.3.refs_0_), channel_id=1, source_target_pairs={{0,4},{1,3},{4,8},{5,1},{8,12},{9,5},{12,14},{13,9},{14,10},{15,13... | collective-permute-start | bytes 3145736 | tf_op jit(solution)/shard_map/ppermute | solution.py:238
  29.3 0.0 collective-permute-done.4.refs_3_
  29.3 0.0 copy-start
  29.3 5.8 %copy-done = bf16[512,16384]{1,0:T(8,128)(2,1)S(1)} copy-done((bf16[512,16384]{1,0:T(8,128)(2,1)S(1)}, bf16[512,16384]{1,0:T(8,128)(2,1)}, u32[]{:S(2)}) %copy-start) | copy-done | bytes 16777240
  35.0 0.0 copy-start.1
  35.0 4.8 %scores.4.refs_6_ = f32[512,512]{1,0:T(8,128)S(1)} custom-call(bf16[512,16384]{1,0:T(8,128)(2,1)S(1)} %copy-done, bf16[32,16384]{1,0:T(8,128)(2,1)S(1)} %precondition.5.refs_0_, bf16[32,16384]{1,0:T(8,128)(2,1)S(1)} %precondition.4.refs_1_, bf16[32,16384]{1,0:T(8,128)(2,1)S(1)} %precondition.3.refs_2_, bf16[32,16384]{1,0:T(8,128)(2,1)S(1)} %collective-permute-done.4.refs_3_), custom_call_target="tpu_custom_call" | custom-call | flops 1 | bytes 1 | tf_op jit(solution)/shard_map/scores/pallas_call | solution.py:170
  39.9 0.0 collective-permute-done.1.refs_2_
  39.9 1.6 %collective-permute-start.5 = (bf16[32,16384]{1,0:T(8,128)(2,1)S(1)}, bf16[32,16384]{1,0:T(8,128)(2,1)S(1)}, u32[]{:S(2)}, u32[]{:S(2)}) collective-permute-start(bf16[32,16384]{1,0:T(8,128)(2,1)S(1)} %collective-permute-done.1.refs_2_), channel_id=1, source_target_pairs={{0,4},{1,3},{4,8},{5,1},{8,12},{9,5},{12,14},{13,9},{14,10},{15,13... | collective-permute-start | bytes 3145736 | tf_op jit(solution)/shard_map/ppermute | solution.py:238
  41.5 0.0 collective-permute-start.11
  41.5 0.5 collective-permute-start.10
  42.0 7.7 %collective-permute-done.8.refs_4_ = bf16[32,16384]{1,0:T(8,128)(2,1)S(1)} collective-permute-done((bf16[32,16384]{1,0:T(8,128)(2,1)S(1)}, bf16[32,16384]{1,0:T(8,128)(2,1)S(1)}, u32[]{:S(2)}, u32[]{:S(2)}) %collective-permute-start.8) | collective-permute-done | bytes 1048608 | tf_op jit(solution)/shard_map/ppermute | solution.py:238
  49.7 0.0 collective-permute-start.12
  49.7 2.1 %collective-permute-start.9 = (bf16[32,16384]{1,0:T(8,128)(2,1)S(1)}, bf16[32,16384]{1,0:T(8,128)(2,1)S(1)}, u32[]{:S(2)}, u32[]{:S(2)}) collective-permute-start(bf16[32,16384]{1,0:T(8,128)(2,1)S(1)} %collective-permute-done.8.refs_4_), channel_id=1, source_target_pairs={{0,4},{1,3},{4,8},{5,1},{8,12},{9,5},{12,14},{13,9},{14,10},{15,13... | collective-permute-start | bytes 3145736 | tf_op jit(solution)/shard_map/ppermute | solution.py:238
  51.7 9.2 %collective-permute-done.5.source_ref.refs_0_ = bf16[32,16384]{1,0:T(8,128)(2,1)S(1)} collective-permute-done((bf16[32,16384]{1,0:T(8,128)(2,1)S(1)}, bf16[32,16384]{1,0:T(8,128)(2,1)S(1)}, u32[]{:S(2)}, u32[]{:S(2)}) %collective-permute-start.5) | collective-permute-done | bytes 1048608 | tf_op jit(solution)/shard_map/ppermute | solution.py:238
  60.9 0.0 collective-permute-start.7
  60.9 0.1 cut.3
  61.0 0.0 collective-permute-done.11.refs_3_
  61.0 2.3 %collective-permute-start.6 = (bf16[32,8704]{1,0:T(8,128)(2,1)S(1)}, bf16[32,8704]{1,0:T(8,128)(2,1)S(1)}, u32[]{:S(2)}, u32[]{:S(2)}) collective-permute-start(bf16[32,8704]{1,0:T(8,128)(2,1)S(1)} %get-tuple-element.33), channel_id=1, source_target_pairs={{0,4},{1,3},{4,8},{5,1},{8,12},{9,5},{12,14},{13,9},{14,10},{15,13... | collective-permute-start | bytes 1671176 | tf_op jit(solution)/shard_map/ppermute | solution.py:238
  63.3 0.0 collective-permute-done.10.refs_1_
  63.3 0.0 collective-permute-done.12.refs_5_
  63.3 0.0 copy-done.1
  63.3 5.0 %scores.5.refs_7_ = f32[512,512]{1,0:T(8,128)S(1)} custom-call(bf16[512,16384]{1,0:T(8,128)(2,1)S(1)} %copy-done.1, bf16[32,16384]{1,0:T(8,128)(2,1)S(1)} %collective-permute-done.3.refs_0_, bf16[32,16384]{1,0:T(8,128)(2,1)S(1)} %collective-permute-done.10.refs_1_, ...), custom_call_target="tpu_custom_call", output_to_operand_aliasing={{}: (7, {})} | custom-call | flops 1 | bytes 1 | tf_op jit(solution)/shard_map/scores/pallas_call | solution.py:170
  68.4 3.8 %collective-permute-done.9.source_ref.refs_1_ = bf16[32,16384]{1,0:T(8,128)(2,1)S(1)} collective-permute-done((bf16[32,16384]{1,0:T(8,128)(2,1)S(1)}, bf16[32,16384]{1,0:T(8,128)(2,1)S(1)}, u32[]{:S(2)}, u32[]{:S(2)}) %collective-permute-start.9) | collective-permute-done | bytes 1048608 | tf_op jit(solution)/shard_map/ppermute | solution.py:238
  72.1 0.1 cut.4
  72.2 0.1 collective-permute-start.13
  72.3 0.5 collective-permute-start.14
  72.8 2.1 %collective-permute-start.15 = (bf16[32,7680]{1,0:T(8,128)(2,1)S(1)}, bf16[32,7680]{1,0:T(8,128)(2,1)S(1)}, u32[]{:S(2)}, u32[]{:S(2)}) collective-permute-start(bf16[32,7680]{1,0:T(8,128)(2,1)S(1)} %get-tuple-element.42), channel_id=1, source_target_pairs={{0,4},{1,3},{4,8},{5,1},{8,12},{9,5},{12,14},{13,9},{14,10},{15,13... | collective-permute-start | bytes 1474568 | tf_op jit(solution)/shard_map/ppermute | solution.py:238
  74.9 0.0 collective-permute-done.7.refs_1_
  74.9 0.1 join.1.refs_0_
  75.0 3.1 %collective-permute-done.6.source_ref.refs_4_ = bf16[32,8704]{1,0:T(8,128)(2,1)S(1)} collective-permute-done((bf16[32,8704]{1,0:T(8,128)(2,1)S(1)}, bf16[32,8704]{1,0:T(8,128)(2,1)S(1)}, u32[]{:S(2)}, u32[]{:S(2)}) %collective-permute-start.6) | collective-permute-done | bytes 557088 | tf_op jit(solution)/shard_map/ppermute | solution.py:238
  78.1 0.1 collective-permute-start.16
  78.2 0.5 collective-permute-start.17
  78.7 1.0 %collective-permute-done.16.refs_5_ = bf16[16,8704]{1,0:T(8,128)(2,1)S(1)} collective-permute-done((bf16[16,8704]{1,0:T(8,128)(2,1)S(1)}, bf16[16,8704]{1,0:T(8,128)(2,1)S(1)}, u32[]{:S(2)}, u32[]{:S(2)}) %collective-permute-start.16) | collective-permute-done | bytes 278560 | tf_op jit(solution)/shard_map/ppermute | solution.py:238
  79.8 0.4 collective-permute-done.17.refs_6_
  80.2 0.0 collective-permute-done.13.refs_2_
  80.2 0.0 collective-permute-done.14.refs_3_
  80.2 3.0 %scores.6.refs_6_ = f32[512,512]{1,0:T(8,128)S(1)} custom-call(bf16[512,16384]{1,0:T(8,128)(2,1)S(1)} %copy-done.1, bf16[64,16384]{1,0:T(8,128)(2,1)S(1)} %join.1.refs_0_, bf16[32,16384]{1,0:T(8,128)(2,1)S(1)} %collective-permute-done.9.source_ref.refs_1_, bf16[16,16384]{1,0:T(8,128)(2,1)S(1)} %collective-permute-done.13.refs_2_, ...), custom_call_target="tpu_custom_call", output_to_operand_aliasing={{}: (8, {})} | custom-call | flops 1 | bytes 1 | tf_op jit(solution)/shard_map/scores/pallas_call | solution.py:170
  83.2 0.2 collective-permute-done.15.refs_4_
  83.4 0.1 collective-permute-start.18
  83.4 1.8 %collective-permute-done.18.refs_5_ = bf16[32,7680]{1,0:T(8,128)(2,1)S(1)} collective-permute-done((bf16[32,7680]{1,0:T(8,128)(2,1)S(1)}, bf16[32,7680]{1,0:T(8,128)(2,1)S(1)}, u32[]{:S(2)}, u32[]{:S(2)}) %collective-permute-start.18) | collective-permute-done | bytes 491552 | tf_op jit(solution)/shard_map/ppermute | solution.py:238
  85.2 3.5 %scores.7 = f32[512,512]{1,0:T(8,128)} custom-call(bf16[512,16384]{1,0:T(8,128)(2,1)S(1)} %copy-done.1, bf16[64,16384]{1,0:T(8,128)(2,1)S(1)} %join.1.refs_0_, bf16[32,16384]{1,0:T(8,128)(2,1)S(1)} %collective-permute-done.9.source_ref.refs_1_, bf16[16,16384]{1,0:T(8,128)(2,1)S(1)} %collective-permute-done.13.refs_2_, ...), custom_call_target="tpu_custom_call" | custom-call | flops 1 | bytes 1 | tf_op jit(solution)/shard_map/scores/pallas_call | solution.py:170
  (1 shorter events, 0.0 us)
Async XLA Ops:
  0.0 3.0 %collective-permute-start.2 = (bf16[32,16384]{1,0:T(8,128)(2,1)}, bf16[32,16384]{1,0:T(8,128)(2,1)S(1)}, u32[]{:S(2)}, u32[]{:S(2)}) collective-permute-start(bf16[32,16384]{1,0:T(8,128)(2,1)} %refs_0_), channel_id=1, source_target_pairs={{0,1},{1,0},{2,3},{3,2},{4,5},{5,4},{6,7},{7,6},{8,9},{9,8},{10,11... | collective-permute-start | bytes 3145736 | tf_op jit(solution)/shard_map/ppermute | solution.py:238
  0.5 15.5 %collective-permute-start = (bf16[32,16384]{1,0:T(8,128)(2,1)}, bf16[32,16384]{1,0:T(8,128)(2,1)S(1)}, u32[]{:S(2)}, u32[]{:S(2)}) collective-permute-start(bf16[32,16384]{1,0:T(8,128)(2,1)} %refs_0_), channel_id=1, source_target_pairs={{0,4},{1,3},{4,8},{5,1},{8,12},{9,5},{12,14},{13,9},{14,10},{15,13... | collective-permute-start | bytes 3145736 | tf_op jit(solution)/shard_map/ppermute | solution.py:238
  6.6 20.6 %collective-permute-start.3 = (bf16[32,16384]{1,0:T(8,128)(2,1)S(1)}, bf16[32,16384]{1,0:T(8,128)(2,1)S(1)}, u32[]{:S(2)}, u32[]{:S(2)}) collective-permute-start(bf16[32,16384]{1,0:T(8,128)(2,1)S(1)} %precondition.4.refs_1_), channel_id=1, source_target_pairs={{0,4},{1,3},{4,8},{5,1},{8,12},{9,5},{12,14},{13,9},{14,10},{15,13... | collective-permute-start | bytes 3145736 | tf_op jit(solution)/shard_map/ppermute | solution.py:238
  19.5 9.8 %collective-permute-start.4 = (bf16[32,16384]{1,0:T(8,128)(2,1)S(1)}, bf16[32,16384]{1,0:T(8,128)(2,1)S(1)}, u32[]{:S(2)}, u32[]{:S(2)}) collective-permute-start(bf16[32,16384]{1,0:T(8,128)(2,1)S(1)} %precondition.3.refs_2_), channel_id=1, source_target_pairs={{0,1},{1,0},{2,3},{3,2},{4,5},{5,4},{6,7},{7,6},{8,9},{9,8},{10,11... | collective-permute-start | bytes 3145736 | tf_op jit(solution)/shard_map/ppermute | solution.py:238
  19.6 20.3 %collective-permute-start.1 = (bf16[32,16384]{1,0:T(8,128)(2,1)S(1)}, bf16[32,16384]{1,0:T(8,128)(2,1)S(1)}, u32[]{:S(2)}, u32[]{:S(2)}) collective-permute-start(bf16[32,16384]{1,0:T(8,128)(2,1)S(1)} %precondition.3.refs_2_), channel_id=1, source_target_pairs={{0,4},{1,3},{4,8},{5,1},{8,12},{9,5},{12,14},{13,9},{14,10},{15,13... | collective-permute-start | bytes 3145736 | tf_op jit(solution)/shard_map/ppermute | solution.py:238
  21.7 1.2 %copy-start.2 = (bf16[32,16384]{1,0:T(8,128)(2,1)S(1)}, bf16[32,16384]{1,0:T(8,128)(2,1)}, u32[]{:S(2)}) copy-start(bf16[32,16384]{1,0:T(8,128)(2,1)} %refs_0_) | copy-start | bytes 3145732
  27.2 22.5 %collective-permute-start.8 = (bf16[32,16384]{1,0:T(8,128)(2,1)S(1)}, bf16[32,16384]{1,0:T(8,128)(2,1)S(1)}, u32[]{:S(2)}, u32[]{:S(2)}) collective-permute-start(bf16[32,16384]{1,0:T(8,128)(2,1)S(1)} %collective-permute-done.3.refs_0_), channel_id=1, source_target_pairs={{0,4},{1,3},{4,8},{5,1},{8,12},{9,5},{12,14},{13,9},{14,10},{15,13... | collective-permute-start | bytes 3145736 | tf_op jit(solution)/shard_map/ppermute | solution.py:238
  29.3 5.8 %copy-start = (bf16[512,16384]{1,0:T(8,128)(2,1)S(1)}, bf16[512,16384]{1,0:T(8,128)(2,1)}, u32[]{:S(2)}) copy-start(bf16[512,16384]{1,0:T(8,128)(2,1)} %query_ref.7) | copy-start | bytes 50331652
  35.0 28.3 %copy-start.1 = (bf16[512,16384]{1,0:T(8,128)(2,1)S(1)}, bf16[512,16384]{1,0:T(8,128)(2,1)}, u32[]{:S(2)}) copy-start(bf16[512,16384]{1,0:T(8,128)(2,1)} %query_ref.7) | copy-start | bytes 50331652
  39.9 21.0 %collective-permute-start.5 = (bf16[32,16384]{1,0:T(8,128)(2,1)S(1)}, bf16[32,16384]{1,0:T(8,128)(2,1)S(1)}, u32[]{:S(2)}, u32[]{:S(2)}) collective-permute-start(bf16[32,16384]{1,0:T(8,128)(2,1)S(1)} %collective-permute-done.1.refs_2_), channel_id=1, source_target_pairs={{0,4},{1,3},{4,8},{5,1},{8,12},{9,5},{12,14},{13,9},{14,10},{15,13... | collective-permute-start | bytes 3145736 | tf_op jit(solution)/shard_map/ppermute | solution.py:238
  41.5 19.5 %collective-permute-start.11 = (bf16[32,16384]{1,0:T(8,128)(2,1)S(1)}, bf16[32,16384]{1,0:T(8,128)(2,1)S(1)}, u32[]{:S(2)}, u32[]{:S(2)}) collective-permute-start(bf16[32,16384]{1,0:T(8,128)(2,1)S(1)} %collective-permute-done.1.refs_2_), channel_id=1, source_target_pairs={{0,1},{1,0},{2,3},{3,2},{4,5},{5,4},{6,7},{7,6},{8,9},{9,8},{10,11... | collective-permute-start | bytes 3145736 | tf_op jit(solution)/shard_map/ppermute | solution.py:238
  41.5 21.8 %collective-permute-start.10 = (bf16[32,16384]{1,0:T(8,128)(2,1)S(1)}, bf16[32,16384]{1,0:T(8,128)(2,1)S(1)}, u32[]{:S(2)}, u32[]{:S(2)}) collective-permute-start(bf16[32,16384]{1,0:T(8,128)(2,1)S(1)} %collective-permute-done.3.refs_0_), channel_id=1, source_target_pairs={{0,1},{1,0},{2,3},{3,2},{4,5},{5,4},{6,7},{7,6},{8,9},{9,8},{10,11... | collective-permute-start | bytes 3145736 | tf_op jit(solution)/shard_map/ppermute | solution.py:238
  49.7 13.6 %collective-permute-start.12 = (bf16[32,16384]{1,0:T(8,128)(2,1)S(1)}, bf16[32,16384]{1,0:T(8,128)(2,1)S(1)}, u32[]{:S(2)}, u32[]{:S(2)}) collective-permute-start(bf16[32,16384]{1,0:T(8,128)(2,1)S(1)} %collective-permute-done.8.refs_4_), channel_id=1, source_target_pairs={{0,1},{1,0},{2,3},{3,2},{4,5},{5,4},{6,7},{7,6},{8,9},{9,8},{10,11... | collective-permute-start | bytes 3145736 | tf_op jit(solution)/shard_map/ppermute | solution.py:238
  49.7 22.5 %collective-permute-start.9 = (bf16[32,16384]{1,0:T(8,128)(2,1)S(1)}, bf16[32,16384]{1,0:T(8,128)(2,1)S(1)}, u32[]{:S(2)}, u32[]{:S(2)}) collective-permute-start(bf16[32,16384]{1,0:T(8,128)(2,1)S(1)} %collective-permute-done.8.refs_4_), channel_id=1, source_target_pairs={{0,4},{1,3},{4,8},{5,1},{8,12},{9,5},{12,14},{13,9},{14,10},{15,13... | collective-permute-start | bytes 3145736 | tf_op jit(solution)/shard_map/ppermute | solution.py:238
  60.9 14.0 %collective-permute-start.7 = (bf16[32,16384]{1,0:T(8,128)(2,1)S(1)}, bf16[32,16384]{1,0:T(8,128)(2,1)S(1)}, u32[]{:S(2)}, u32[]{:S(2)}) collective-permute-start(bf16[32,16384]{1,0:T(8,128)(2,1)S(1)} %collective-permute-done.5.source_ref.refs_0_), channel_id=1, source_target_pairs={{0,1},{1,0},{2,3},{3,2},{4,5},{5,4},{6,7},{7,6},{8,9},{9,8},{10,11... | collective-permute-start | bytes 3145736 | tf_op jit(solution)/shard_map/ppermute | solution.py:238
  61.0 17.1 %collective-permute-start.6 = (bf16[32,8704]{1,0:T(8,128)(2,1)S(1)}, bf16[32,8704]{1,0:T(8,128)(2,1)S(1)}, u32[]{:S(2)}, u32[]{:S(2)}) collective-permute-start(bf16[32,8704]{1,0:T(8,128)(2,1)S(1)} %get-tuple-element.33), channel_id=1, source_target_pairs={{0,4},{1,3},{4,8},{5,1},{8,12},{9,5},{12,14},{13,9},{14,10},{15,13... | collective-permute-start | bytes 1671176 | tf_op jit(solution)/shard_map/ppermute | solution.py:238
  72.2 8.0 %collective-permute-start.13 = (bf16[16,16384]{1,0:T(8,128)(2,1)S(1)}, bf16[16,16384]{1,0:T(8,128)(2,1)S(1)}, u32[]{:S(2)}, u32[]{:S(2)}) collective-permute-start(bf16[16,16384]{1,0:T(8,128)(2,1)S(1)} %get-tuple-element.40), channel_id=1, source_target_pairs={{0,1},{1,0},{2,3},{3,2},{4,5},{5,4},{6,7},{7,6},{8,9},{9,8},{10,11... | collective-permute-start | bytes 1572872 | tf_op jit(solution)/shard_map/ppermute | solution.py:238
  72.3 7.9 %collective-permute-start.14 = (bf16[16,16384]{1,0:T(8,128)(2,1)S(1)}, bf16[16,16384]{1,0:T(8,128)(2,1)S(1)}, u32[]{:S(2)}, u32[]{:S(2)}) collective-permute-start(bf16[16,16384]{1,0:T(8,128)(2,1)S(1)} %get-tuple-element.41), channel_id=1, source_target_pairs={{0,1},{1,0},{2,3},{3,2},{4,5},{5,4},{6,7},{7,6},{8,9},{9,8},{10,11... | collective-permute-start | bytes 1572872 | tf_op jit(solution)/shard_map/ppermute | solution.py:238
  72.8 10.6 %collective-permute-start.15 = (bf16[32,7680]{1,0:T(8,128)(2,1)S(1)}, bf16[32,7680]{1,0:T(8,128)(2,1)S(1)}, u32[]{:S(2)}, u32[]{:S(2)}) collective-permute-start(bf16[32,7680]{1,0:T(8,128)(2,1)S(1)} %get-tuple-element.42), channel_id=1, source_target_pairs={{0,4},{1,3},{4,8},{5,1},{8,12},{9,5},{12,14},{13,9},{14,10},{15,13... | collective-permute-start | bytes 1474568 | tf_op jit(solution)/shard_map/ppermute | solution.py:238
  78.1 1.6 %collective-permute-start.16 = (bf16[16,8704]{1,0:T(8,128)(2,1)S(1)}, bf16[16,8704]{1,0:T(8,128)(2,1)S(1)}, u32[]{:S(2)}, u32[]{:S(2)}) collective-permute-start(bf16[16,8704]{1,0:T(8,128)(2,1)S(1)} %get-tuple-element.44), channel_id=1, source_target_pairs={{0,1},{1,0},{2,3},{3,2},{4,5},{5,4},{6,7},{7,6},{8,9},{9,8},{10,11... | collective-permute-start | bytes 835592 | tf_op jit(solution)/shard_map/ppermute | solution.py:238
  78.2 1.9 %collective-permute-start.17 = (bf16[16,8704]{1,0:T(8,128)(2,1)S(1)}, bf16[16,8704]{1,0:T(8,128)(2,1)S(1)}, u32[]{:S(2)}, u32[]{:S(2)}) collective-permute-start(bf16[16,8704]{1,0:T(8,128)(2,1)S(1)} %get-tuple-element.45), channel_id=1, source_target_pairs={{0,1},{1,0},{2,3},{3,2},{4,5},{5,4},{6,7},{7,6},{8,9},{9,8},{10,11... | collective-permute-start | bytes 835592 | tf_op jit(solution)/shard_map/ppermute | solution.py:238
  83.4 1.9 %collective-permute-start.18 = (bf16[32,7680]{1,0:T(8,128)(2,1)S(1)}, bf16[32,7680]{1,0:T(8,128)(2,1)S(1)}, u32[]{:S(2)}, u32[]{:S(2)}) collective-permute-start(bf16[32,7680]{1,0:T(8,128)(2,1)S(1)} %collective-permute-done.15.refs_4_), channel_id=1, source_target_pairs={{0,1},{1,0},{2,3},{3,2},{4,5},{5,4},{6,7},{7,6},{8,9},{9,8},{10,11... | collective-permute-start | bytes 1474568 | tf_op jit(solution)/shard_map/ppermute | solution.py:238

commit v6 on v5

--- a/solution.py
+++ b/solution.py
@@ -10,13 +10,13 @@
 A_DIM = 128
 B_DIM = 128
 LANES = 128
-K_TILE = 9216
+K_TILE = 12288
 RESULT_PARTS = 4
 KERNEL_VMEM = 16 << 20
 PREPARE_COST = pl.CostEstimate(flops=1, bytes_accessed=1, transcendentals=0)
 SCORE_COST = pl.CostEstimate(flops=1, bytes_accessed=1, transcendentals=0)
 CUT_COST = pl.CostEstimate(flops=1, bytes_accessed=1, transcendentals=0)
-LAST_PARTS = 17, 15
+LAST_PARTS = 21, 11
 ANY_SPEC = pl.BlockSpec(memory_space=pl.ANY)
 VMEM_SPEC = pl.BlockSpec(memory_space=pltpu.VMEM)
 
@@ -97,18 +97,20 @@
     return 2 * chip + (1 - core if (side + crossed) % 2 else core)
 
 
-def scores_kernel(entries, count, begin, first, last, query_ref, *refs):
+def scores_kernel(entries, count, begin, first, stage, query_ref, *refs):
     blocks, refs = refs[:count], refs[count:]
     if not first:
         total_ref, refs = refs[0], refs[1:]
-    out_ref, sum_ref = refs[:2]
+    if stage == "close":
+        begun_ref, refs = refs[0], refs[1:]
+    out_ref = refs[0]
+    sum_ref = out_ref if stage == "open" else refs[1]
     height = sum(block.shape[0] for block in blocks) // len(entries)
     width = min(block.shape[1] for block in blocks)
     tile = column_tile(width)
     steps = width // tile
     missing = sum_ref.shape[1] - sum(block.shape[0] for block in blocks)
-    chips = out_ref.shape[1] // height // 2
-    if first:
+    if first and stage is None:
         out_ref[...] = jnp.zeros_like(out_ref)
 
     def product(step):
@@ -123,13 +125,16 @@
             preferred_element_type=jnp.float32,
         )
 
-    sum_ref[...] = product(0)
+    sum_ref[...] = begun_ref[...] + product(0) if stage == "close" else product(0)
     if steps > 1:
         @pl.loop(1, steps)
         def _(step):
             sum_ref[...] += product(step)
 
+    if stage == "open":
+        return
     per_tile = LANES // height
+    chips = out_ref.shape[1] // height // 2
     owners = [owner_of(entry, chips) for entry in entries]
 
     def add(target_ref, rows):
@@ -141,7 +146,7 @@
             lanes = pl.ds(pl.multiple_of(lax.div(owner, per_tile) * LANES, LANES), LANES)
             target_ref[rows, lanes] += jnp.where(place == spot, moved, 0.0)
 
-    if not last:
+    if stage is None:
         add(out_ref, pl.ds(0, out_ref.shape[0]))
         return
     result_ref, sems = refs[2:]
@@ -161,19 +166,22 @@
     return max(t for t in range(LANES, min(K_TILE, width) + 1, LANES) if width % t == 0)
 
 
-def add_scores(total, queries, entries, blocks, train_count, begin=0, last=False):
+def add_scores(total, queries, entries, blocks, train_count, begin=0, stage=None, begun=None):
     rows = queries.shape[0]
     first = total is None
-    operands = [pltpu.with_memory_space_constraint(queries, pltpu.VMEM), *blocks] + ([] if first else [total])
     lanes = -(-sum(block.shape[0] for block in blocks) // LANES) * LANES
-    result = [pltpu.VMEM((rows, train_count), jnp.float32), pltpu.SemaphoreType.DMA((RESULT_PARTS,))]
+    operands = [pltpu.with_memory_space_constraint(queries, pltpu.VMEM), *blocks]
+    operands += [array for array in (total, begun) if array is not None]
+    scratch = [pltpu.VMEM((rows, lanes), jnp.float32)] if stage != "open" else []
+    if stage == "close":
+        scratch += [pltpu.VMEM((rows, train_count), jnp.float32), pltpu.SemaphoreType.DMA((RESULT_PARTS,))]
     return pl.pallas_call(
-        functools.partial(scores_kernel, entries, len(blocks), begin, first, last),
-        out_shape=jax.ShapeDtypeStruct((rows, train_count), jnp.float32),
+        functools.partial(scores_kernel, entries, len(blocks), begin, first, stage),
+        out_shape=jax.ShapeDtypeStruct((rows, lanes if stage == "open" else train_count), jnp.float32),
         in_specs=[VMEM_SPEC] * len(operands),
-        out_specs=ANY_SPEC if last else VMEM_SPEC,
-        scratch_shapes=[pltpu.VMEM((rows, lanes), jnp.float32)] + (result if last else []),
-        input_output_aliases={} if first or last else {len(operands) - 1: 0},
+        out_specs=ANY_SPEC if stage == "close" else VMEM_SPEC,
+        scratch_shapes=scratch,
+        input_output_aliases={} if first or stage else {len(operands) - 1: 0},
         compiler_params=pltpu.CompilerParams(vmem_limit_bytes=KERNEL_VMEM),
         cost_estimate=SCORE_COST,
         name="scores",
@@ -253,7 +261,7 @@
     pairs = [[own, other]]
     groups = [[a, a + 1] for a in range(0, chips - 6, 2)] + [[chips - 6, chips - 5, chips - 4]]
     total = None
-    for arrival in range(1, chips - 1):
+    for arrival in range(1, chips - 2):
         chain = (arrival + 1) % 2
         block = send(chains[chain], along)
         if groups[0][-1] == arrival - 2:
@@ -268,28 +276,34 @@
             else:
                 total, block = after(total, block)
         chains[chain] = block
-        halves = cut(block, [(height // 2, width)] * 2) if arrival == chips - 2 else [block]
+        halves = cut(block, [(height // 2, width)] * 2) if arrival == chips - 3 else [block]
         pairs.append([block] + [send(half, across) for half in halves])
 
     group = [chips - 3, chips - 2, chips - 1]
     widths = [width * part // sum(LAST_PARTS) for part in LAST_PARTS]
-    begin = 0
     joined = join(*pairs[chips - 3])
-    for i, piece in enumerate(cut(chains[0], [(height, w) for w in widths])):
-        if i == 1:
-            piece, block = after(piece, block)
-            pairs[-2 if len(pairs) == chips else -1][0] = block
-        last = i == len(widths) - 1
-        part = send(piece, along)
-        if i == 0:
-            part, joined = after(part, joined)
-        if i:
-            total = score(total, group, blocks, begin=begin)
-            begin += widths[i - 1]
-            part, total = after(part, total)
-        swapped = [part] if last else cut(part, [(height // 2, widths[i])] * 2)
-        blocks = [joined] + pairs[chips - 2] + [part] + [send(piece, across) for piece in swapped]
-    return score(total, group, blocks, begin=begin, last=True)
+    cuts = [cut(chains[chain], [(height, w) for w in widths]) for chain in (1, 0)]
+
+    def crossed(block):
+        return [send(half, across) for half in cut(block, [(height // 2, block.shape[1])] * 2)]
+
+    early = send(cuts[0][0], along)
+    total = score(total, groups[0], [block for a in groups[0] for block in pairs[a]])
+    early, total = after(early, total)
+    late = send(cuts[1][0], along)
+    late, joined = after(late, joined)
+    blocks = [joined, early, send(early, across), late] + crossed(late)
+    source, early = after(cuts[0][1], early)
+    blocks[1] = early
+    early = send(source, along)
+    source, late = after(cuts[1][1], late)
+    blocks[3] = late
+    late = send(source, along)
+    blocks[3], early = after(blocks[3], early)
+    begun = score(None, group, blocks, stage="open")
+    late, begun = after(late, begun)
+    blocks = [joined, early, send(early, across), late, send(late, across)]
+    return score(total, group, blocks, begin=widths[0], stage="close", begun=begun)
 
 
 def solution(mesh):

time: 89.2 us -> 88.5 us (level)
  waiting for transfers between devices: 34.3 us -> 32.4 us
  starting transfers between devices: 20 us -> 21.7 us
    ppermute x19 -> x21, waiting for transfers between devices: 34.3 us -> 32.4 us  [per_device(): send = lambda block, pairs: lax.ppermute(block, 'wide', pairs)]
    ppermute x19 -> x21, starting transfers between devices: 20 us -> 21.7 us  [per_device(): send = lambda block, pairs: lax.ppermute(block, 'wide', pairs)]
  transfers between devices with their start and end apart: 19 -> 21, of which waited for: 10 -> 9; matrix products, arithmetic and copies ran while one was open for 0% -> 0% of each run, Pallas kernels for 27% -> 27%
where the time goes in v6:
time: 88.5 us; the launch traced here: 88.1 us
  waiting for transfers between devices  32.4 us (37%)
  Pallas kernels  26.7 us (30%)
  starting transfers between devices  21.7 us (25%)
  local copies, waits for them, and re-layouts  7 us (8%)
    ppermute x21, waiting for transfers between devices, per_device(): send = lambda block, pairs: lax.ppermute(block, 'wide', pairs)  32.4 us
    ppermute x21, starting transfers between devices, per_device(): send = lambda block, pairs: lax.ppermute(block, 'wide', pairs)  21.7 us
    pallas_call x4, Pallas kernels, add_scores(): pl.pallas_call(functools.partial(scores_kernel, entries, len(blocks), beg...  15.8 us
    pallas_call x3, Pallas kernels, precondition(): pl.pallas_call(precondition_kernel, out_shape=jax.ShapeDtypeStruct(rows.s...  10.6 us
    unnamed x6, local copies, waits for them, and re-layouts  7 us
  transfers between devices with their start and end apart: 21, of which 9 were waited for; matrix products, arithmetic and copies ran while one was open for 0% of the time, Pallas kernels for 27%

profile of v6, /device:TPU:0, one launch (start us, length us, event | category | flops | bytes accessed | tf_op | source)
XLA Modules:
  0.0 88.1 jit_solution(5813745393225899845)
XLA Ops:
  0.0 0.5 collective-permute-start.2
  0.5 2.6 %collective-permute-start = (bf16[32,16384]{1,0:T(8,128)(2,1)}, bf16[32,16384]{1,0:T(8,128)(2,1)S(1)}, u32[]{:S(2)}, u32[]{:S(2)}) collective-permute-start(bf16[32,16384]{1,0:T(8,128)(2,1)} %refs_0_), channel_id=1, source_target_pairs={{0,4},{1,3},{4,8},{5,1},{8,12},{9,5},{12,14},{13,9},{14,10},{15,13... | collective-permute-start | bytes 3145736 | tf_op jit(solution)/shard_map/ppermute | solution.py:246
  3.0 0.0 collective-permute-done.2.refs_0_
  3.0 3.5 %precondition.4.refs_1_ = bf16[32,16384]{1,0:T(8,128)(2,1)S(1)} custom-call(bf16[32,16384]{1,0:T(8,128)(2,1)S(1)} %collective-permute-done.2.refs_0_, bf16[128,128]{1,0:T(8,128)(2,1)} %refs_1_.5, bf16[128,128]{1,0:T(8,128)(2,1)} %refs_2_.5, f32[128,128]{1,0:T(8,128)} %refs_3_.5), custom_call_target="tpu_custom_call" | custom-call | flops 1 | bytes 1 | tf_op jit(solution)/shard_map/precondition/pallas_call | solution.py:73
  6.6 2.9 %collective-permute-start.3 = (bf16[32,16384]{1,0:T(8,128)(2,1)S(1)}, bf16[32,16384]{1,0:T(8,128)(2,1)S(1)}, u32[]{:S(2)}, u32[]{:S(2)}) collective-permute-start(bf16[32,16384]{1,0:T(8,128)(2,1)S(1)} %precondition.4.refs_1_), channel_id=1, source_target_pairs={{0,4},{1,3},{4,8},{5,1},{8,12},{9,5},{12,14},{13,9},{14,10},{15,13... | collective-permute-start | bytes 3145736 | tf_op jit(solution)/shard_map/ppermute | solution.py:246
  9.5 6.5 %collective-permute-done.refs_0_ = bf16[32,16384]{1,0:T(8,128)(2,1)S(1)} collective-permute-done((bf16[32,16384]{1,0:T(8,128)(2,1)}, bf16[32,16384]{1,0:T(8,128)(2,1)S(1)}, u32[]{:S(2)}, u32[]{:S(2)}) %collective-permute-start) | collective-permute-done | bytes 1048608 | tf_op jit(solution)/shard_map/ppermute | solution.py:246
  16.0 3.5 %precondition.3.refs_2_ = bf16[32,16384]{1,0:T(8,128)(2,1)S(1)} custom-call(bf16[32,16384]{1,0:T(8,128)(2,1)S(1)} %collective-permute-done.refs_0_, bf16[128,128]{1,0:T(8,128)(2,1)} %refs_1_.5, bf16[128,128]{1,0:T(8,128)(2,1)} %refs_2_.5, f32[128,128]{1,0:T(8,128)} %refs_3_.5), custom_call_target="tpu_custom_call" | custom-call | flops 1 | bytes 1 | tf_op jit(solution)/shard_map/precondition/pallas_call | solution.py:73
  19.5 0.1 collective-permute-start.4
  19.6 2.1 %collective-permute-start.1 = (bf16[32,16384]{1,0:T(8,128)(2,1)S(1)}, bf16[32,16384]{1,0:T(8,128)(2,1)S(1)}, u32[]{:S(2)}, u32[]{:S(2)}) collective-permute-start(bf16[32,16384]{1,0:T(8,128)(2,1)S(1)} %precondition.3.refs_2_), channel_id=1, source_target_pairs={{0,4},{1,3},{4,8},{5,1},{8,12},{9,5},{12,14},{13,9},{14,10},{15,13... | collective-permute-start | bytes 3145736 | tf_op jit(solution)/shard_map/ppermute | solution.py:246
  21.7 0.0 copy-start.2
  21.7 1.2 %copy-done.2 = bf16[32,16384]{1,0:T(8,128)(2,1)S(1)} copy-done((bf16[32,16384]{1,0:T(8,128)(2,1)S(1)}, bf16[32,16384]{1,0:T(8,128)(2,1)}, u32[]{:S(2)}) %copy-start.2) | copy-done | bytes 1048600
  22.9 3.5 %precondition.5.refs_0_ = bf16[32,16384]{1,0:T(8,128)(2,1)S(1)} custom-call(bf16[32,16384]{1,0:T(8,128)(2,1)S(1)} %copy-done.2, bf16[128,128]{1,0:T(8,128)(2,1)} %refs_1_.5, bf16[128,128]{1,0:T(8,128)(2,1)} %refs_2_.5, f32[128,128]{1,0:T(8,128)} %refs_3_.5), custom_call_target="tpu_custom_call" | custom-call | flops 1 | bytes 1 | tf_op jit(solution)/shard_map/precondition/pallas_call | solution.py:73
  26.4 0.7 collective-permute-done.3.refs_0_
  27.2 2.1 %collective-permute-start.9 = (bf16[32,16384]{1,0:T(8,128)(2,1)S(1)}, bf16[32,16384]{1,0:T(8,128)(2,1)S(1)}, u32[]{:S(2)}, u32[]{:S(2)}) collective-permute-start(bf16[32,16384]{1,0:T(8,128)(2,1)S(1)} %collective-permute-done.3.refs_0_), channel_id=1, source_target_pairs={{0,4},{1,3},{4,8},{5,1},{8,12},{9,5},{12,14},{13,9},{14,10},{15,13... | collective-permute-start | bytes 3145736 | tf_op jit(solution)/shard_map/ppermute | solution.py:246
  29.3 0.0 collective-permute-done.4.refs_3_
  29.3 0.0 copy-start
  29.3 5.8 %copy-done = bf16[512,16384]{1,0:T(8,128)(2,1)S(1)} copy-done((bf16[512,16384]{1,0:T(8,128)(2,1)S(1)}, bf16[512,16384]{1,0:T(8,128)(2,1)}, u32[]{:S(2)}) %copy-start) | copy-done | bytes 16777240
  35.0 0.0 copy-start.1
  35.0 4.8 %scores.4.refs_6_ = f32[512,512]{1,0:T(8,128)S(1)} custom-call(bf16[512,16384]{1,0:T(8,128)(2,1)S(1)} %copy-done, bf16[32,16384]{1,0:T(8,128)(2,1)S(1)} %precondition.5.refs_0_, bf16[32,16384]{1,0:T(8,128)(2,1)S(1)} %precondition.4.refs_1_, bf16[32,16384]{1,0:T(8,128)(2,1)S(1)} %precondition.3.refs_2_, bf16[32,16384]{1,0:T(8,128)(2,1)S(1)} %collective-permute-done.4.refs_3_), custom_call_target="tpu_custom_call" | custom-call | flops 1 | bytes 1 | tf_op jit(solution)/shard_map/scores/pallas_call | solution.py:178
  39.9 0.0 collective-permute-done.1.refs_2_
  39.9 1.6 %collective-permute-start.5 = (bf16[32,16384]{1,0:T(8,128)(2,1)S(1)}, bf16[32,16384]{1,0:T(8,128)(2,1)S(1)}, u32[]{:S(2)}, u32[]{:S(2)}) collective-permute-start(bf16[32,16384]{1,0:T(8,128)(2,1)S(1)} %collective-permute-done.1.refs_2_), channel_id=1, source_target_pairs={{0,4},{1,3},{4,8},{5,1},{8,12},{9,5},{12,14},{13,9},{14,10},{15,13... | collective-permute-start | bytes 3145736 | tf_op jit(solution)/shard_map/ppermute | solution.py:246
  41.5 0.0 collective-permute-start.12
  41.5 0.5 collective-permute-start.11
  42.0 7.7 %collective-permute-done.9.source_ref.refs_4_ = bf16[32,16384]{1,0:T(8,128)(2,1)S(1)} collective-permute-done((bf16[32,16384]{1,0:T(8,128)(2,1)S(1)}, bf16[32,16384]{1,0:T(8,128)(2,1)S(1)}, u32[]{:S(2)}, u32[]{:S(2)}) %collective-permute-start.9) | collective-permute-done | bytes 1048608 | tf_op jit(solution)/shard_map/ppermute | solution.py:246
  49.7 0.0 collective-permute-start.13
  49.7 0.1 cut.6
  49.7 2.1 %collective-permute-start.10 = (bf16[32,10752]{1,0:T(8,128)(2,1)S(1)}, bf16[32,10752]{1,0:T(8,128)(2,1)S(1)}, u32[]{:S(2)}, u32[]{:S(2)}) collective-permute-start(bf16[32,10752]{1,0:T(8,128)(2,1)S(1)} %get-tuple-element.48), channel_id=1, source_target_pairs={{0,4},{1,3},{4,8},{5,1},{8,12},{9,5},{12,14},{13,9},{14,10},{15,13... | collective-permute-start | bytes 2064392 | tf_op jit(solution)/shard_map/ppermute | solution.py:246
  51.9 9.0 %collective-permute-done.5.source_ref.refs_0_ = bf16[32,16384]{1,0:T(8,128)(2,1)S(1)} collective-permute-done((bf16[32,16384]{1,0:T(8,128)(2,1)S(1)}, bf16[32,16384]{1,0:T(8,128)(2,1)S(1)}, u32[]{:S(2)}, u32[]{:S(2)}) %collective-permute-start.5) | collective-permute-done | bytes 1048608 | tf_op jit(solution)/shard_map/ppermute | solution.py:246
  60.9 0.1 cut.4
  61.0 2.3 %collective-permute-start.6 = (bf16[32,10752]{1,0:T(8,128)(2,1)S(1)}, bf16[32,10752]{1,0:T(8,128)(2,1)S(1)}, u32[]{:S(2)}, u32[]{:S(2)}) collective-permute-start(bf16[32,10752]{1,0:T(8,128)(2,1)S(1)} %get-tuple-element.39), channel_id=1, source_target_pairs={{0,4},{1,3},{4,8},{5,1},{8,12},{9,5},{12,14},{13,9},{14,10},{15,13... | collective-permute-start | bytes 2064392 | tf_op jit(solution)/shard_map/ppermute | solution.py:246
  63.3 0.1 cut.5
  63.4 0.0 collective-permute-done.12.refs_3_
  63.4 0.1 collective-permute-start.7
  63.4 0.0 collective-permute-done.11.refs_1_
  63.5 0.5 collective-permute-start.8
  63.9 0.0 collective-permute-done.13.refs_5_
  63.9 0.0 copy-done.1
  64.0 5.0 %scores.5.refs_5_ = f32[512,512]{1,0:T(8,128)S(1)} custom-call(bf16[512,16384]{1,0:T(8,128)(2,1)S(1)} %copy-done.1, bf16[32,16384]{1,0:T(8,128)(2,1)S(1)} %collective-permute-done.3.refs_0_, bf16[32,16384]{1,0:T(8,128)(2,1)S(1)} %collective-permute-done.11.refs_1_, ...), custom_call_target="tpu_custom_call", output_to_operand_aliasing={{}: (7, {})} | custom-call | flops 1 | bytes 1 | tf_op jit(solution)/shard_map/scores/pallas_call | solution.py:178
  69.0 0.0 collective-permute-done.10.refs_1_
  69.0 0.1 collective-permute-start.17
  69.2 1.6 %collective-permute-start.14 = (bf16[32,5632]{1,0:T(8,128)(2,1)S(1)}, bf16[32,5632]{1,0:T(8,128)(2,1)S(1)}, u32[]{:S(2)}, u32[]{:S(2)}) collective-permute-start(bf16[32,5632]{1,0:T(8,128)(2,1)S(1)} %get-tuple-element.51), channel_id=1, source_target_pairs={{0,4},{1,3},{4,8},{5,1},{8,12},{9,5},{12,14},{13,9},{14,10},{15,13... | collective-permute-start | bytes 1081352 | tf_op jit(solution)/shard_map/ppermute | solution.py:246
  70.7 0.0 collective-permute-done.7.refs_1_
  70.7 0.0 collective-permute-done.8.refs_2_
  70.7 0.1 join.1.refs_0_
  70.9 4.8 %collective-permute-done.6.source_ref.refs_3_ = bf16[32,10752]{1,0:T(8,128)(2,1)S(1)} collective-permute-done((bf16[32,10752]{1,0:T(8,128)(2,1)S(1)}, bf16[32,10752]{1,0:T(8,128)(2,1)S(1)}, u32[]{:S(2)}, u32[]{:S(2)}) %collective-permute-start.6) | collective-permute-done | bytes 688160 | tf_op jit(solution)/shard_map/ppermute | solution.py:246
  75.6 2.1 %collective-permute-start.16 = (bf16[32,5632]{1,0:T(8,128)(2,1)S(1)}, bf16[32,5632]{1,0:T(8,128)(2,1)S(1)}, u32[]{:S(2)}, u32[]{:S(2)}) collective-permute-start(bf16[32,5632]{1,0:T(8,128)(2,1)S(1)} %get-tuple-element.53), channel_id=1, source_target_pairs={{0,4},{1,3},{4,8},{5,1},{8,12},{9,5},{12,14},{13,9},{14,10},{15,13... | collective-permute-start | bytes 1081352 | tf_op jit(solution)/shard_map/ppermute | solution.py:246
  77.8 0.1 collective-permute-start.18
  77.9 0.5 collective-permute-start.19
  78.4 1.2 %collective-permute-done.14.refs_1_ = bf16[32,5632]{1,0:T(8,128)(2,1)S(1)} collective-permute-done((bf16[32,5632]{1,0:T(8,128)(2,1)S(1)}, bf16[32,5632]{1,0:T(8,128)(2,1)S(1)}, u32[]{:S(2)}, u32[]{:S(2)}) %collective-permute-start.14) | collective-permute-done | bytes 360480 | tf_op jit(solution)/shard_map/ppermute | solution.py:246
  79.5 0.0 collective-permute-start.15
  79.5 0.0 collective-permute-done.18.refs_4_
  79.5 0.5 collective-permute-done.19.refs_5_
  80.0 0.0 collective-permute-done.17.refs_2_
  80.0 3.0 %scores.6.refs_6_ = f32[512,256]{1,0:T(8,128)S(1)} custom-call(bf16[512,16384]{1,0:T(8,128)(2,1)S(1)} %copy-done.1, bf16[64,16384]{1,0:T(8,128)(2,1)S(1)} %join.1.refs_0_, bf16[32,10752]{1,0:T(8,128)(2,1)S(1)} %collective-permute-done.10.refs_1_, bf16[32,10752]{1,0:T(8,128)(2,1)S(1)} %collective-permute-done.17.refs_2_, ...), custom_call_target="tpu_custom_call" | custom-call | flops 1 | bytes 1 | tf_op jit(solution)/shard_map/scores/pallas_call | solution.py:178
  83.0 0.4 collective-permute-done.16.refs_3_
  83.4 0.0 collective-permute-start.20
  83.4 0.0 collective-permute-done.15.refs_2_
  83.4 1.7 %collective-permute-done.20.refs_4_ = bf16[32,5632]{1,0:T(8,128)(2,1)S(1)} collective-permute-done((bf16[32,5632]{1,0:T(8,128)(2,1)S(1)}, bf16[32,5632]{1,0:T(8,128)(2,1)S(1)}, u32[]{:S(2)}, u32[]{:S(2)}) %collective-permute-start.20) | collective-permute-done | bytes 360480 | tf_op jit(solution)/shard_map/ppermute | solution.py:246
  85.0 2.9 %scores.7 = f32[512,512]{1,0:T(8,128)} custom-call(bf16[512,16384]{1,0:T(8,128)(2,1)S(1)} %copy-done.1, bf16[64,16384]{1,0:T(8,128)(2,1)S(1)} %join.1.refs_0_, bf16[32,5632]{1,0:T(8,128)(2,1)S(1)} %collective-permute-done.14.refs_1_, bf16[32,5632]{1,0:T(8,128)(2,1)S(1)} %collective-permute-done.15.refs_2_, ...), custom_call_target="tpu_custom_call" | custom-call | flops 1 | bytes 1 | tf_op jit(solution)/shard_map/scores/pallas_call | solution.py:178
  (1 shorter events, 0.0 us)
Async XLA Ops:
  0.0 3.0 %collective-permute-start.2 = (bf16[32,16384]{1,0:T(8,128)(2,1)}, bf16[32,16384]{1,0:T(8,128)(2,1)S(1)}, u32[]{:S(2)}, u32[]{:S(2)}) collective-permute-start(bf16[32,16384]{1,0:T(8,128)(2,1)} %refs_0_), channel_id=1, source_target_pairs={{0,1},{1,0},{2,3},{3,2},{4,5},{5,4},{6,7},{7,6},{8,9},{9,8},{10,11... | collective-permute-start | bytes 3145736 | tf_op jit(solution)/shard_map/ppermute | solution.py:246
  0.5 15.5 %collective-permute-start = (bf16[32,16384]{1,0:T(8,128)(2,1)}, bf16[32,16384]{1,0:T(8,128)(2,1)S(1)}, u32[]{:S(2)}, u32[]{:S(2)}) collective-permute-start(bf16[32,16384]{1,0:T(8,128)(2,1)} %refs_0_), channel_id=1, source_target_pairs={{0,4},{1,3},{4,8},{5,1},{8,12},{9,5},{12,14},{13,9},{14,10},{15,13... | collective-permute-start | bytes 3145736 | tf_op jit(solution)/shard_map/ppermute | solution.py:246
  6.6 20.6 %collective-permute-start.3 = (bf16[32,16384]{1,0:T(8,128)(2,1)S(1)}, bf16[32,16384]{1,0:T(8,128)(2,1)S(1)}, u32[]{:S(2)}, u32[]{:S(2)}) collective-permute-start(bf16[32,16384]{1,0:T(8,128)(2,1)S(1)} %precondition.4.refs_1_), channel_id=1, source_target_pairs={{0,4},{1,3},{4,8},{5,1},{8,12},{9,5},{12,14},{13,9},{14,10},{15,13... | collective-permute-start | bytes 3145736 | tf_op jit(solution)/shard_map/ppermute | solution.py:246
  19.5 9.8 %collective-permute-start.4 = (bf16[32,16384]{1,0:T(8,128)(2,1)S(1)}, bf16[32,16384]{1,0:T(8,128)(2,1)S(1)}, u32[]{:S(2)}, u32[]{:S(2)}) collective-permute-start(bf16[32,16384]{1,0:T(8,128)(2,1)S(1)} %precondition.3.refs_2_), channel_id=1, source_target_pairs={{0,1},{1,0},{2,3},{3,2},{4,5},{5,4},{6,7},{7,6},{8,9},{9,8},{10,11... | collective-permute-start | bytes 3145736 | tf_op jit(solution)/shard_map/ppermute | solution.py:246
  19.6 20.3 %collective-permute-start.1 = (bf16[32,16384]{1,0:T(8,128)(2,1)S(1)}, bf16[32,16384]{1,0:T(8,128)(2,1)S(1)}, u32[]{:S(2)}, u32[]{:S(2)}) collective-permute-start(bf16[32,16384]{1,0:T(8,128)(2,1)S(1)} %precondition.3.refs_2_), channel_id=1, source_target_pairs={{0,4},{1,3},{4,8},{5,1},{8,12},{9,5},{12,14},{13,9},{14,10},{15,13... | collective-permute-start | bytes 3145736 | tf_op jit(solution)/shard_map/ppermute | solution.py:246
  21.7 1.2 %copy-start.2 = (bf16[32,16384]{1,0:T(8,128)(2,1)S(1)}, bf16[32,16384]{1,0:T(8,128)(2,1)}, u32[]{:S(2)}) copy-start(bf16[32,16384]{1,0:T(8,128)(2,1)} %refs_0_) | copy-start | bytes 3145732
  27.2 22.5 %collective-permute-start.9 = (bf16[32,16384]{1,0:T(8,128)(2,1)S(1)}, bf16[32,16384]{1,0:T(8,128)(2,1)S(1)}, u32[]{:S(2)}, u32[]{:S(2)}) collective-permute-start(bf16[32,16384]{1,0:T(8,128)(2,1)S(1)} %collective-permute-done.3.refs_0_), channel_id=1, source_target_pairs={{0,4},{1,3},{4,8},{5,1},{8,12},{9,5},{12,14},{13,9},{14,10},{15,13... | collective-permute-start | bytes 3145736 | tf_op jit(solution)/shard_map/ppermute | solution.py:246
  29.3 5.8 %copy-start = (bf16[512,16384]{1,0:T(8,128)(2,1)S(1)}, bf16[512,16384]{1,0:T(8,128)(2,1)}, u32[]{:S(2)}) copy-start(bf16[512,16384]{1,0:T(8,128)(2,1)} %query_ref.7) | copy-start | bytes 50331652
  35.0 28.9 %copy-start.1 = (bf16[512,16384]{1,0:T(8,128)(2,1)S(1)}, bf16[512,16384]{1,0:T(8,128)(2,1)}, u32[]{:S(2)}) copy-start(bf16[512,16384]{1,0:T(8,128)(2,1)} %query_ref.7) | copy-start | bytes 50331652
  39.9 21.0 %collective-permute-start.5 = (bf16[32,16384]{1,0:T(8,128)(2,1)S(1)}, bf16[32,16384]{1,0:T(8,128)(2,1)S(1)}, u32[]{:S(2)}, u32[]{:S(2)}) collective-permute-start(bf16[32,16384]{1,0:T(8,128)(2,1)S(1)} %collective-permute-done.1.refs_2_), channel_id=1, source_target_pairs={{0,4},{1,3},{4,8},{5,1},{8,12},{9,5},{12,14},{13,9},{14,10},{15,13... | collective-permute-start | bytes 3145736 | tf_op jit(solution)/shard_map/ppermute | solution.py:246
  41.5 21.9 %collective-permute-start.12 = (bf16[32,16384]{1,0:T(8,128)(2,1)S(1)}, bf16[32,16384]{1,0:T(8,128)(2,1)S(1)}, u32[]{:S(2)}, u32[]{:S(2)}) collective-permute-start(bf16[32,16384]{1,0:T(8,128)(2,1)S(1)} %collective-permute-done.1.refs_2_), channel_id=1, source_target_pairs={{0,1},{1,0},{2,3},{3,2},{4,5},{5,4},{6,7},{7,6},{8,9},{9,8},{10,11... | collective-permute-start | bytes 3145736 | tf_op jit(solution)/shard_map/ppermute | solution.py:246
  41.5 21.9 %collective-permute-start.11 = (bf16[32,16384]{1,0:T(8,128)(2,1)S(1)}, bf16[32,16384]{1,0:T(8,128)(2,1)S(1)}, u32[]{:S(2)}, u32[]{:S(2)}) collective-permute-start(bf16[32,16384]{1,0:T(8,128)(2,1)S(1)} %collective-permute-done.3.refs_0_), channel_id=1, source_target_pairs={{0,1},{1,0},{2,3},{3,2},{4,5},{5,4},{6,7},{7,6},{8,9},{9,8},{10,11... | collective-permute-start | bytes 3145736 | tf_op jit(solution)/shard_map/ppermute | solution.py:246
  49.7 14.3 %collective-permute-start.13 = (bf16[32,16384]{1,0:T(8,128)(2,1)S(1)}, bf16[32,16384]{1,0:T(8,128)(2,1)S(1)}, u32[]{:S(2)}, u32[]{:S(2)}) collective-permute-start(bf16[32,16384]{1,0:T(8,128)(2,1)S(1)} %collective-permute-done.9.source_ref.refs_4_), channel_id=1, source_target_pairs={{0,1},{1,0},{2,3},{3,2},{4,5},{5,4},{6,7},{7,6},{8,9},{9,8},{10,11... | collective-permute-start | bytes 3145736 | tf_op jit(solution)/shard_map/ppermute | solution.py:246
  49.7 19.3 %collective-permute-start.10 = (bf16[32,10752]{1,0:T(8,128)(2,1)S(1)}, bf16[32,10752]{1,0:T(8,128)(2,1)S(1)}, u32[]{:S(2)}, u32[]{:S(2)}) collective-permute-start(bf16[32,10752]{1,0:T(8,128)(2,1)S(1)} %get-tuple-element.48), channel_id=1, source_target_pairs={{0,4},{1,3},{4,8},{5,1},{8,12},{9,5},{12,14},{13,9},{14,10},{15,13... | collective-permute-start | bytes 2064392 | tf_op jit(solution)/shard_map/ppermute | solution.py:246
  61.0 14.7 %collective-permute-start.6 = (bf16[32,10752]{1,0:T(8,128)(2,1)S(1)}, bf16[32,10752]{1,0:T(8,128)(2,1)S(1)}, u32[]{:S(2)}, u32[]{:S(2)}) collective-permute-start(bf16[32,10752]{1,0:T(8,128)(2,1)S(1)} %get-tuple-element.39), channel_id=1, source_target_pairs={{0,4},{1,3},{4,8},{5,1},{8,12},{9,5},{12,14},{13,9},{14,10},{15,13... | collective-permute-start | bytes 2064392 | tf_op jit(solution)/shard_map/ppermute | solution.py:246
  63.4 7.4 %collective-permute-start.7 = (bf16[16,16384]{1,0:T(8,128)(2,1)S(1)}, bf16[16,16384]{1,0:T(8,128)(2,1)S(1)}, u32[]{:S(2)}, u32[]{:S(2)}) collective-permute-start(bf16[16,16384]{1,0:T(8,128)(2,1)S(1)} %get-tuple-element.40), channel_id=1, source_target_pairs={{0,1},{1,0},{2,3},{3,2},{4,5},{5,4},{6,7},{7,6},{8,9},{9,8},{10,11... | collective-permute-start | bytes 1572872 | tf_op jit(solution)/shard_map/ppermute | solution.py:246
  63.5 7.3 %collective-permute-start.8 = (bf16[16,16384]{1,0:T(8,128)(2,1)S(1)}, bf16[16,16384]{1,0:T(8,128)(2,1)S(1)}, u32[]{:S(2)}, u32[]{:S(2)}) collective-permute-start(bf16[16,16384]{1,0:T(8,128)(2,1)S(1)} %get-tuple-element.41), channel_id=1, source_target_pairs={{0,1},{1,0},{2,3},{3,2},{4,5},{5,4},{6,7},{7,6},{8,9},{9,8},{10,11... | collective-permute-start | bytes 1572872 | tf_op jit(solution)/shard_map/ppermute | solution.py:246
  69.0 11.0 %collective-permute-start.17 = (bf16[32,10752]{1,0:T(8,128)(2,1)S(1)}, bf16[32,10752]{1,0:T(8,128)(2,1)S(1)}, u32[]{:S(2)}, u32[]{:S(2)}) collective-permute-start(bf16[32,10752]{1,0:T(8,128)(2,1)S(1)} %collective-permute-done.10.refs_1_), channel_id=1, source_target_pairs={{0,1},{1,0},{2,3},{3,2},{4,5},{5,4},{6,7},{7,6},{8,9},{9,8},{10,11... | collective-permute-start | bytes 2064392 | tf_op jit(solution)/shard_map/ppermute | solution.py:246
  69.2 10.3 %collective-permute-start.14 = (bf16[32,5632]{1,0:T(8,128)(2,1)S(1)}, bf16[32,5632]{1,0:T(8,128)(2,1)S(1)}, u32[]{:S(2)}, u32[]{:S(2)}) collective-permute-start(bf16[32,5632]{1,0:T(8,128)(2,1)S(1)} %get-tuple-element.51), channel_id=1, source_target_pairs={{0,4},{1,3},{4,8},{5,1},{8,12},{9,5},{12,14},{13,9},{14,10},{15,13... | collective-permute-start | bytes 1081352 | tf_op jit(solution)/shard_map/ppermute | solution.py:246
  75.6 7.7 %collective-permute-start.16 = (bf16[32,5632]{1,0:T(8,128)(2,1)S(1)}, bf16[32,5632]{1,0:T(8,128)(2,1)S(1)}, u32[]{:S(2)}, u32[]{:S(2)}) collective-permute-start(bf16[32,5632]{1,0:T(8,128)(2,1)S(1)} %get-tuple-element.53), channel_id=1, source_target_pairs={{0,4},{1,3},{4,8},{5,1},{8,12},{9,5},{12,14},{13,9},{14,10},{15,13... | collective-permute-start | bytes 1081352 | tf_op jit(solution)/shard_map/ppermute | solution.py:246
  77.8 1.7 %collective-permute-start.18 = (bf16[16,10752]{1,0:T(8,128)(2,1)S(1)}, bf16[16,10752]{1,0:T(8,128)(2,1)S(1)}, u32[]{:S(2)}, u32[]{:S(2)}) collective-permute-start(bf16[16,10752]{1,0:T(8,128)(2,1)S(1)} %get-tuple-element.56), channel_id=1, source_target_pairs={{0,1},{1,0},{2,3},{3,2},{4,5},{5,4},{6,7},{7,6},{8,9},{9,8},{10,11... | collective-permute-start | bytes 1032200 | tf_op jit(solution)/shard_map/ppermute | solution.py:246
  77.9 2.1 %collective-permute-start.19 = (bf16[16,10752]{1,0:T(8,128)(2,1)S(1)}, bf16[16,10752]{1,0:T(8,128)(2,1)S(1)}, u32[]{:S(2)}, u32[]{:S(2)}) collective-permute-start(bf16[16,10752]{1,0:T(8,128)(2,1)S(1)} %get-tuple-element.57), channel_id=1, source_target_pairs={{0,1},{1,0},{2,3},{3,2},{4,5},{5,4},{6,7},{7,6},{8,9},{9,8},{10,11... | collective-permute-start | bytes 1032200 | tf_op jit(solution)/shard_map/ppermute | solution.py:246
  79.5 3.9 %collective-permute-start.15 = (bf16[32,5632]{1,0:T(8,128)(2,1)S(1)}, bf16[32,5632]{1,0:T(8,128)(2,1)S(1)}, u32[]{:S(2)}, u32[]{:S(2)}) collective-permute-start(bf16[32,5632]{1,0:T(8,128)(2,1)S(1)} %collective-permute-done.14.refs_1_), channel_id=1, source_target_pairs={{0,1},{1,0},{2,3},{3,2},{4,5},{5,4},{6,7},{7,6},{8,9},{9,8},{10,11... | collective-permute-start | bytes 1081352 | tf_op jit(solution)/shard_map/ppermute | solution.py:246
  83.4 1.7 %collective-permute-start.20 = (bf16[32,5632]{1,0:T(8,128)(2,1)S(1)}, bf16[32,5632]{1,0:T(8,128)(2,1)S(1)}, u32[]{:S(2)}, u32[]{:S(2)}) collective-permute-start(bf16[32,5632]{1,0:T(8,128)(2,1)S(1)} %collective-permute-done.16.refs_3_), channel_id=1, source_target_pairs={{0,1},{1,0},{2,3},{3,2},{4,5},{5,4},{6,7},{7,6},{8,9},{9,8},{10,11... | collective-permute-start | bytes 1081352 | tf_op jit(solution)/shard_map/ppermute | solution.py:246
